TPU v7x, 32 devices: a whole 2x2x4 slice. The times are simulated.
32 devices in a mesh: groups: 2 (over y), blk: 4 (over z), dp: 4 (over x, core).
Axes of the slice: x: 2, y: 2, z: 4, core: 2. Of those that a mesh axis runs over, the one named last changes fastest.
Arguments:
- inputs: bfloat16 [1024, 4096], P(('groups', 'dp'), 'blk'), parts along dimension 0, may hold values from -6 to 6
- out_grad: bfloat16 [1024, 4096], P(('groups', 'dp'), 'blk'), parts along dimension 0, may hold values from -6 to 6
- gate_blocks: bfloat16 [4, 4, 10, 128, 128], P('blk', 'dp'), may hold values from -0.5 to 0.5
- up_blocks: bfloat16 [4, 4, 10, 128, 128], P('blk', 'dp'), may hold values from -0.5 to 0.5
- down_blocks: bfloat16 [4, 4, 10, 128, 128], P('blk', 'dp'), may hold values from -0.25 to 0.25
- gate_slots: int32 [4, 4, 10], P('blk'), may hold values from 0 to 256, as said below
- up_slots: int32 [4, 4, 10], P('blk'), may hold values from 0 to 256, as said below
- down_slots: int32 [4, 4, 10], P('blk'), may hold values from 0 to 256, as said below
Outputs:
- input_grad: bfloat16 [1024, 4096], P(('groups', 'dp'), 'blk'), parts along dimension 0
- gate_grad: bfloat16 [8, 4, 10, 128, 128], P(('groups', 'blk'), 'dp'), parts along dimension 0
- up_grad: bfloat16 [8, 4, 10, 128, 128], P(('groups', 'blk'), 'dp'), parts along dimension 0
- down_grad: bfloat16 [8, 4, 10, 128, 128], P(('groups', 'blk'), 'dp'), parts along dimension 0
There are 2 independent parts, one for each index of `groups`. A program takes and returns all parts, laid end to end along the dimension named above; an argument that names none is the same for every part. Nothing has to cross between parts.
Inputs may be any that keep to these rules, and one draw needn't show every extreme that they name: `gate_slots`: for each matrix and each [r, k], the entries of [r, k, :] that are below 256 come first and are distinct; the remaining slots hold 256. At most 10 kept blocks per matrix on one [r, k], and in every draw some [r, k] uses all 10 slots. `up_slots`: as for gate_slots. `down_slots`: as for gate_slots.
All inputs are finite; a program needn't handle non-finite values.
Results may differ from a plain program's by a relative error of at most 0.005.
Values may be sent and summed in bfloat16 or wider, within the bound.
No kernel may reach another device: no remote copies, remote signals or barrier semaphores. Data moves between devices by JAX's collectives and lax.ppermute only.
A program may use at most 320 MiB of HBM per device.

v0:
```python
import jax
import jax.numpy as jnp
from jax import lax
from jax.sharding import PartitionSpec as P

D = 4096
FF = 16384
BLOCK = 128


def slot_layout(slot_ids, local_rows, local_cols, owners):
    block_limit = local_rows * local_cols
    usable = slot_ids < block_limit
    clipped = jnp.minimum(slot_ids, block_limit - 1)
    owner_ids = jnp.arange(owners, dtype=jnp.int32)[:, None]
    row_global = owner_ids * local_rows + clipped // local_cols
    return (usable.reshape(-1), row_global.reshape(-1), (clipped % local_cols).reshape(-1))


def own_layout(slot_ids, local_rows, local_cols):
    block_limit = local_rows * local_cols
    clipped = jnp.minimum(slot_ids, block_limit - 1)
    return (slot_ids < block_limit, clipped // local_cols, clipped % local_cols)


def hot_table(index_list, width_total, usable, dtype):
    matches = index_list[:, None] == jnp.arange(width_total, dtype=jnp.int32)[None, :]
    return (matches & usable[:, None]).astype(dtype)


def unpack_dense(blocks, first_hot, second_hot):
    slot_total = blocks.shape[0]
    spread = (blocks[:, :, None, :] * second_hot[:, None, :, None]).reshape(slot_total, -1)
    placed = lax.dot_general(
        first_hot, spread, (((0,), (0,)), ((), ())), preferred_element_type=jnp.float32
    )
    return placed.astype(jnp.bfloat16).reshape(
        first_hot.shape[1] * BLOCK, second_hot.shape[1] * BLOCK
    )


def select_blocks(total, first_index, second_index, first_count, second_count):
    first_hot = (first_index[:, None] == jnp.arange(first_count, dtype=jnp.int32)[None, :]).astype(
        jnp.float32
    )
    second_hot = (
        second_index[:, None] == jnp.arange(second_count, dtype=jnp.int32)[None, :]
    ).astype(jnp.float32)
    rows_picked = jnp.dot(
        first_hot, total.reshape(first_count, -1), precision=lax.Precision.HIGHEST
    )
    rows_picked = rows_picked.reshape(first_index.shape[0], BLOCK, second_count, BLOCK)
    return jnp.sum(rows_picked * second_hot[:, None, :, None], axis=2)


def finish_blocks(total, usable):
    return (total * usable[:, None, None].astype(jnp.float32)).astype(jnp.bfloat16)[None, None]


def shards(inputs, out_grad, gate_blocks, up_blocks, down_blocks, gate_slots, up_slots, down_slots):
    dp_count = lax.axis_size("dp")
    local_rows = D // (BLOCK * dp_count)
    local_cols = FF // (BLOCK * lax.axis_size("blk"))
    row_blocks = D // BLOCK
    full_inputs, full_grads = (
        lax.all_gather(inputs, "blk", axis=1, tiled=True),
        lax.all_gather(out_grad, "blk", axis=1, tiled=True),
    )
    gathered = (
        lax.all_gather(gate_blocks, "dp", axis=1, tiled=True),
        lax.all_gather(up_blocks, "dp", axis=1, tiled=True),
        lax.all_gather(down_blocks, "dp", axis=1, tiled=True),
    )
    gate_all = gathered[0].reshape(-1, BLOCK, BLOCK)
    up_all = gathered[1].reshape(-1, BLOCK, BLOCK)
    down_all = gathered[2].reshape(-1, BLOCK, BLOCK)
    gate_use, gate_row, gate_col = slot_layout(gate_slots[0], local_rows, local_cols, dp_count)
    up_use, up_row, up_col = slot_layout(up_slots[0], local_rows, local_cols, dp_count)
    down_use, down_row, down_col = slot_layout(down_slots[0], local_rows, local_cols, dp_count)
    gate_dense = unpack_dense(
        gate_all,
        hot_table(gate_row, row_blocks, gate_use, jnp.bfloat16),
        hot_table(gate_col, local_cols, gate_use, jnp.bfloat16),
    )
    up_dense = unpack_dense(
        up_all,
        hot_table(up_row, row_blocks, up_use, jnp.bfloat16),
        hot_table(up_col, local_cols, up_use, jnp.bfloat16),
    )
    down_dense = unpack_dense(
        down_all,
        hot_table(down_col, local_cols, down_use, jnp.bfloat16),
        hot_table(down_row, row_blocks, down_use, jnp.bfloat16),
    )
    gate_pre = jnp.dot(full_inputs, gate_dense, preferred_element_type=jnp.float32)
    up_pre = jnp.dot(full_inputs, up_dense, preferred_element_type=jnp.float32)
    hidden_delta = jnp.einsum(
        "td,fd->tf", full_grads, down_dense, preferred_element_type=jnp.float32
    )
    sigmoid_gate = jax.nn.sigmoid(gate_pre)
    activated = gate_pre * sigmoid_gate
    hidden_act = (activated * up_pre).astype(jnp.bfloat16)
    gate_delta = (
        hidden_delta * up_pre * sigmoid_gate * (1.0 + gate_pre * (1.0 - sigmoid_gate))
    ).astype(jnp.bfloat16)
    up_delta = (hidden_delta * activated).astype(jnp.bfloat16)
    feature_part = jnp.einsum(
        "tf,df->td", gate_delta, gate_dense, preferred_element_type=jnp.float32
    )
    feature_part = feature_part + jnp.einsum(
        "tf,df->td", up_delta, up_dense, preferred_element_type=jnp.float32
    )
    input_grad = lax.psum_scatter(feature_part, "blk", scatter_dimension=1, tiled=True).astype(
        jnp.bfloat16
    )
    mine_inputs, mine_grads = (
        lax.all_to_all(full_inputs, "dp", split_axis=1, concat_axis=0, tiled=True),
        lax.all_to_all(full_grads, "dp", split_axis=1, concat_axis=0, tiled=True),
    )
    own_index = lax.axis_index("dp")
    gate_own = own_layout(
        lax.dynamic_index_in_dim(gate_slots[0], own_index, 0, keepdims=False),
        local_rows,
        local_cols,
    )
    up_own = own_layout(
        lax.dynamic_index_in_dim(up_slots[0], own_index, 0, keepdims=False), local_rows, local_cols
    )
    down_own = own_layout(
        lax.dynamic_index_in_dim(down_slots[0], own_index, 0, keepdims=False),
        local_rows,
        local_cols,
    )
    gate_piece = lax.all_gather(gate_delta, "dp", axis=0, tiled=True)
    up_piece = lax.all_gather(up_delta, "dp", axis=0, tiled=True)
    hidden_piece = lax.all_gather(hidden_act, "dp", axis=0, tiled=True)
    contract = (((0,), (0,)), ((), ()))
    gate_term = lax.dot_general(
        mine_inputs, gate_piece, contract, preferred_element_type=jnp.float32
    )
    up_term = lax.dot_general(mine_inputs, up_piece, contract, preferred_element_type=jnp.float32)
    down_term = lax.dot_general(
        hidden_piece, mine_grads, contract, preferred_element_type=jnp.float32
    )
    gate_total = gate_term
    up_total = up_term
    down_total = down_term
    gate_total = select_blocks(gate_total, gate_own[1], gate_own[2], local_rows, local_cols)
    up_total = select_blocks(up_total, up_own[1], up_own[2], local_rows, local_cols)
    down_total = select_blocks(down_total, down_own[2], down_own[1], local_cols, local_rows)
    gate_grad = finish_blocks(gate_total, gate_own[0])
    up_grad = finish_blocks(up_total, up_own[0])
    down_grad = finish_blocks(down_total, down_own[0])
    return (input_grad, gate_grad, up_grad, down_grad)


def solution(mesh):
    in_specs = (
        P(("groups", "dp"), "blk"),
        P(("groups", "dp"), "blk"),
        P("blk", "dp", None, None, None),
        P("blk", "dp", None, None, None),
        P("blk", "dp", None, None, None),
        P("blk", None, None),
        P("blk", None, None),
        P("blk", None, None),
    )
    out_specs = (
        P(("groups", "dp"), "blk"),
        P(("groups", "blk"), "dp", None, None, None),
        P(("groups", "blk"), "dp", None, None, None),
        P(("groups", "blk"), "dp", None, None, None),
    )
    return jax.shard_map(shards, mesh=mesh, in_specs=in_specs, out_specs=out_specs, check_vma=False)
```

profile of v0, /device:TPU:8, one launch (start us, length us, event | category | flops | bytes accessed | tf_op | source)
XLA Modules:
  0.0 853.3 jit_solution(15286448379233074644)
XLA Ops:
  7.2 0.7 all-gather.17.cloned.1.call-update
  7.9 0.7 all-gather.9.cloned.1.call-update
  8.7 0.7 all-gather.13.cloned.1.call-update
  9.4 1.8 copy.25
  11.3 1.8 copy.23
  13.2 0.7 broadcast_minimum_fusion
  13.9 0.7 broadcast_compare_fusion
  14.5 0.7 broadcast_minimum_fusion.2
  15.2 0.7 broadcast_compare_fusion.2
  15.9 0.7 broadcast_minimum_fusion.1
  16.6 0.7 broadcast_compare_fusion.1
  17.4 0.1 add.143
  17.4 0.1 min.79
  17.5 0.1 min.81
  17.6 0.1 min.83
  17.7 0.1 lt.95
  17.8 0.1 lt.90
  17.9 0.1 lt.92
  18.1 0.1 fusion.21
  18.2 10.7 %all-gather.17.cloned.1.call-done = bf16[1,4,10,128,128]{4,3,2,0,1:T(8,128)(2,1)} async-done(((bf16[1,1,10,128,128]{4,3,2,0,1:T(8,128)(2,1)}), bf16[1,4,10,128,128]{4,3,2,0,1:T(8,128)(2,1)}) %all-gather.17.cloned.1.call-update) | async-done | bytes 1310736 | tf_op jit(solution)/shard_map/all_gather | solution.py:70
  28.9 14.8 %broadcast_multiply_fusion = bf16[40,128,32,128]{3,2,1,0:T(8,128)(2,1)} fusion(bf16[40,32]{1,0:T(8,128)(2,1)S(1)} %fusion.25, bf16[40,128,128]{2,1,0:T(8,128)(2,1)} %bitcast.151), kind=kLoop, calls=%fused_computation.11 | loop fusion | flops 20971520 | bytes 43256320 | tf_op jit(solution)/shard_map/mul | solution.py:33
  43.8 105.9 %convolution_convert_fusion = bf16[32,524288]{1,0:T(8,128)(2,1)} fusion(bf16[5,8,4096,128]{3,2,1,0:T(8,128)(2,1)} %bitcast.141, s32[40]{0:T(128)S(1)} %get-tuple-element.19, pred[40]{0:T(512)(128)(4,1)S(1)} %lt.95), kind=kOutput, calls=%fused_computation | convolution fusion | flops 1358957056 | bytes 75497672 | tf_op jit(solution)/shard_map/dot_general | solution.py:34
  149.7 41.6 %reshape.558 = bf16[4096,4096]{1,0:T(8,128)(2,1)} reshape(bf16[32,524288]{1,0:T(8,128)(2,1)} %convolution_convert_fusion) | data formatting | bytes 67108864 | tf_op jit(solution)/shard_map/reshape | solution.py:37
  191.3 14.4 %broadcast_multiply_fusion.2 = bf16[40,128,32,128]{3,2,1,0:T(8,128)(2,1)} fusion(bf16[40,32]{1,0:T(8,128)(2,1)S(1)} %fusion.17, bf16[40,128,128]{2,1,0:T(8,128)(2,1)} %bitcast.150), kind=kLoop, calls=%fused_computation.13 | loop fusion | flops 20971520 | bytes 43256320 | tf_op jit(solution)/shard_map/mul | solution.py:33
  205.7 106.1 %convolution_convert_fusion.2 = bf16[32,524288]{1,0:T(8,128)(2,1)} fusion(bf16[5,8,4096,128]{3,2,1,0:T(8,128)(2,1)} %bitcast.142, s32[40]{0:T(128)S(1)} %get-tuple-element.22, pred[40]{0:T(512)(128)(4,1)S(1)} %lt.90), kind=kOutput, calls=%fused_computation.2 | convolution fusion | flops 1358957056 | bytes 75497672 | tf_op jit(solution)/shard_map/dot_general | solution.py:34
  311.7 41.8 %reshape.556 = bf16[4096,4096]{1,0:T(8,128)(2,1)} reshape(bf16[32,524288]{1,0:T(8,128)(2,1)} %convolution_convert_fusion.2) | data formatting | bytes 67108864 | tf_op jit(solution)/shard_map/reshape | solution.py:37
  353.5 14.4 %broadcast_multiply_fusion.1 = bf16[40,128,32,128]{3,2,1,0:T(8,128)(2,1)} fusion(bf16[40,32]{1,0:T(8,128)(2,1)S(1)} %fusion.21, bf16[40,128,128]{2,1,0:T(8,128)(2,1)} %bitcast.149), kind=kLoop, calls=%fused_computation.12 | loop fusion | flops 20971520 | bytes 43256320 | tf_op jit(solution)/shard_map/mul | solution.py:33
  367.9 106.1 %convolution_convert_fusion.1 = bf16[32,524288]{1,0:T(8,128)(2,1)} fusion(bf16[5,8,4096,128]{3,2,1,0:T(8,128)(2,1)} %bitcast.140, s32[40]{0:T(128)S(1)} %get-tuple-element.17, pred[40]{0:T(512)(128)(4,1)S(1)} %lt.92), kind=kOutput, calls=%fused_computation.1 | convolution fusion | flops 1358957056 | bytes 75497672 | tf_op jit(solution)/shard_map/dot_general | solution.py:34
  474.0 41.6 %reshape.557 = bf16[4096,4096]{1,0:T(8,128)(2,1)} reshape(bf16[32,524288]{1,0:T(8,128)(2,1)} %convolution_convert_fusion.1) | data formatting | bytes 67108864 | tf_op jit(solution)/shard_map/reshape | solution.py:37
  515.6 15.5 %convolution_bitcast_fusion.2 = f32[128,4096]{0,1:T(8,128)S(1)} fusion(bf16[4096,4096]{1,0:T(8,128)(2,1)} %reshape.558, bf16[128,4096]{0,1:T(8,128)(2,1)} %all-gather.15.cloned.1.call-done), kind=kOutput, calls=%fused_computation.19 | convolution fusion | flops 4294967296 | bytes 36700160 | tf_op jit(solution)/shard_map/dot_general | solution.py:95
  531.2 15.0 %convolution_bitcast_fusion.4 = f32[128,4096]{0,1:T(8,128)S(1)} fusion(bf16[4096,4096]{1,0:T(8,128)(2,1)} %reshape.556, bf16[128,4096]{0,1:T(8,128)(2,1)} %all-gather.11.cloned.1.call-done), kind=kOutput, calls=%fused_computation.21 | convolution fusion | flops 4294967296 | bytes 36700160 | tf_op jit(solution)/shard_map/td,fd->tf/dot_general | solution.py:97
  546.2 17.3 %multiply_convert_fusion = (bf16[128,4096]{0,1:T(8,128)(2,1)}, bf16[128,4096]{0,1:T(8,128)(2,1)S(1)}, bf16[128,4096]{0,1:T(8,128)(2,1)}) fusion(f32[128,4096]{0,1:T(8,128)S(1)} %convolution_bitcast_fusion.2, f32[128,4096]{0,1:T(8,128)S(1)} %convolution_bitcast_fusion.4, bf16[4096,4096]{1,0:T(8,128)(2,1)} %reshape.557, ...), kind=kOutput, calls=%fused_computation.23 | convolution fusion | flops 4302831616 | bytes 41943040 | tf_op jit(solution)/shard_map/dot_general | solution.py:96
  563.4 16.3 %fusion.50 = f32[128,4096]{1,0:T(8,128)S(1)} fusion(bf16[128,4096]{0,1:T(8,128)(2,1)S(1)} %get-tuple-element.15, bf16[4096,4096]{1,0:T(8,128)(2,1)} %reshape.558), kind=kOutput, calls=%fused_computation.122 | convolution fusion | flops 4294967296 | bytes 36700160 | tf_op jit(solution)/shard_map/tf,df->td/dot_general | solution.py:107
  579.8 17.2 %convolution_add_fusion = f32[128,4096]{1,0:T(8,128)} fusion(f32[128,4096]{1,0:T(8,128)S(1)} %fusion.50, bf16[128,4096]{0,1:T(8,128)(2,1)} %get-tuple-element.16, bf16[4096,4096]{1,0:T(8,128)(2,1)} %reshape.557), kind=kOutput, calls=%fused_computation.22 | convolution fusion | flops 4295491584 | bytes 38797312 | tf_op jit(solution)/shard_map/tf,df->td/dot_general | solution.py:110
  597.1 0.7 all-gather.21.cloned.1.call-update
  597.8 0.7 all-gather.23.cloned.1.call-update
  598.5 3.5 all-to-all-start
  602.2 0.6 all-gather.19.cloned.1.call-update
  602.8 13.7 %all-to-all-done = bf16[128,4,1024]{0,2,1:T(8,128)(2,1)S(1)} async-done(((bf16[128,4,1024]{0,2,1:T(8,128)(2,1)}), bf16[128,4,1024]{0,2,1:T(8,128)(2,1)S(1)}, u32[]{:S(2)}, u32[]{:S(2)}) %all-to-all-start) | async-done | bytes 1048608 | tf_op jit(solution)/shard_map/all_to_all | solution.py:117
  616.5 3.7 all-to-all-start.1
  620.3 0.5 copy.27
  620.9 13.8 %all-to-all-done.1 = bf16[128,4,1024]{0,2,1:T(8,128)(2,1)S(1)} async-done(((bf16[128,4,1024]{0,2,1:T(8,128)(2,1)}), bf16[128,4,1024]{0,2,1:T(8,128)(2,1)S(1)}, u32[]{:S(2)}, u32[]{:S(2)}) %all-to-all-start.1) | async-done | bytes 1048608 | tf_op jit(solution)/shard_map/all_to_all | solution.py:118
  634.6 0.5 copy.30
  635.2 3.7 reduce-scatter.2.cloned.1.call-done
  638.8 1.8 convert_element_type.140
  640.6 36.5 %all-gather.21.cloned.1.call-done = bf16[512,4096]{0,1:T(8,128)(2,1)} async-done(((bf16[128,4096]{0,1:T(8,128)(2,1)}), bf16[512,4096]{0,1:T(8,128)(2,1)}) %all-gather.21.cloned.1.call-update) | async-done | bytes 4194320 | tf_op jit(solution)/shard_map/all_gather | solution.py:135
  677.1 11.0 %convolution_bitcast_fusion = f32[1024,4096]{0,1:T(8,128)} fusion(bf16[512,4096]{0,1:T(8,128)(2,1)} %all-gather.21.cloned.1.call-done, bf16[512,1024]{1,0:T(8,128)(2,1)S(1)} %bitcast.152), kind=kOutput, calls=%fused_computation.16 | convolution fusion | flops 4294967296 | bytes 22020096 | tf_op jit(solution)/shard_map/dot_general | solution.py:141
  688.1 17.5 %copy.29 = f32[1024,4096]{1,0:T(8,128)} copy(f32[1024,4096]{0,1:T(8,128)} %convolution_bitcast_fusion) | data formatting | bytes 33554432 | tf_op jit(solution)/shard_map/dot_general | solution.py:141
  705.6 14.5 %reshape.560 = f32[8,524288]{1,0:T(8,128)} reshape(f32[1024,4096]{1,0:T(8,128)} %copy.29) | data formatting | bytes 33554432 | tf_op jit(solution)/shard_map/reshape | solution.py:50
  720.1 18.0 %multiply_reduce_fusion = f32[10,128,128]{2,0,1:T(8,128)S(1)} fusion(f32[10,32]{0,1:T(8,128)S(1)} %fusion.27, f32[128,32,128,8]{2,3,1,0:T(8,128)} %bitcast.143, s32[10]{0:T(128)S(1)} %get-tuple-element.10), kind=kOutput, calls=%fused_computation.9 | convolution fusion | flops 513638464 | bytes 17433896 | tf_op jit(solution)/shard_map/dot_general | solution.py:49
  738.0 0.2 fusion.12
  738.2 0.8 copy.33
  739.0 10.9 %fusion.51 = f32[4096,1024]{1,0:T(8,128)} fusion(bf16[512,4096]{0,1:T(8,128)(2,1)} %all-gather.23.cloned.1.call-done, bf16[512,1024]{1,0:T(8,128)(2,1)S(1)} %bitcast.154), kind=kOutput, calls=%fused_computation.123 | convolution fusion | flops 4294967296 | bytes 22020096 | tf_op jit(solution)/shard_map/dot_general | solution.py:142
  749.9 12.1 %reshape.561 = f32[32,131072]{1,0:T(8,128)} reshape(f32[4096,1024]{1,0:T(8,128)} %fusion.51) | data formatting | bytes 33554432 | tf_op jit(solution)/shard_map/reshape | solution.py:50
  762.0 9.4 %copy.41 = f32[4,8,1024,128]{3,2,1,0:T(8,128)S(1)} copy(f32[4,8,1024,128]{3,1,2,0:T(8,128)} %bitcast.146) | data formatting | bytes 33554432
  771.4 13.1 %multiply_reduce_fusion.2 = f32[10,128,128]{2,0,1:T(8,128)S(1)} fusion(f32[10,8]{0,1:T(8,128)S(1)} %fusion.41, f32[128,8,128,32]{2,1,0,3:T(8,128)S(1)} %bitcast.145, s32[10]{0:T(128)S(1)} %get-tuple-element.8), kind=kOutput, calls=%fused_computation.18 | convolution fusion | flops 505774400 | bytes 17432936 | tf_op jit(solution)/shard_map/dot_general | solution.py:49
  784.5 0.2 fusion.11
  784.6 0.8 copy.34
  785.5 10.5 %convolution_bitcast_fusion.1 = f32[1024,4096]{0,1:T(8,128)} fusion(bf16[512,4096]{0,1:T(8,128)(2,1)} %all-gather.19.cloned.1.call-done, bf16[512,1024]{1,0:T(8,128)(2,1)S(1)} %bitcast.153), kind=kOutput, calls=%fused_computation.17 | convolution fusion | flops 4294967296 | bytes 22020096 | tf_op jit(solution)/shard_map/dot_general | solution.py:138
  796.0 17.5 %copy.28 = f32[1024,4096]{1,0:T(8,128)} copy(f32[1024,4096]{0,1:T(8,128)} %convolution_bitcast_fusion.1) | data formatting | bytes 33554432 | tf_op jit(solution)/shard_map/dot_general | solution.py:138
  813.4 14.5 %reshape.559 = f32[8,524288]{1,0:T(8,128)} reshape(f32[1024,4096]{1,0:T(8,128)} %copy.28) | data formatting | bytes 33554432 | tf_op jit(solution)/shard_map/reshape | solution.py:50
  827.9 17.7 %multiply_reduce_fusion.1 = f32[10,128,128]{2,0,1:T(8,128)S(1)} fusion(f32[10,32]{0,1:T(8,128)S(1)} %fusion.26, f32[128,32,128,8]{2,3,1,0:T(8,128)} %bitcast.144, s32[10]{0:T(128)S(1)} %get-tuple-element.12), kind=kOutput, calls=%fused_computation.10 | convolution fusion | flops 513638464 | bytes 17433896 | tf_op jit(solution)/shard_map/dot_general | solution.py:49
  845.6 0.2 fusion.13
  845.8 0.8 copy.32
  (41 shorter events, 0.8 us)
Async XLA Ops:
  7.2 21.8 %all-gather.17.cloned.1.call-start = ((), (), s32[]{:S(2)}) async-start(), calls=%async_computation.7 | async-start | bytes 1638400 | tf_op jit(solution)/shard_map/all_gather | solution.py:70
  7.9 183.4 %all-gather.9.cloned.1.call-start = ((), (), s32[]{:S(2)}) async-start(), calls=%async_computation.3 | async-start | bytes 1638400 | tf_op jit(solution)/shard_map/all_gather | solution.py:72
  8.6 344.9 %all-gather.13.cloned.1.call-start = ((), (), s32[]{:S(2)}) async-start(), calls=%async_computation.5 | async-start | bytes 1638400 | tf_op jit(solution)/shard_map/all_gather | solution.py:71
  9.4 506.2 %all-gather.15.cloned.1.call-start = ((), (), s32[]{:S(2)}) async-start(), calls=%async_computation.6 | async-start | bytes 1310720 | tf_op jit(solution)/shard_map/all_gather | solution.py:66
  11.2 519.9 %all-gather.11.cloned.1.call-start = ((), (), s32[]{:S(2)}) async-start(), calls=%async_computation.4 | async-start | bytes 1310720 | tf_op jit(solution)/shard_map/all_gather | solution.py:67
  13.1 625.7 %reduce-scatter.2.cloned.1.call-start = ((), (), s32[]{:S(2)}) async-start(), calls=%async_computation.8 | async-start | bytes 2621440 | tf_op jit(solution)/shard_map/reduce_scatter | solution.py:113
  563.4 16.3 %copy-start = (bf16[128,4096]{0,1:T(8,128)(2,1)}, bf16[128,4096]{0,1:T(8,128)(2,1)S(1)}, u32[]{:S(2)}) copy-start(bf16[128,4096]{0,1:T(8,128)(2,1)S(1)} %get-tuple-element.15) | copy-start | bytes 3145732
  579.7 22.4 %copy-start.2 = (s32[1,4,10]{2,1,0:T(4,128)S(1)}, s32[1,4,10]{2,1,0:T(4,128)}, u32[]{:S(2)}) copy-start(s32[1,4,10]{2,1,0:T(4,128)} %param.14) | copy-start | bytes 484
  579.7 22.4 %copy-start.1 = (s32[1,4,10]{2,1,0:T(4,128)S(1)}, s32[1,4,10]{2,1,0:T(4,128)}, u32[]{:S(2)}) copy-start(s32[1,4,10]{2,1,0:T(4,128)} %param.15) | copy-start | bytes 484
  579.8 22.4 %copy-start.3 = (s32[1,4,10]{2,1,0:T(4,128)S(1)}, s32[1,4,10]{2,1,0:T(4,128)}, u32[]{:S(2)}) copy-start(s32[1,4,10]{2,1,0:T(4,128)} %param.13) | copy-start | bytes 484
  597.0 80.0 %all-gather.21.cloned.1.call-start = ((), (), s32[]{:S(2)}) async-start(), calls=%async_computation.10 | async-start | bytes 5242880 | tf_op jit(solution)/shard_map/all_gather | solution.py:135
  597.8 141.2 %all-gather.23.cloned.1.call-start = ((), (), s32[]{:S(2)}) async-start(), calls=%async_computation.11 | async-start | bytes 5242880 | tf_op jit(solution)/shard_map/all_gather | solution.py:136
  598.5 18.0 %all-to-all-start = ((bf16[128,4,1024]{0,2,1:T(8,128)(2,1)}), bf16[128,4,1024]{0,2,1:T(8,128)(2,1)S(1)}, u32[]{:S(2)}, u32[]{:S(2)}) async-start(bf16[128,4,1024]{0,2,1:T(8,128)(2,1)} %bitcast.12), calls=%async_computation.1 | async-start | bytes 2097152 | tf_op jit(solution)/shard_map/all_to_all | solution.py:117
  602.1 183.4 %all-gather.19.cloned.1.call-start = ((), (), s32[]{:S(2)}) async-start(), calls=%async_computation.9 | async-start | bytes 5242880 | tf_op jit(solution)/shard_map/all_gather | solution.py:134
  616.5 18.1 %all-to-all-start.1 = ((bf16[128,4,1024]{0,2,1:T(8,128)(2,1)}), bf16[128,4,1024]{0,2,1:T(8,128)(2,1)S(1)}, u32[]{:S(2)}, u32[]{:S(2)}) async-start(bf16[128,4,1024]{0,2,1:T(8,128)(2,1)} %bitcast.31), calls=%async_computation.2 | async-start | bytes 2097152 | tf_op jit(solution)/shard_map/all_to_all | solution.py:118
Sparse Core Ops, SparseCore 0:
  9.6 19.3 all-gather.16
  30.5 18.2 all-gather.8
  50.3 18.1 all-gather.12
  70.5 27.8 all-gather.14
  100.5 27.4 all-gather.10
  597.2 41.6 reduce-scatter.1
  640.5 36.5 all-gather.20
  678.7 35.0 all-gather.22
  715.4 35.0 all-gather.18
where the time goes:
time: 870 us; the launch traced here: 853 us
  matrix products  480 us (55%)
  local copies, waits for them, and re-layouts  218 us (25%)
  waiting for transfers between devices  82.4 us (9%)
  other arithmetic  50.3 us (6%)
  between operations  14.3 us (2%)
    dot_general x3, matrix products, unpack_dense(): lax.dot_general(first_hot, spread, (((0,), (0,)), ((), ())), preferred_el...  318 us
    reshape x3, local copies, waits for them, and re-layouts, unpack_dense(): placed.astype(jnp.bfloat16)  125 us
    dot_general x3, matrix products, select_blocks(): jnp.dot(first_hot, total.reshape(first_count, -1), precision=lax.Precisio...  48.8 us
    mul x3, other arithmetic, unpack_dense(): blocks[:, :, None, :] * second_hot[:, None, :, None]  43.6 us
    reshape x3, local copies, waits for them, and re-layouts, select_blocks(): total.reshape(first_count, -1)  41 us
    all_gather x1, waiting for transfers between devices, shards(): up_piece = lax.all_gather(up_delta, 'dp', axis=0, tiled=True)  36.5 us
    dot_general x1, local copies, waits for them, and re-layouts, shards(): lax.dot_general(mine_inputs, up_piece, contract, preferred_element_type=j...  17.5 us
    dot_general x1, local copies, waits for them, and re-layouts, shards(): lax.dot_general(mine_inputs, gate_piece, contract, preferred_element_type...  17.5 us
  transfers between devices with their start and end apart: 11, of which 5 were waited for; matrix products, arithmetic and copies ran while one was open for 73% of the time, Pallas kernels for 0%

commit v1 on v0

v1 whole, which is shorter than its diff:
```python
import functools

import jax
import jax.numpy as jnp
from jax import lax
from jax.experimental import pallas as pl
from jax.experimental.pallas import tpu as pltpu
from jax.sharding import PartitionSpec as P

BLOCK = 128
F32 = jnp.float32
BF16 = jnp.bfloat16
NN = (((1,), (0,)), ((), ()))
NT = (((1,), (1,)), ((), ()))


def line_pieces(x, axis):
    n = lax.axis_size(axis)
    to_right = [(i, i + 1) for i in range(n - 1)]
    to_left = [(i + 1, i) for i in range(n - 1)]
    pieces, offsets = [x], [0]
    rightward = leftward = x
    for step in range(1, n):
        rightward = lax.ppermute(rightward, axis, to_right)
        leftward = lax.ppermute(leftward, axis, to_left)
        pieces += [rightward, leftward]
        offsets += [-step, step]
    return pieces, offsets


def xor_swap(x, axis, bit):
    return lax.ppermute(x, axis, [(i, i ^ bit) for i in range(lax.axis_size(axis))])


def xor_gather(x, axis):
    n = lax.axis_size(axis)
    held = {0: x}
    bit = n // 2
    while bit:
        held.update({place ^ bit: xor_swap(piece, axis, bit) for place, piece in held.items()})
        bit //= 2
    return [held[place] for place in range(n)]


def compute_kernel(
    dims, offsets, where_ref, gate_ref, up_ref, down_ref, *refs
):
    n_dp, cap, row_count, col_count, shard_blocks, n_blk = dims
    n_pieces = len(offsets)
    x_refs, g_refs = refs[:n_pieces], refs[n_pieces : 2 * n_pieces]
    at = 2 * n_pieces
    w_refs = refs[at : at + n_dp]
    at += n_dp
    part_refs = refs[at : at + n_dp]
    at += n_dp
    far_refs = refs[at : at + n_blk - 1]
    at += n_blk - 1
    own_ref = refs[at]
    at += 1
    (xs, xt, gs, gate_acc, up_acc, down_acc, tmp, gate_delta, up_delta, act_t, feature_acc) = refs[at:]
    slot_refs = (gate_ref, up_ref, down_ref)
    me_blk, me_dp = where_ref[0], where_ref[1]
    limit = row_count * col_count

    for offset, x_ref, g_ref in zip(offsets, x_refs, g_refs):
        shard = me_blk + offset

        @pl.when((shard >= 0) & (shard < n_blk))
        def _():
            for b in range(shard_blocks):
                piece = x_ref[:, b * BLOCK : (b + 1) * BLOCK]
                xs[shard * shard_blocks + b] = piece
                xt[shard * shard_blocks + b] = piece.T
                gs[shard * shard_blocks + b] = g_ref[:, b * BLOCK : (b + 1) * BLOCK]

    for acc in (gate_acc, up_acc, down_acc):
        acc[...] = jnp.zeros_like(acc)
    feature_acc[...] = jnp.zeros_like(feature_acc)

    def place(matrix, owner, slot):
        entry = slot_refs[matrix][owner, slot]
        kept = jnp.minimum(entry, limit - 1)
        return entry < limit, owner * row_count + kept // col_count, kept % col_count

    for j in range(n_dp):
        owner = me_dp ^ j
        for matrix, source, acc, form in ((0, xs, gate_acc, NN), (1, xs, up_acc, NN), (2, gs, down_acc, NT)):
            for s in range(cap):
                _, row, _ = place(matrix, owner, s)
                tmp[s] = lax.dot_general(
                    source[row], w_refs[j][matrix * cap + s], form, preferred_element_type=F32
                )
            for s in range(cap):
                used, _, col = place(matrix, owner, s)
                acc[jnp.where(used, col, col_count)] += tmp[s]

    def deltas(c, _):
        gate, up, hidden = gate_acc[c], up_acc[c], down_acc[c]
        sig = jax.nn.sigmoid(gate)
        activated = gate * sig
        act_t[c] = (activated * up).astype(BF16).T
        gate_delta[c] = (hidden * up * sig * (1.0 + gate * (1.0 - sig))).astype(BF16)
        up_delta[c] = (hidden * activated).astype(BF16)
        return 0

    lax.fori_loop(0, col_count, deltas, 0)

    for j in range(n_dp):
        owner = me_dp ^ j
        for matrix, delta in ((0, gate_delta), (1, up_delta)):
            for s in range(cap):
                _, _, col = place(matrix, owner, s)
                tmp[s] = lax.dot_general(
                    delta[col], w_refs[j][matrix * cap + s], NT, preferred_element_type=F32
                )
            for s in range(cap):
                used, row, _ = place(matrix, owner, s)
                feature_acc[jnp.where(used, row, n_blk * shard_blocks)] += tmp[s]

    for b in range(shard_blocks):
        own_ref[:, b * BLOCK : (b + 1) * BLOCK] = feature_acc[me_blk * shard_blocks + b]
    for shift in range(1, n_blk):
        shard = lax.rem(me_blk + shift, n_blk)
        for b in range(shard_blocks):
            far_refs[shift - 1][:, b * BLOCK : (b + 1) * BLOCK] = feature_acc[
                shard * shard_blocks + b
            ].astype(BF16)

    for j in range(n_dp):
        owner = me_dp ^ j
        for matrix in range(3):
            for s in range(cap):
                used, row, col = place(matrix, owner, s)
                if matrix == 2:
                    left, right = act_t[col], gs[row]
                else:
                    left, right = xt[row], (gate_delta, up_delta)[matrix][col]
                product = lax.dot_general(left, right, NN, preferred_element_type=F32)
                part_refs[j][matrix * cap + s] = jnp.where(used, product, 0.0).astype(part_refs[j].dtype)


def shards(inputs, out_grad, gate_blocks, up_blocks, down_blocks, gate_slots, up_slots, down_slots):
    n_dp, n_blk = lax.axis_size("dp"), lax.axis_size("blk")
    tokens, width = inputs.shape
    cap = gate_blocks.shape[2]
    row_blocks = n_blk * width // BLOCK
    row_count = row_blocks // n_dp
    hidden = 16384 // n_blk
    col_count = hidden // BLOCK
    blocks = jnp.concatenate([gate_blocks[0, 0], up_blocks[0, 0], down_blocks[0, 0]])
    weights = xor_gather(blocks, "dp")
    x_pieces, offsets = line_pieces(inputs, "blk")
    g_pieces, _ = line_pieces(out_grad, "blk")
    where = jnp.stack([lax.axis_index("blk"), lax.axis_index("dp")]).astype(jnp.int32)
    vmem = pl.BlockSpec(memory_space=pltpu.VMEM)
    smem = pl.BlockSpec(memory_space=pltpu.SMEM)
    shard_blocks = width // BLOCK
    n_slots = 3 * cap
    dims = (n_dp, cap, row_count, col_count, shard_blocks, n_blk)
    sent_on = [F32 if j % 2 == 0 else BF16 for j in range(n_dp)]
    results = pl.pallas_call(
        functools.partial(compute_kernel, dims, offsets),
        out_shape=(
            [jax.ShapeDtypeStruct((n_slots, BLOCK, BLOCK), kind) for kind in sent_on]
            + [jax.ShapeDtypeStruct((tokens, width), BF16)] * (n_blk - 1)
            + [jax.ShapeDtypeStruct((tokens, width), F32)]
        ),
        in_specs=[smem] * 4 + [vmem] * (2 * len(offsets) + n_dp),
        out_specs=[vmem] * (n_dp + n_blk),
        scratch_shapes=[
            pltpu.VMEM((row_blocks, tokens, BLOCK), BF16),
            pltpu.VMEM((row_blocks, BLOCK, tokens), BF16),
            pltpu.VMEM((row_blocks, tokens, BLOCK), BF16),
            pltpu.VMEM((col_count + 1, tokens, BLOCK), F32),
            pltpu.VMEM((col_count + 1, tokens, BLOCK), F32),
            pltpu.VMEM((col_count + 1, tokens, BLOCK), F32),
            pltpu.VMEM((cap, tokens, BLOCK), F32),
            pltpu.VMEM((col_count, tokens, BLOCK), BF16),
            pltpu.VMEM((col_count, tokens, BLOCK), BF16),
            pltpu.VMEM((col_count, BLOCK, tokens), BF16),
            pltpu.VMEM((row_blocks + 1, tokens, BLOCK), F32),
        ],
        compiler_params=pltpu.CompilerParams(vmem_limit_bytes=52 * 1024 * 1024),
    )(where, gate_slots[0], up_slots[0], down_slots[0], *x_pieces, *g_pieces, *weights)

    parts, far, total = results[:n_dp], results[n_dp:-1], results[-1]
    for shift in range(1, n_blk):
        moved = lax.ppermute(
            far[shift - 1], "blk", [(i, (i + shift) % n_blk) for i in range(n_blk)]
        )
        total = total + moved.astype(F32)
    input_grad = total.astype(BF16)

    bit = 1
    while bit < n_dp:
        arrived = [
            xor_swap(parts[j + 1].astype(BF16), "dp", bit) for j in range(0, len(parts), 2)
        ]
        parts = [kept + other.astype(F32) for kept, other in zip(parts[::2], arrived)]
        bit *= 2
    grads = parts[0].astype(BF16).reshape(3, 1, 1, cap, BLOCK, BLOCK)
    return input_grad, grads[0], grads[1], grads[2]


def solution(mesh):
    in_specs = (
        P(("groups", "dp"), "blk"),
        P(("groups", "dp"), "blk"),
        P("blk", "dp", None, None, None),
        P("blk", "dp", None, None, None),
        P("blk", "dp", None, None, None),
        P("blk", None, None),
        P("blk", None, None),
        P("blk", None, None),
    )
    out_specs = (
        P(("groups", "dp"), "blk"),
        P(("groups", "blk"), "dp", None, None, None),
        P(("groups", "blk"), "dp", None, None, None),
        P(("groups", "blk"), "dp", None, None, None),
    )
    return jax.shard_map(shards, mesh=mesh, in_specs=in_specs, out_specs=out_specs, check_vma=False)
```

time: 870 us -> 112 us (0.13); the launches traced: 853 us -> 111 us
  matrix products: 480 us -> 0 us
  local copies, waits for them, and re-layouts: 218 us -> 1.03 us
  other arithmetic: 50.3 us -> 4.75 us
  waiting for transfers between devices: 82.4 us -> 46.5 us
  starting transfers between devices: 7.61 us -> 42.7 us
  Pallas kernels: 0 us -> 15.4 us
  between operations: 14.3 us -> 0.97 us
    dot_general x14 -> x0, matrix products: 480 us -> none  [the longest x3 318 us: unpack_dense(): lax.dot_general(first_hot, spread, (((0,), (0,)), ((), ())), preferred_el...]
    reshape x6 -> x0, local copies, waits for them, and re-layouts: 166 us -> none  [the longest x3 125 us: unpack_dense(): placed.astype(jnp.bfloat16)]
    all_gather x8 -> x0, waiting for transfers between devices: 47.2 us -> none  [the longest x1 36.5 us: shards(): up_piece = lax.all_gather(up_delta, 'dp', axis=0, tiled=True)]
    ppermute x0 -> x21, waiting for transfers between devices: none -> 46.5 us  [the longest x3 22.2 us: shards(): lax.ppermute(far[shift - 1], 'blk', [(i, (i + shift) % n_blk) for i in ra...]
    mul x4 -> x0, other arithmetic: 43.6 us -> none  [the longest x3 43.6 us: unpack_dense(): blocks[:, :, None, :] * second_hot[:, None, :, None]]
    ppermute x0 -> x21, starting transfers between devices: none -> 42.7 us  [the longest x6 20.3 us: line_pieces(): rightward = lax.ppermute(rightward, axis, to_right)]
    dot_general x2 -> x0, local copies, waits for them, and re-layouts: 35 us -> none  [the longest x1 17.5 us: shards(): lax.dot_general(mine_inputs, up_piece, contract, preferred_element_type=j...]
    all_to_all x2 -> x0, waiting for transfers between devices: 27.5 us -> none  [the longest x1 13.8 us: shards(): lax.all_to_all(full_grads, 'dp', split_axis=1, concat_axis=0, tiled=True)]
  transfers between devices with their start and end apart: 11 -> 21, of which waited for: 5 -> 10; matrix products, arithmetic and copies ran while one was open for 73% -> 3% of each run, Pallas kernels for 0% -> 0%
where the time goes in v1:
time: 112 us; the launch traced here: 111 us
  waiting for transfers between devices  46.5 us (42%)
  starting transfers between devices  42.7 us (38%)
  Pallas kernels  15.4 us (14%)
  other arithmetic  4.75 us (4%)
    ppermute x3, waiting for transfers between devices, shards(): lax.ppermute(far[shift - 1], 'blk', [(i, (i + shift) % n_blk) for i in ra...  22.2 us
    ppermute x6, starting transfers between devices, line_pieces(): rightward = lax.ppermute(rightward, axis, to_right)  20.3 us
    pallas_call x1, Pallas kernels, shards(): pl.pallas_call(functools.partial(compute_kernel, dims, offsets), out_shap...  15.4 us
    ppermute x6, waiting for transfers between devices, xor_swap(): lax.ppermute(x, axis, [(i, i ^ bit) for i in range(lax.axis_size(axis))])  14.8 us
    ppermute x6, starting transfers between devices, line_pieces(): leftward = lax.ppermute(leftward, axis, to_left)  14.8 us
    ppermute x6, waiting for transfers between devices, line_pieces(): leftward = lax.ppermute(leftward, axis, to_left)  7.09 us
    ppermute x3, starting transfers between devices, shards(): lax.ppermute(far[shift - 1], 'blk', [(i, (i + shift) % n_blk) for i in ra...  3.91 us
    ppermute x6, starting transfers between devices, xor_swap(): lax.ppermute(x, axis, [(i, i ^ bit) for i in range(lax.axis_size(axis))])  3.7 us
  transfers between devices with their start and end apart: 21, of which 10 were waited for; matrix products, arithmetic and copies ran while one was open for 3% of the time, Pallas kernels for 0%

profile of v1, /device:TPU:8, one launch (start us, length us, event | category | flops | bytes accessed | tf_op | source)
XLA Modules:
  0.0 111.3 jit_solution(11136498478803468229)
XLA Ops:
  0.6 0.0 copy-start
  0.6 0.0 copy-start.8
  0.7 0.0 copy-start.3
  0.7 0.0 copy-start.2
  0.7 0.0 copy-start.1
  0.7 1.3 %pad_maximum_fusion.refs_14_ = bf16[30,128,128]{2,1,0:T(8,128)(2,1)S(1)} fusion(bf16[10,128,128]{2,1,0:T(8,128)(2,1)} %bitcast.17, bf16[10,128,128]{2,1,0:T(8,128)(2,1)} %bitcast.18, bf16[10,128,128]{2,1,0:T(8,128)(2,1)} %bitcast.19), kind=kLoop, calls=%fused_computation.2 | loop fusion | flops 983040 | bytes 1966080 | tf_op jit(solution)/shard_map/concatenate | solution.py:150
  2.0 0.0 copy-start.4
  2.0 1.6 %collective-permute-start.13 = (bf16[30,128,128]{2,1,0:T(8,128)(2,1)S(1)}, bf16[30,128,128]{2,1,0:T(8,128)(2,1)S(1)}, u32[]{:S(2)}, u32[]{:S(2)}) collective-permute-start(bf16[30,128,128]{2,1,0:T(8,128)(2,1)S(1)} %pad_maximum_fusion.refs_14_), channel_id=1, source_target_pairs={{0,2},{1,3},{2,0},{3,1},{4,6},{5,7},{6,4},{7,5},{8,10},{9,11},{10,... | collective-permute-start | bytes 2949128 | tf_op jit(solution)/shard_map/ppermute | solution.py:32
  3.6 0.0 copy-done
  3.6 3.5 %collective-permute-start = (bf16[128,1024]{1,0:T(8,128)(2,1)S(1)}, bf16[128,1024]{1,0:T(8,128)(2,1)S(1)}, u32[]{:S(2)}, u32[]{:S(2)}) collective-permute-start(bf16[128,1024]{1,0:T(8,128)(2,1)S(1)} %copy-done), channel_id=1, source_target_pairs={{0,4},{4,8},{8,12},{1,5},{5,9},{9,13},{2,6},{6,10},{10,14},{3,7},{... | collective-permute-start | bytes 786440 | tf_op jit(solution)/shard_map/ppermute | solution.py:24
  7.1 2.4 %collective-permute-start.1 = (bf16[128,1024]{1,0:T(8,128)(2,1)S(1)}, bf16[128,1024]{1,0:T(8,128)(2,1)S(1)}, u32[]{:S(2)}, u32[]{:S(2)}) collective-permute-start(bf16[128,1024]{1,0:T(8,128)(2,1)S(1)} %copy-done), channel_id=1, source_target_pairs={{4,0},{8,4},{12,8},{5,1},{9,5},{13,9},{6,2},{10,6},{14,10},{7,3},{... | collective-permute-start | bytes 786440 | tf_op jit(solution)/shard_map/ppermute | solution.py:25
  9.4 0.0 copy-done.8
  9.5 3.5 %collective-permute-start.6 = (bf16[128,1024]{1,0:T(8,128)(2,1)S(1)}, bf16[128,1024]{1,0:T(8,128)(2,1)S(1)}, u32[]{:S(2)}, u32[]{:S(2)}) collective-permute-start(bf16[128,1024]{1,0:T(8,128)(2,1)S(1)} %copy-done.8), channel_id=1, source_target_pairs={{0,4},{4,8},{8,12},{1,5},{5,9},{9,13},{2,6},{6,10},{10,14},{3,7},{... | collective-permute-start | bytes 786440 | tf_op jit(solution)/shard_map/ppermute | solution.py:24
  12.9 0.1 collective-permute-start.12
  13.0 12.6 %collective-permute-done.13.refs_16_ = bf16[30,128,128]{2,1,0:T(8,128)(2,1)S(1)} collective-permute-done((bf16[30,128,128]{2,1,0:T(8,128)(2,1)S(1)}, bf16[30,128,128]{2,1,0:T(8,128)(2,1)S(1)}, u32[]{:S(2)}, u32[]{:S(2)}) %collective-permute-start.13) | collective-permute-done | bytes 983072 | tf_op jit(solution)/shard_map/ppermute | solution.py:32
  25.6 0.0 collective-permute-start.14
  25.6 0.0 collective-permute-done.refs_1_
  25.6 2.1 %collective-permute-start.7 = (bf16[128,1024]{1,0:T(8,128)(2,1)S(1)}, bf16[128,1024]{1,0:T(8,128)(2,1)S(1)}, u32[]{:S(2)}, u32[]{:S(2)}) collective-permute-start(bf16[128,1024]{1,0:T(8,128)(2,1)S(1)} %copy-done.8), channel_id=1, source_target_pairs={{4,0},{8,4},{12,8},{5,1},{9,5},{13,9},{6,2},{10,6},{14,10},{7,3},{... | collective-permute-start | bytes 786440 | tf_op jit(solution)/shard_map/ppermute | solution.py:25
  27.7 0.0 collective-permute-done.1.refs_2_
  27.7 3.7 %collective-permute-start.2 = (bf16[128,1024]{1,0:T(8,128)(2,1)S(1)}, bf16[128,1024]{1,0:T(8,128)(2,1)S(1)}, u32[]{:S(2)}, u32[]{:S(2)}) collective-permute-start(bf16[128,1024]{1,0:T(8,128)(2,1)S(1)} %collective-permute-done.refs_1_), channel_id=1, source_target_pairs={{0,4},{4,8},{8,12},{1,5},{5,9},{9,13},{2,6},{6,10},{10,14},{3,7},{... | collective-permute-start | bytes 786440 | tf_op jit(solution)/shard_map/ppermute | solution.py:24
  31.5 0.0 collective-permute-done.6.refs_8_
  31.5 0.0 copy-start.9
  31.5 2.1 %collective-permute-start.3 = (bf16[128,1024]{1,0:T(8,128)(2,1)S(1)}, bf16[128,1024]{1,0:T(8,128)(2,1)}, u32[]{:S(2)}, u32[]{:S(2)}) collective-permute-start(bf16[128,1024]{1,0:T(8,128)(2,1)S(1)} %collective-permute-done.1.refs_2_), channel_id=1, source_target_pairs={{4,0},{8,4},{12,8},{5,1},{9,5},{13,9},{6,2},{10,6},{14,10},{7,3},{... | collective-permute-start | bytes 786440 | tf_op jit(solution)/shard_map/ppermute | solution.py:25
  33.6 2.8 %collective-permute-done.7.refs_9_ = bf16[128,1024]{1,0:T(8,128)(2,1)S(1)} collective-permute-done((bf16[128,1024]{1,0:T(8,128)(2,1)S(1)}, bf16[128,1024]{1,0:T(8,128)(2,1)S(1)}, u32[]{:S(2)}, u32[]{:S(2)}) %collective-permute-start.7) | collective-permute-done | bytes 262176 | tf_op jit(solution)/shard_map/ppermute | solution.py:25
  36.4 3.5 %collective-permute-start.8 = (bf16[128,1024]{1,0:T(8,128)(2,1)S(1)}, bf16[128,1024]{1,0:T(8,128)(2,1)S(1)}, u32[]{:S(2)}, u32[]{:S(2)}) collective-permute-start(bf16[128,1024]{1,0:T(8,128)(2,1)S(1)} %collective-permute-done.6.refs_8_), channel_id=1, source_target_pairs={{0,4},{4,8},{8,12},{1,5},{5,9},{9,13},{2,6},{6,10},{10,14},{3,7},{... | collective-permute-start | bytes 786440 | tf_op jit(solution)/shard_map/ppermute | solution.py:24
  39.9 0.0 collective-permute-done.2.refs_3_
  39.9 2.4 %collective-permute-start.9 = (bf16[128,1024]{1,0:T(8,128)(2,1)S(1)}, bf16[128,1024]{1,0:T(8,128)(2,1)}, u32[]{:S(2)}, u32[]{:S(2)}) collective-permute-start(bf16[128,1024]{1,0:T(8,128)(2,1)S(1)} %collective-permute-done.7.refs_9_), channel_id=1, source_target_pairs={{4,0},{8,4},{12,8},{5,1},{9,5},{13,9},{6,2},{10,6},{14,10},{7,3},{... | collective-permute-start | bytes 786440 | tf_op jit(solution)/shard_map/ppermute | solution.py:25
  42.3 0.0 collective-permute-done.3.refs_4_
  42.3 3.5 %collective-permute-start.4 = (bf16[128,1024]{1,0:T(8,128)(2,1)S(1)}, bf16[128,1024]{1,0:T(8,128)(2,1)S(1)}, u32[]{:S(2)}, u32[]{:S(2)}) collective-permute-start(bf16[128,1024]{1,0:T(8,128)(2,1)S(1)} %collective-permute-done.2.refs_3_), channel_id=1, source_target_pairs={{0,4},{4,8},{8,12},{1,5},{5,9},{9,13},{2,6},{6,10},{10,14},{3,7},{... | collective-permute-start | bytes 786440 | tf_op jit(solution)/shard_map/ppermute | solution.py:24
  45.8 0.4 collective-permute-done.8.refs_10_
  46.2 2.0 %collective-permute-start.5 = (bf16[128,1024]{1,0:T(8,128)(2,1)}, bf16[128,1024]{1,0:T(8,128)(2,1)}, u32[]{:S(2)}, u32[]{:S(2)}) collective-permute-start(bf16[128,1024]{1,0:T(8,128)(2,1)} %collective-permute-done.3.refs_4_), channel_id=1, source_target_pairs={{4,0},{8,4},{12,8},{5,1},{9,5},{13,9},{6,2},{10,6},{14,10},{7,3},{... | collective-permute-start | bytes 786440 | tf_op jit(solution)/shard_map/ppermute | solution.py:25
  48.2 1.1 %collective-permute-done.9.refs_11_ = bf16[128,1024]{1,0:T(8,128)(2,1)} collective-permute-done((bf16[128,1024]{1,0:T(8,128)(2,1)S(1)}, bf16[128,1024]{1,0:T(8,128)(2,1)}, u32[]{:S(2)}, u32[]{:S(2)}) %collective-permute-start.9) | collective-permute-done | bytes 262176 | tf_op jit(solution)/shard_map/ppermute | solution.py:25
  49.3 2.7 %collective-permute-start.10 = (bf16[128,1024]{1,0:T(8,128)(2,1)S(1)}, bf16[128,1024]{1,0:T(8,128)(2,1)}, u32[]{:S(2)}, u32[]{:S(2)}) collective-permute-start(bf16[128,1024]{1,0:T(8,128)(2,1)S(1)} %collective-permute-done.8.refs_10_), channel_id=1, source_target_pairs={{0,4},{4,8},{8,12},{1,5},{5,9},{9,13},{2,6},{6,10},{10,14},{3,7},{... | collective-permute-start | bytes 786440 | tf_op jit(solution)/shard_map/ppermute | solution.py:24
  52.1 0.0 collective-permute-done.4.refs_5_
  52.1 0.0 copy-done.10
  52.1 0.0 copy-start.12
  52.1 3.8 %collective-permute-start.11 = (bf16[128,1024]{1,0:T(8,128)(2,1)}, bf16[128,1024]{1,0:T(8,128)(2,1)}, u32[]{:S(2)}, u32[]{:S(2)}) collective-permute-start(bf16[128,1024]{1,0:T(8,128)(2,1)} %collective-permute-done.9.refs_11_), channel_id=1, source_target_pairs={{4,0},{8,4},{12,8},{5,1},{9,5},{13,9},{6,2},{10,6},{14,10},{7,3},{... | collective-permute-start | bytes 786440 | tf_op jit(solution)/shard_map/ppermute | solution.py:25
  55.9 0.0 copy-done.12
  55.9 0.1 pad_add_fusion.where_ref
  56.0 0.0 collective-permute-done.5.refs_6_
  56.0 1.9 %collective-permute-done.10.refs_12_ = bf16[128,1024]{1,0:T(8,128)(2,1)} collective-permute-done((bf16[128,1024]{1,0:T(8,128)(2,1)S(1)}, bf16[128,1024]{1,0:T(8,128)(2,1)}, u32[]{:S(2)}, u32[]{:S(2)}) %collective-permute-start.10) | collective-permute-done | bytes 262176 | tf_op jit(solution)/shard_map/ppermute | solution.py:24
  57.8 3.1 %collective-permute-done.11.refs_13_ = bf16[128,1024]{1,0:T(8,128)(2,1)} collective-permute-done((bf16[128,1024]{1,0:T(8,128)(2,1)}, bf16[128,1024]{1,0:T(8,128)(2,1)}, u32[]{:S(2)}, u32[]{:S(2)}) %collective-permute-start.11) | collective-permute-done | bytes 262176 | tf_op jit(solution)/shard_map/ppermute | solution.py:25
  61.0 0.0 collective-permute-done.12.refs_15_
  61.0 0.0 collective-permute-done.14.refs_17_
  61.0 0.0 copy-done.4
  61.0 0.0 copy-done.6
  61.1 15.4 %shard_map.111 = (f32[30,128,128]{2,1,0:T(8,128)}, bf16[30,128,128]{2,1,0:T(8,128)(2,1)}, f32[30,128,128]{2,1,0:T(8,128)}, bf16[30,128,128]{2,1,0:T(8,128)(2,1)}...) custom-call(s32[2]{0:T(128)S(1)} %pad_add_fusion.where_ref, ...), custom_call_target="tpu_custom_call" | custom-call | tf_op jit(solution)/shard_map/pallas_call | solution.py:161
  76.5 0.0 collective-permute-start.19
  76.5 0.5 collective-permute-start.18
  77.0 2.3 %collective-permute-done.19 = bf16[30,128,128]{2,1,0:T(8,128)(2,1)S(1)} collective-permute-done((bf16[30,128,128]{2,1,0:T(8,128)(2,1)}, bf16[30,128,128]{2,1,0:T(8,128)(2,1)S(1)}, u32[]{:S(2)}, u32[]{:S(2)}) %collective-permute-start.19) | collective-permute-done | bytes 983072 | tf_op jit(solution)/shard_map/ppermute | solution.py:32
  79.3 2.0 %add_convert_fusion.1 = bf16[30,128,128]{2,1,0:T(8,128)(2,1)S(1)} fusion(f32[30,128,128]{2,1,0:T(8,128)} %get-tuple-element.18, bf16[30,128,128]{2,1,0:T(8,128)(2,1)S(1)} %collective-permute-done.19), kind=kLoop, calls=%fused_computation.1 | loop fusion | flops 1474560 | bytes 3932160 | tf_op jit(solution)/shard_map/convert_element_type | solution.py:197
  81.3 1.6 %collective-permute-start.20 = (bf16[30,128,128]{2,1,0:T(8,128)(2,1)S(1)}, bf16[30,128,128]{2,1,0:T(8,128)(2,1)S(1)}, u32[]{:S(2)}, u32[]{:S(2)}) collective-permute-start(bf16[30,128,128]{2,1,0:T(8,128)(2,1)S(1)} %add_convert_fusion.1), channel_id=1, source_target_pairs={{0,2},{1,3},{2,0},{3,1},{4,6},{5,7},{6,4},{7,5},{8,10},{9,11},{10,... | collective-permute-start | bytes 2949128 | tf_op jit(solution)/shard_map/ppermute | solution.py:32
  82.9 2.0 %collective-permute-start.15 = (bf16[128,1024]{1,0:T(8,128)(2,1)S(1)}, bf16[128,1024]{1,0:T(8,128)(2,1)S(1)}, u32[]{:S(2)}, u32[]{:S(2)}) collective-permute-start(bf16[128,1024]{1,0:T(8,128)(2,1)S(1)} %get-tuple-element.13), channel_id=1, source_target_pairs={{0,4},{4,8},{8,12},{12,0},{1,5},{5,9},{9,13},{13,1},{2,6},{6,10},{... | collective-permute-start | bytes 786440 | tf_op jit(solution)/shard_map/ppermute | solution.py:188
  84.8 1.9 %collective-permute-start.16 = (bf16[128,1024]{1,0:T(8,128)(2,1)S(1)}, bf16[128,1024]{1,0:T(8,128)(2,1)S(1)}, u32[]{:S(2)}, u32[]{:S(2)}) collective-permute-start(bf16[128,1024]{1,0:T(8,128)(2,1)S(1)} %get-tuple-element.14), channel_id=1, source_target_pairs={{0,8},{4,12},{8,0},{12,4},{1,9},{5,13},{9,1},{13,5},{2,10},{6,14},... | collective-permute-start | bytes 786440 | tf_op jit(solution)/shard_map/ppermute | solution.py:188
  86.8 0.0 collective-permute-start.17
  86.8 16.0 %collective-permute-done.15 = bf16[128,1024]{1,0:T(8,128)(2,1)S(1)} collective-permute-done((bf16[128,1024]{1,0:T(8,128)(2,1)S(1)}, bf16[128,1024]{1,0:T(8,128)(2,1)S(1)}, u32[]{:S(2)}, u32[]{:S(2)}) %collective-permute-start.15) | collective-permute-done | bytes 262176 | tf_op jit(solution)/shard_map/ppermute | solution.py:188
  102.8 4.5 %collective-permute-done.16 = bf16[128,1024]{1,0:T(8,128)(2,1)S(1)} collective-permute-done((bf16[128,1024]{1,0:T(8,128)(2,1)S(1)}, bf16[128,1024]{1,0:T(8,128)(2,1)S(1)}, u32[]{:S(2)}, u32[]{:S(2)}) %collective-permute-start.16) | collective-permute-done | bytes 262176 | tf_op jit(solution)/shard_map/ppermute | solution.py:188
  107.3 1.7 %collective-permute-done.17 = bf16[128,1024]{1,0:T(8,128)(2,1)S(1)} collective-permute-done((bf16[128,1024]{1,0:T(8,128)(2,1)S(1)}, bf16[128,1024]{1,0:T(8,128)(2,1)S(1)}, u32[]{:S(2)}, u32[]{:S(2)}) %collective-permute-start.17) | collective-permute-done | bytes 262176 | tf_op jit(solution)/shard_map/ppermute | solution.py:188
  109.0 0.0 copy-done.7
  109.0 0.9 add_convert_fusion.2
  109.9 0.0 collective-permute-done.18
  109.9 0.0 collective-permute-done.20
  109.9 0.5 add_convert_fusion
  110.4 1.0 slice_bitcast_fusion
  (11 shorter events, 0.0 us)
Async XLA Ops:
  0.6 3.0 %copy-start = (bf16[128,1024]{1,0:T(8,128)(2,1)S(1)}, bf16[128,1024]{1,0:T(8,128)(2,1)}, u32[]{:S(2)}) copy-start(bf16[128,1024]{1,0:T(8,128)(2,1)} %refs_0_.1) | copy-start | bytes 786436
  0.6 8.8 %copy-start.8 = (bf16[128,1024]{1,0:T(8,128)(2,1)S(1)}, bf16[128,1024]{1,0:T(8,128)(2,1)}, u32[]{:S(2)}) copy-start(bf16[128,1024]{1,0:T(8,128)(2,1)} %refs_7_.1) | copy-start | bytes 786436
  0.7 60.4 %copy-start.3 = (s32[1,4,10]{2,1,0:T(4,128)S(1)}, s32[1,4,10]{2,1,0:T(4,128)}, u32[]{:S(2)}) copy-start(s32[1,4,10]{2,1,0:T(4,128)} %param.15) | copy-start | bytes 484
  0.7 60.4 %copy-start.2 = (s32[1,4,10]{2,1,0:T(4,128)S(1)}, s32[1,4,10]{2,1,0:T(4,128)}, u32[]{:S(2)}) copy-start(s32[1,4,10]{2,1,0:T(4,128)} %param.14) | copy-start | bytes 484
  0.7 60.4 %copy-start.1 = (s32[1,4,10]{2,1,0:T(4,128)S(1)}, s32[1,4,10]{2,1,0:T(4,128)}, u32[]{:S(2)}) copy-start(s32[1,4,10]{2,1,0:T(4,128)} %param.13) | copy-start | bytes 484
  2.0 59.0 %copy-start.4 = (bf16[30,128,128]{2,1,0:T(8,128)(2,1)}, bf16[30,128,128]{2,1,0:T(8,128)(2,1)S(1)}, u32[]{:S(2)}) copy-start(bf16[30,128,128]{2,1,0:T(8,128)(2,1)S(1)} %pad_maximum_fusion.refs_14_) | copy-start | bytes 2949124
  2.0 23.6 %collective-permute-start.13 = (bf16[30,128,128]{2,1,0:T(8,128)(2,1)S(1)}, bf16[30,128,128]{2,1,0:T(8,128)(2,1)S(1)}, u32[]{:S(2)}, u32[]{:S(2)}) collective-permute-start(bf16[30,128,128]{2,1,0:T(8,128)(2,1)S(1)} %pad_maximum_fusion.refs_14_), channel_id=1, source_target_pairs={{0,2},{1,3},{2,0},{3,1},{4,6},{5,7},{6,4},{7,5},{8,10},{9,11},{10,... | collective-permute-start | bytes 2949128 | tf_op jit(solution)/shard_map/ppermute | solution.py:32
  3.6 22.0 %collective-permute-start = (bf16[128,1024]{1,0:T(8,128)(2,1)S(1)}, bf16[128,1024]{1,0:T(8,128)(2,1)S(1)}, u32[]{:S(2)}, u32[]{:S(2)}) collective-permute-start(bf16[128,1024]{1,0:T(8,128)(2,1)S(1)} %copy-done), channel_id=1, source_target_pairs={{0,4},{4,8},{8,12},{1,5},{5,9},{9,13},{2,6},{6,10},{10,14},{3,7},{... | collective-permute-start | bytes 786440 | tf_op jit(solution)/shard_map/ppermute | solution.py:24
  7.1 20.7 %collective-permute-start.1 = (bf16[128,1024]{1,0:T(8,128)(2,1)S(1)}, bf16[128,1024]{1,0:T(8,128)(2,1)S(1)}, u32[]{:S(2)}, u32[]{:S(2)}) collective-permute-start(bf16[128,1024]{1,0:T(8,128)(2,1)S(1)} %copy-done), channel_id=1, source_target_pairs={{4,0},{8,4},{12,8},{5,1},{9,5},{13,9},{6,2},{10,6},{14,10},{7,3},{... | collective-permute-start | bytes 786440 | tf_op jit(solution)/shard_map/ppermute | solution.py:25
  9.5 22.0 %collective-permute-start.6 = (bf16[128,1024]{1,0:T(8,128)(2,1)S(1)}, bf16[128,1024]{1,0:T(8,128)(2,1)S(1)}, u32[]{:S(2)}, u32[]{:S(2)}) collective-permute-start(bf16[128,1024]{1,0:T(8,128)(2,1)S(1)} %copy-done.8), channel_id=1, source_target_pairs={{0,4},{4,8},{8,12},{1,5},{5,9},{9,13},{2,6},{6,10},{10,14},{3,7},{... | collective-permute-start | bytes 786440 | tf_op jit(solution)/shard_map/ppermute | solution.py:24
  12.9 48.1 %collective-permute-start.12 = (bf16[30,128,128]{2,1,0:T(8,128)(2,1)S(1)}, bf16[30,128,128]{2,1,0:T(8,128)(2,1)}, u32[]{:S(2)}, u32[]{:S(2)}) collective-permute-start(bf16[30,128,128]{2,1,0:T(8,128)(2,1)S(1)} %pad_maximum_fusion.refs_14_), channel_id=1, source_target_pairs={{0,1},{1,0},{2,3},{3,2},{4,5},{5,4},{6,7},{7,6},{8,9},{9,8},{10,11... | collective-permute-start | bytes 2949128 | tf_op jit(solution)/shard_map/ppermute | solution.py:32
  25.6 35.4 %copy-start.6 = (bf16[30,128,128]{2,1,0:T(8,128)(2,1)}, bf16[30,128,128]{2,1,0:T(8,128)(2,1)S(1)}, u32[]{:S(2)}) copy-start(bf16[30,128,128]{2,1,0:T(8,128)(2,1)S(1)} %collective-permute-done.13.refs_16_) | copy-start | bytes 2949124
  25.6 35.4 %collective-permute-start.14 = (bf16[30,128,128]{2,1,0:T(8,128)(2,1)S(1)}, bf16[30,128,128]{2,1,0:T(8,128)(2,1)}, u32[]{:S(2)}, u32[]{:S(2)}) collective-permute-start(bf16[30,128,128]{2,1,0:T(8,128)(2,1)S(1)} %collective-permute-done.13.refs_16_), channel_id=1, source_target_pairs={{0,1},{1,0},{2,3},{3,2},{4,5},{5,4},{6,7},{7,6},{8,9},{9,8},{10,11... | collective-permute-start | bytes 2949128 | tf_op jit(solution)/shard_map/ppermute | solution.py:32
  25.6 10.8 %collective-permute-start.7 = (bf16[128,1024]{1,0:T(8,128)(2,1)S(1)}, bf16[128,1024]{1,0:T(8,128)(2,1)S(1)}, u32[]{:S(2)}, u32[]{:S(2)}) collective-permute-start(bf16[128,1024]{1,0:T(8,128)(2,1)S(1)} %copy-done.8), channel_id=1, source_target_pairs={{4,0},{8,4},{12,8},{5,1},{9,5},{13,9},{6,2},{10,6},{14,10},{7,3},{... | collective-permute-start | bytes 786440 | tf_op jit(solution)/shard_map/ppermute | solution.py:25
  27.7 12.2 %collective-permute-start.2 = (bf16[128,1024]{1,0:T(8,128)(2,1)S(1)}, bf16[128,1024]{1,0:T(8,128)(2,1)S(1)}, u32[]{:S(2)}, u32[]{:S(2)}) collective-permute-start(bf16[128,1024]{1,0:T(8,128)(2,1)S(1)} %collective-permute-done.refs_1_), channel_id=1, source_target_pairs={{0,4},{4,8},{8,12},{1,5},{5,9},{9,13},{2,6},{6,10},{10,14},{3,7},{... | collective-permute-start | bytes 786440 | tf_op jit(solution)/shard_map/ppermute | solution.py:24
  31.5 29.5 %copy-start.9 = (bf16[128,1024]{1,0:T(8,128)(2,1)}, bf16[128,1024]{1,0:T(8,128)(2,1)S(1)}, u32[]{:S(2)}) copy-start(bf16[128,1024]{1,0:T(8,128)(2,1)S(1)} %collective-permute-done.6.refs_8_) | copy-start | bytes 786436
  31.5 10.8 %collective-permute-start.3 = (bf16[128,1024]{1,0:T(8,128)(2,1)S(1)}, bf16[128,1024]{1,0:T(8,128)(2,1)}, u32[]{:S(2)}, u32[]{:S(2)}) collective-permute-start(bf16[128,1024]{1,0:T(8,128)(2,1)S(1)} %collective-permute-done.1.refs_2_), channel_id=1, source_target_pairs={{4,0},{8,4},{12,8},{5,1},{9,5},{13,9},{6,2},{10,6},{14,10},{7,3},{... | collective-permute-start | bytes 786440 | tf_op jit(solution)/shard_map/ppermute | solution.py:25
  36.4 15.7 %copy-start.10 = (bf16[128,1024]{1,0:T(8,128)(2,1)}, bf16[128,1024]{1,0:T(8,128)(2,1)S(1)}, u32[]{:S(2)}) copy-start(bf16[128,1024]{1,0:T(8,128)(2,1)S(1)} %collective-permute-done.7.refs_9_) | copy-start | bytes 786436
  36.4 9.8 %collective-permute-start.8 = (bf16[128,1024]{1,0:T(8,128)(2,1)S(1)}, bf16[128,1024]{1,0:T(8,128)(2,1)S(1)}, u32[]{:S(2)}, u32[]{:S(2)}) collective-permute-start(bf16[128,1024]{1,0:T(8,128)(2,1)S(1)} %collective-permute-done.6.refs_8_), channel_id=1, source_target_pairs={{0,4},{4,8},{8,12},{1,5},{5,9},{9,13},{2,6},{6,10},{10,14},{3,7},{... | collective-permute-start | bytes 786440 | tf_op jit(solution)/shard_map/ppermute | solution.py:24
  39.9 9.4 %collective-permute-start.9 = (bf16[128,1024]{1,0:T(8,128)(2,1)S(1)}, bf16[128,1024]{1,0:T(8,128)(2,1)}, u32[]{:S(2)}, u32[]{:S(2)}) collective-permute-start(bf16[128,1024]{1,0:T(8,128)(2,1)S(1)} %collective-permute-done.7.refs_9_), channel_id=1, source_target_pairs={{4,0},{8,4},{12,8},{5,1},{9,5},{13,9},{6,2},{10,6},{14,10},{7,3},{... | collective-permute-start | bytes 786440 | tf_op jit(solution)/shard_map/ppermute | solution.py:25
  42.3 9.8 %collective-permute-start.4 = (bf16[128,1024]{1,0:T(8,128)(2,1)S(1)}, bf16[128,1024]{1,0:T(8,128)(2,1)S(1)}, u32[]{:S(2)}, u32[]{:S(2)}) collective-permute-start(bf16[128,1024]{1,0:T(8,128)(2,1)S(1)} %collective-permute-done.2.refs_3_), channel_id=1, source_target_pairs={{0,4},{4,8},{8,12},{1,5},{5,9},{9,13},{2,6},{6,10},{10,14},{3,7},{... | collective-permute-start | bytes 786440 | tf_op jit(solution)/shard_map/ppermute | solution.py:24
  46.2 14.8 %copy-start.11 = (bf16[128,1024]{1,0:T(8,128)(2,1)}, bf16[128,1024]{1,0:T(8,128)(2,1)S(1)}, u32[]{:S(2)}) copy-start(bf16[128,1024]{1,0:T(8,128)(2,1)S(1)} %collective-permute-done.8.refs_10_) | copy-start | bytes 786436
  46.2 9.8 %collective-permute-start.5 = (bf16[128,1024]{1,0:T(8,128)(2,1)}, bf16[128,1024]{1,0:T(8,128)(2,1)}, u32[]{:S(2)}, u32[]{:S(2)}) collective-permute-start(bf16[128,1024]{1,0:T(8,128)(2,1)} %collective-permute-done.3.refs_4_), channel_id=1, source_target_pairs={{4,0},{8,4},{12,8},{5,1},{9,5},{13,9},{6,2},{10,6},{14,10},{7,3},{... | collective-permute-start | bytes 786440 | tf_op jit(solution)/shard_map/ppermute | solution.py:25
  49.3 8.5 %collective-permute-start.10 = (bf16[128,1024]{1,0:T(8,128)(2,1)S(1)}, bf16[128,1024]{1,0:T(8,128)(2,1)}, u32[]{:S(2)}, u32[]{:S(2)}) collective-permute-start(bf16[128,1024]{1,0:T(8,128)(2,1)S(1)} %collective-permute-done.8.refs_10_), channel_id=1, source_target_pairs={{0,4},{4,8},{8,12},{1,5},{5,9},{9,13},{2,6},{6,10},{10,14},{3,7},{... | collective-permute-start | bytes 786440 | tf_op jit(solution)/shard_map/ppermute | solution.py:24
  52.1 3.8 %copy-start.12 = (bf16[128,1024]{1,0:T(8,128)(2,1)}, bf16[128,1024]{1,0:T(8,128)(2,1)S(1)}, u32[]{:S(2)}) copy-start(bf16[128,1024]{1,0:T(8,128)(2,1)S(1)} %collective-permute-done.4.refs_5_) | copy-start | bytes 786436
  52.1 8.9 %collective-permute-start.11 = (bf16[128,1024]{1,0:T(8,128)(2,1)}, bf16[128,1024]{1,0:T(8,128)(2,1)}, u32[]{:S(2)}, u32[]{:S(2)}) collective-permute-start(bf16[128,1024]{1,0:T(8,128)(2,1)} %collective-permute-done.9.refs_11_), channel_id=1, source_target_pairs={{4,0},{8,4},{12,8},{5,1},{9,5},{13,9},{6,2},{10,6},{14,10},{7,3},{... | collective-permute-start | bytes 786440 | tf_op jit(solution)/shard_map/ppermute | solution.py:25
  76.5 2.8 %collective-permute-start.19 = (bf16[30,128,128]{2,1,0:T(8,128)(2,1)}, bf16[30,128,128]{2,1,0:T(8,128)(2,1)S(1)}, u32[]{:S(2)}, u32[]{:S(2)}) collective-permute-start(bf16[30,128,128]{2,1,0:T(8,128)(2,1)} %get-tuple-element.19), channel_id=1, source_target_pairs={{0,1},{1,0},{2,3},{3,2},{4,5},{5,4},{6,7},{7,6},{8,9},{9,8},{10,11... | collective-permute-start | bytes 2949128 | tf_op jit(solution)/shard_map/ppermute | solution.py:32
  76.5 33.4 %collective-permute-start.18 = (bf16[30,128,128]{2,1,0:T(8,128)(2,1)}, bf16[30,128,128]{2,1,0:T(8,128)(2,1)S(1)}, u32[]{:S(2)}, u32[]{:S(2)}) collective-permute-start(bf16[30,128,128]{2,1,0:T(8,128)(2,1)} %get-tuple-element.17), channel_id=1, source_target_pairs={{0,1},{1,0},{2,3},{3,2},{4,5},{5,4},{6,7},{7,6},{8,9},{9,8},{10,11... | collective-permute-start | bytes 2949128 | tf_op jit(solution)/shard_map/ppermute | solution.py:32
  79.3 29.7 %copy-start.7 = (f32[128,1024]{1,0:T(8,128)S(1)}, f32[128,1024]{1,0:T(8,128)}, u32[]{:S(2)}) copy-start(f32[128,1024]{1,0:T(8,128)} %get-tuple-element.12) | copy-start | bytes 1572868
  79.3 30.6 %copy-start.5 = (f32[30,128,128]{2,1,0:T(8,128)S(1)}, f32[30,128,128]{2,1,0:T(8,128)}, u32[]{:S(2)}) copy-start(f32[30,128,128]{2,1,0:T(8,128)} %get-tuple-element.16) | copy-start | bytes 5898244
  81.3 28.6 %collective-permute-start.20 = (bf16[30,128,128]{2,1,0:T(8,128)(2,1)S(1)}, bf16[30,128,128]{2,1,0:T(8,128)(2,1)S(1)}, u32[]{:S(2)}, u32[]{:S(2)}) collective-permute-start(bf16[30,128,128]{2,1,0:T(8,128)(2,1)S(1)} %add_convert_fusion.1), channel_id=1, source_target_pairs={{0,2},{1,3},{2,0},{3,1},{4,6},{5,7},{6,4},{7,5},{8,10},{9,11},{10,... | collective-permute-start | bytes 2949128 | tf_op jit(solution)/shard_map/ppermute | solution.py:32
  82.9 19.9 %collective-permute-start.15 = (bf16[128,1024]{1,0:T(8,128)(2,1)S(1)}, bf16[128,1024]{1,0:T(8,128)(2,1)S(1)}, u32[]{:S(2)}, u32[]{:S(2)}) collective-permute-start(bf16[128,1024]{1,0:T(8,128)(2,1)S(1)} %get-tuple-element.13), channel_id=1, source_target_pairs={{0,4},{4,8},{8,12},{12,0},{1,5},{5,9},{9,13},{13,1},{2,6},{6,10},{... | collective-permute-start | bytes 786440 | tf_op jit(solution)/shard_map/ppermute | solution.py:188
  84.8 22.4 %collective-permute-start.16 = (bf16[128,1024]{1,0:T(8,128)(2,1)S(1)}, bf16[128,1024]{1,0:T(8,128)(2,1)S(1)}, u32[]{:S(2)}, u32[]{:S(2)}) collective-permute-start(bf16[128,1024]{1,0:T(8,128)(2,1)S(1)} %get-tuple-element.14), channel_id=1, source_target_pairs={{0,8},{4,12},{8,0},{12,4},{1,9},{5,13},{9,1},{13,5},{2,10},{6,14},... | collective-permute-start | bytes 786440 | tf_op jit(solution)/shard_map/ppermute | solution.py:188
  86.8 22.2 %collective-permute-start.17 = (bf16[128,1024]{1,0:T(8,128)(2,1)S(1)}, bf16[128,1024]{1,0:T(8,128)(2,1)S(1)}, u32[]{:S(2)}, u32[]{:S(2)}) collective-permute-start(bf16[128,1024]{1,0:T(8,128)(2,1)S(1)} %get-tuple-element.15), channel_id=1, source_target_pairs={{0,12},{4,0},{8,4},{12,8},{1,13},{5,1},{9,5},{13,9},{2,14},{6,2},{... | collective-permute-start | bytes 786440 | tf_op jit(solution)/shard_map/ppermute | solution.py:188

commit v2 on v1

v2 whole, which is shorter than its diff:
```python
import functools

import jax
import jax.numpy as jnp
from jax import lax
from jax.experimental import pallas as pl
from jax.experimental.pallas import tpu as pltpu
from jax.sharding import PartitionSpec as P

BLOCK = 128
FF = 16384
F32 = jnp.float32
BF16 = jnp.bfloat16
NN = (((1,), (0,)), ((), ()))
NT = (((1,), (1,)), ((), ()))
TN = (((0,), (0,)), ((), ()))
MIB = 1024 * 1024
LONGEST_RING = 8
EVEN_MIB, ODD_MIB, DELTA_MIB, INPUT_MIB, NEAR_MIB = 20, 24, 28, 16, 14
EVEN_COST, ODD_COST, DELTA_COST, INPUT_COST, NEAR_COST = 1, 1, 12, 12, 6


def rotate(x, axis, shift):
    n = lax.axis_size(axis)
    return lax.ppermute(x, axis, [(i, (i + shift) % n) for i in range(n)])


def xor_swap(x, axis, bit):
    return lax.ppermute(x, axis, [(i, i ^ bit) for i in range(lax.axis_size(axis))])


def ring_gather(x, g, axis, ready):
    n = lax.axis_size(axis)
    if n > LONGEST_RING:
        me = lax.axis_index(axis)
        return [
            [piece] + [
                lax.dynamic_index_in_dim(whole, (me - i + n) % n, 0, keepdims=False) for i in range(1, n)
            ]
            for piece, whole in ((x, lax.all_gather(x, axis)), (g, lax.all_gather(g, axis)))
        ]
    xs, gs = [x], [g]
    for step in range(1, n):
        xs.append(rotate(xs[-1], axis, 1))
        gs.append(rotate(after(gs[-1], *ready) if step == 2 else gs[-1], axis, 1))
    return xs, gs


def after(x, *others):
    return lax.optimization_barrier((x, *others))[0]


class Dims:
    def __init__(self, n_dp, n_blk, cap, tokens, width):
        self.n_dp, self.n_blk, self.cap, self.tokens, self.width = n_dp, n_blk, cap, tokens, width
        self.shard_blocks = width // BLOCK
        self.rows = n_blk * self.shard_blocks
        self.own_rows = self.rows // n_dp
        self.cols = FF // (BLOCK * n_blk)
        self.limit = self.own_rows * self.cols
        self.paired = self.own_rows == self.shard_blocks

    def here(self, meta):
        return meta[0], meta[1]

    def place(self, meta, matrix, owner, slot):
        entry = meta[2 + (matrix * self.n_dp + owner) * self.cap + slot]
        kept = jnp.minimum(entry, self.limit - 1)
        return entry < self.limit, owner * self.own_rows + kept // self.cols, kept % self.cols

    def spread(self, piece_ref, shard, target):
        for b in range(self.shard_blocks):
            target[shard * self.shard_blocks + b] = piece_ref[:, b * BLOCK : (b + 1) * BLOCK]


def block(d, group, matrix, slot):
    return group[0][matrix * d.cap + slot] if len(group) == 1 else group[matrix][slot]


def add_products(d, meta, matrix, owner, group, source, form, acc):
    for s in range(d.cap):
        used, row, col = d.place(meta, matrix, owner, s)
        acc[jnp.where(used, col, d.cols)] += lax.dot_general(
            source[row], block(d, group, matrix, s), form, preferred_element_type=F32
        )


def forward_products(d, meta, group, j, xs, gs, gate_acc, up_acc, hidden):
    me_blk, me_dp = d.here(meta)
    owner = me_dp ^ j
    add_products(d, meta, 0, owner, group, xs, NN, gate_acc)
    add_products(d, meta, 1, owner, group, xs, NN, up_acc)
    if d.paired:
        there = owner != shard_at(d, me_blk, d.n_blk - 1)
        pl.when(there)(functools.partial(add_products, d, meta, 2, owner, group, gs, NT, hidden))


def take_groups(refs, places):
    groups, at = {}, 0
    for j in places:
        size = 1 if j < 2 else 3
        groups[j] = refs[at : at + size]
        at += size
    return groups, refs[at:]


def shard_at(d, me, i):
    return lax.rem(me - i + d.n_blk, d.n_blk)


def even_kernel(d, meta, own_ref, *refs):
    x_refs, g_refs = refs[: d.n_blk - 1], refs[d.n_blk - 1 : 2 * d.n_blk - 3]
    groups, outs = take_groups(refs[2 * d.n_blk - 3 :], range(0, d.n_dp, 2))
    xs, gs, gate_acc, up_acc, hidden = outs
    me_blk, _ = d.here(meta)
    own_x, own_g = own_ref.at[0], own_ref.at[1]
    for i, x_ref in enumerate((own_x, *x_refs)):
        d.spread(x_ref, shard_at(d, me_blk, i), xs)
    for i, g_ref in enumerate((own_g, *g_refs)):
        d.spread(g_ref, shard_at(d, me_blk, i), gs)
    for acc in (gate_acc, up_acc, hidden):
        acc[...] = jnp.zeros_like(acc)
    for j, group in groups.items():
        forward_products(d, meta, group, j, xs, gs, gate_acc, up_acc, hidden)


def odd_kernel(d, meta, xs, gs, gate_even, up_even, *refs):
    groups, outs = take_groups(refs, range(1, d.n_dp, 2))
    gate_slope, up_slope, act, hidden, gate_acc, up_acc = outs
    for acc in (gate_acc, up_acc, hidden):
        acc[...] = jnp.zeros_like(acc)
    for j, group in groups.items():
        forward_products(d, meta, group, j, xs, gs, gate_acc, up_acc, hidden)

    def activation(c, _):
        gate, up = gate_even[c] + gate_acc[c], up_even[c] + up_acc[c]
        sig = jax.nn.sigmoid(gate)
        activated = gate * sig
        act[c] = (activated * up).astype(BF16)
        gate_slope[c] = up * sig * (1.0 + gate * (1.0 - sig))
        up_slope[c] = activated
        return 0

    lax.fori_loop(0, d.cols, activation, 0)


def partial_grads(d, j, meta, xs, gs, act, gate_delta, up_delta, out_ref):
    owner = meta[1] ^ j
    for matrix in (2, 0, 1):
        for s in range(d.cap):
            used, row, col = d.place(meta, matrix, owner, s)
            if matrix == 2:
                left, right = act[col], gs[row]
            else:
                left, right = xs[row], (gate_delta, up_delta)[matrix][col]
            product = lax.dot_general(left, right, TN, preferred_element_type=F32)
            out_ref[matrix * d.cap + s] = jnp.where(used, product, 0.0).astype(out_ref.dtype)


def delta_kernel(d, places, meta, xs, gs_early, act, gate_slope, up_slope, hidden_even, hidden_odd, g_ref, *refs):
    groups, outs = take_groups(refs, range(d.n_dp))
    gate_delta, up_delta, gs = outs[:3]
    part_refs, more = outs[3:-1], outs[-1]
    me_blk, me_dp = d.here(meta)
    last = shard_at(d, me_blk, d.n_blk - 1)
    gs[...] = gs_early[...]
    d.spread(g_ref, last, gs)
    more[...] = jnp.zeros_like(more)
    for j in range(d.n_dp):
        owner = me_dp ^ j
        late = functools.partial(add_products, d, meta, 2, owner, groups[j], gs, NT, more)
        if d.paired:
            pl.when(owner == last)(late)
        else:
            late()

    def deltas(c, _):
        total = (hidden_even[c] + hidden_odd[c]) + more[c]
        gate_delta[c] = (total * gate_slope[c]).astype(BF16)
        up_delta[c] = (total * up_slope[c]).astype(BF16)
        return 0

    lax.fori_loop(0, d.cols, deltas, 0)
    for j, part_ref in zip(places, part_refs):
        partial_grads(d, j, meta, xs, gs, act, gate_delta, up_delta, part_ref)


def input_kernel(d, meta, gate_delta, up_delta, *refs):
    groups, outs = take_groups(refs, range(d.n_dp))
    out_refs, acc = outs[:-1], outs[-1]
    me_blk, me_dp = d.here(meta)
    acc[...] = jnp.zeros_like(acc)
    for j in range(d.n_dp):
        owner = me_dp ^ j
        for matrix, delta in ((0, gate_delta), (1, up_delta)):
            for s in range(d.cap):
                used, row, col = d.place(meta, matrix, owner, s)
                acc[jnp.where(used, row, d.rows)] += lax.dot_general(
                    delta[col], block(d, groups[j], matrix, s), NT, preferred_element_type=F32
                )
    for shift, out_ref in enumerate(out_refs):
        shard = lax.rem(me_blk + shift, d.n_blk)
        for b in range(d.shard_blocks):
            out_ref[:, b * BLOCK : (b + 1) * BLOCK] = acc[shard * d.shard_blocks + b].astype(out_ref.dtype)


def near_kernel(d, places, meta, xs, gs, act, gate_delta, up_delta, *part_refs):
    for j, part_ref in zip(places, part_refs):
        partial_grads(d, j, meta, xs, gs, act, gate_delta, up_delta, part_ref)


def call(kernel, outs, scratch, mib, cost, meta, *operands):
    vmem = pl.BlockSpec(memory_space=pltpu.VMEM)
    return pl.pallas_call(
        kernel,
        out_shape=outs,
        in_specs=[pl.BlockSpec(memory_space=pltpu.SMEM)] + [vmem] * len(operands),
        out_specs=[vmem] * len(outs),
        scratch_shapes=scratch,
        compiler_params=pltpu.CompilerParams(vmem_limit_bytes=mib * MIB),
        cost_estimate=pl.CostEstimate(flops=MIB, bytes_accessed=cost * MIB, transcendentals=0),
    )(meta, *operands)


def shards(inputs, out_grad, gate_blocks, up_blocks, down_blocks, gate_slots, up_slots, down_slots):
    n_dp, n_blk = lax.axis_size("dp"), lax.axis_size("blk")
    tokens, width = inputs.shape
    cap = gate_blocks.shape[2]
    d = Dims(n_dp, n_blk, cap, tokens, width)
    where = jnp.stack([lax.axis_index("blk"), lax.axis_index("dp")]).astype(jnp.int32)
    meta = jnp.concatenate([where] + [slots.reshape(-1) for slots in (gate_slots, up_slots, down_slots)])
    own_pair = jnp.stack([inputs, out_grad])

    matrices = [blocks[0, 0] for blocks in (gate_blocks, up_blocks, down_blocks)]
    groups = {0: [jnp.concatenate(matrices)]}
    groups[1] = [xor_swap(groups[0][0], "dp", 1)]
    x_pieces, g_pieces = ring_gather(inputs, out_grad, "blk", (own_pair, groups[0][0], groups[1][0], meta))
    bit = 2
    while bit < n_dp:
        for j in range(0, bit, 2):
            groups[j ^ bit] = [xor_swap(x, "dp", bit) for x in (groups[j] if j else matrices)]
        bit *= 2
    for j in range(2, n_dp, 2):
        groups[j + 1] = [xor_swap(after(x, *x_pieces[-2:-1]), "dp", 1) for x in groups[j]]

    def grid(count, kind):
        return jax.ShapeDtypeStruct((count, tokens, BLOCK), kind)

    def part(j):
        return jax.ShapeDtypeStruct((3 * cap, BLOCK, BLOCK), BF16 if j % 2 else F32)

    def blocks_at(places):
        return [x for j in places for x in groups[j]]

    sums = [grid(d.cols + 1, F32)] * 3
    xs, gs, gate_even, up_even, hidden_even = call(
        functools.partial(even_kernel, d), [grid(d.rows, BF16)] * 2 + sums, [], EVEN_MIB, EVEN_COST,
        meta, own_pair, *x_pieces[1:], *g_pieces[1:-1], *blocks_at(range(0, n_dp, 2)),
    )
    gate_slope, up_slope, act, hidden_odd = call(
        functools.partial(odd_kernel, d),
        [grid(d.cols, F32), grid(d.cols, F32), grid(d.cols, BF16), grid(d.cols + 1, F32)],
        [pltpu.VMEM((d.cols + 1, tokens, BLOCK), F32)] * 2, ODD_MIB, ODD_COST,
        meta, xs, gs, gate_even, up_even, *blocks_at(range(1, n_dp, 2)),
    )
    later = list(range(n_dp - 1, 1, -1))
    gate_delta, up_delta, gs, *parts_later = call(
        functools.partial(delta_kernel, d, later),
        [grid(d.cols, BF16), grid(d.cols, BF16), grid(d.rows, BF16)] + [part(j) for j in later],
        [pltpu.VMEM((d.cols + 1, tokens, BLOCK), F32)],
        DELTA_MIB, DELTA_COST, meta, xs, gs, act, gate_slope, up_slope, hidden_even, hidden_odd,
        g_pieces[-1], *blocks_at(range(n_dp)),
    )
    own, *far = call(
        functools.partial(input_kernel, d),
        [jax.ShapeDtypeStruct((tokens, width), F32)] + [jax.ShapeDtypeStruct((tokens, width), BF16)] * (n_blk - 1),
        [pltpu.VMEM((d.rows + 1, tokens, BLOCK), F32)],
        INPUT_MIB, INPUT_COST, meta, gate_delta, up_delta, *blocks_at(range(n_dp)),
    )
    near = [1, 0]
    parts_near = call(
        functools.partial(near_kernel, d, near),
        [part(j) for j in near], [], NEAR_MIB, NEAR_COST, meta, xs, gs, act, gate_delta, up_delta,
    )
    by_place = dict(zip(later + near, [*parts_later, *parts_near]))
    parts = [by_place[j] for j in range(n_dp)]

    bit = 1
    while bit < n_dp:
        arrived = [xor_swap(parts[j + 1].astype(BF16), "dp", bit) for j in range(0, len(parts), 2)]
        kept = parts[::2]
        bit *= 2
        if bit < n_dp:
            parts = [a + b.astype(F32) for a, b in zip(kept, arrived)]
    grads = [
        (kept[0][m * cap : (m + 1) * cap] + arrived[0][m * cap : (m + 1) * cap].astype(F32))
        .astype(BF16)
        .reshape(1, 1, cap, BLOCK, BLOCK)
        for m in range(3)
    ]
    for shift in range(1, n_blk):
        own = own + rotate(far[shift - 1], "blk", shift).astype(F32)
    return own.astype(BF16), *grads


def solution(mesh):
    in_specs = (
        P(("groups", "dp"), "blk"),
        P(("groups", "dp"), "blk"),
        P("blk", "dp", None, None, None),
        P("blk", "dp", None, None, None),
        P("blk", "dp", None, None, None),
        P("blk", None, None),
        P("blk", None, None),
        P("blk", None, None),
    )
    out_specs = (
        P(("groups", "dp"), "blk"),
        P(("groups", "blk"), "dp", None, None, None),
        P(("groups", "blk"), "dp", None, None, None),
        P(("groups", "blk"), "dp", None, None, None),
    )
    return jax.shard_map(shards, mesh=mesh, in_specs=in_specs, out_specs=out_specs, check_vma=False)
```

time: 112 us -> 83.8 us (0.75)
  starting transfers between devices: 42.7 us -> 19.3 us
  Pallas kernels: 15.4 us -> 12.4 us
    ppermute x15 -> x9, starting transfers between devices: 39 us -> 13 us  [rotate(): return lax.ppermute(x, axis, [(i, (i + shift) % n) for i in range(n)])]
    ppermute x6 -> x10, waiting for transfers between devices: 14.8 us -> 3.35 us  [xor_swap(): lax.ppermute(x, axis, [(i, i ^ bit) for i in range(lax.axis_size(axis))])]
    ppermute x15 -> x9, waiting for transfers between devices: 31.6 us -> 42.5 us  [rotate(): return lax.ppermute(x, axis, [(i, (i + shift) % n) for i in range(n)])]
    pallas_call x1 -> x5, Pallas kernels: 15.4 us -> 12.4 us  [call(): pl.pallas_call(kernel, out_shape=outs, in_specs=[pl.BlockSpec(memory_spac...]
    ppermute x6 -> x10, starting transfers between devices: 3.7 us -> 6.3 us  [xor_swap(): lax.ppermute(x, axis, [(i, i ^ bit) for i in range(lax.axis_size(axis))])]
    convert_element_type x1, other arithmetic: 2.02 us -> 0.33 us  [shards(): parts[j + 1].astype(BF16)]
  transfers between devices with their start and end apart: 21 -> 19, of which waited for: 10 -> 10; matrix products, arithmetic and copies ran while one was open for 3% -> 3% of each run, Pallas kernels for 0% -> 12%
where the time goes in v2:
time: 83.8 us; the launch traced here: 83.6 us
  waiting for transfers between devices  45.9 us (55%)
  starting transfers between devices  19.3 us (23%)
  Pallas kernels  12.4 us (15%)
  other arithmetic  4.98 us (6%)
    ppermute x9, waiting for transfers between devices, rotate(): return lax.ppermute(x, axis, [(i, (i + shift) % n) for i in range(n)])  42.5 us
    ppermute x9, starting transfers between devices, rotate(): return lax.ppermute(x, axis, [(i, (i + shift) % n) for i in range(n)])  13 us
    pallas_call x5, Pallas kernels, call(): pl.pallas_call(kernel, out_shape=outs, in_specs=[pl.BlockSpec(memory_spac...  12.4 us
    ppermute x10, starting transfers between devices, xor_swap(): lax.ppermute(x, axis, [(i, i ^ bit) for i in range(lax.axis_size(axis))])  6.3 us
    ppermute x10, waiting for transfers between devices, xor_swap(): lax.ppermute(x, axis, [(i, i ^ bit) for i in range(lax.axis_size(axis))])  3.35 us
  transfers between devices with their start and end apart: 19, of which 10 were waited for; matrix products, arithmetic and copies ran while one was open for 3% of the time, Pallas kernels for 12%

profile of v2, /device:TPU:8, one launch (start us, length us, event | category | flops | bytes accessed | tf_op | source)
XLA Modules:
  0.0 83.6 jit_solution(13284428243672113771)
XLA Ops:
  0.6 0.0 copy-start
  0.6 0.0 copy-start.1
  0.7 0.0 copy-start.2
  0.7 0.0 copy-start.3
  0.7 1.3 %pad_maximum_fusion.refs_5_.refs_0_ = bf16[30,128,128]{2,1,0:T(8,128)(2,1)S(1)} fusion(bf16[10,128,128]{2,1,0:T(8,128)(2,1)} %bitcast.6, bf16[10,128,128]{2,1,0:T(8,128)(2,1)} %bitcast.5, bf16[10,128,128]{2,1,0:T(8,128)(2,1)} %bitcast.4), kind=kLoop, calls=%fused_computation.2 | loop fusion | flops 983040 | bytes 1966080 | tf_op jit(solution)/shard_map/concatenate | solution.py:235
  2.0 0.1 collective-permute-start.4
  2.1 0.0 copy-done
  2.1 1.6 %collective-permute-start = (bf16[128,1024]{1,0:T(8,128)(2,1)S(1)}, bf16[128,1024]{1,0:T(8,128)(2,1)S(1)}, u32[]{:S(2)}, u32[]{:S(2)}) collective-permute-start(bf16[128,1024]{1,0:T(8,128)(2,1)S(1)} %copy-done), channel_id=1, source_target_pairs={{0,4},{4,8},{8,12},{12,0},{1,5},{5,9},{9,13},{13,1},{2,6},{6,10},{... | collective-permute-start | bytes 786440 | tf_op jit(solution)/shard_map/ppermute | solution.py:25
  3.7 1.6 %collective-permute-start.3 = (bf16[128,1024]{1,0:T(8,128)(2,1)}, bf16[128,1024]{1,0:T(8,128)(2,1)S(1)}, u32[]{:S(2)}, u32[]{:S(2)}) collective-permute-start(bf16[128,1024]{1,0:T(8,128)(2,1)} %param.9), channel_id=1, source_target_pairs={{0,4},{4,8},{8,12},{12,0},{1,5},{5,9},{9,13},{13,1},{2,6},{6,10},{... | collective-permute-start | bytes 786440 | tf_op jit(solution)/shard_map/ppermute | solution.py:25
  5.3 1.5 %collective-permute-start.6 = (bf16[10,128,128]{2,1,0:T(8,128)(2,1)}, bf16[10,128,128]{2,1,0:T(8,128)(2,1)S(1)}, u32[]{:S(2)}, u32[]{:S(2)}) collective-permute-start(bf16[10,128,128]{2,1,0:T(8,128)(2,1)} %bitcast.4), channel_id=1, source_target_pairs={{0,2},{1,3},{2,0},{3,1},{4,6},{5,7},{6,4},{7,5},{8,10},{9,11},{10,... | collective-permute-start | bytes 983048 | tf_op jit(solution)/shard_map/ppermute | solution.py:29
  6.8 0.5 collective-permute-start.7
  7.3 3.9 %collective-permute-done.refs_0_ = bf16[128,1024]{1,0:T(8,128)(2,1)S(1)} collective-permute-done((bf16[128,1024]{1,0:T(8,128)(2,1)S(1)}, bf16[128,1024]{1,0:T(8,128)(2,1)S(1)}, u32[]{:S(2)}, u32[]{:S(2)}) %collective-permute-start) | collective-permute-done | bytes 262176 | tf_op jit(solution)/shard_map/ppermute | solution.py:25
  11.2 1.5 %collective-permute-start.8 = (bf16[10,128,128]{2,1,0:T(8,128)(2,1)}, bf16[10,128,128]{2,1,0:T(8,128)(2,1)S(1)}, u32[]{:S(2)}, u32[]{:S(2)}) collective-permute-start(bf16[10,128,128]{2,1,0:T(8,128)(2,1)} %bitcast.6), channel_id=1, source_target_pairs={{0,2},{1,3},{2,0},{3,1},{4,6},{5,7},{6,4},{7,5},{8,10},{9,11},{10,... | collective-permute-start | bytes 983048 | tf_op jit(solution)/shard_map/ppermute | solution.py:29
  12.7 0.0 copy-done.1
  12.7 0.1 reshape.26
  12.8 0.0 copy-done.2
  12.8 0.1 reshape.27
  12.9 0.0 copy-done.3
  12.9 0.1 reshape.28
  13.0 0.1 concatenate.6.meta
  13.1 3.3 %collective-permute-done.3.refs_3_ = bf16[128,1024]{1,0:T(8,128)(2,1)S(1)} collective-permute-done((bf16[128,1024]{1,0:T(8,128)(2,1)}, bf16[128,1024]{1,0:T(8,128)(2,1)S(1)}, u32[]{:S(2)}, u32[]{:S(2)}) %collective-permute-start.3) | collective-permute-done | bytes 262176 | tf_op jit(solution)/shard_map/ppermute | solution.py:25
  16.4 1.6 %collective-permute-start.1 = (bf16[128,1024]{1,0:T(8,128)(2,1)S(1)}, bf16[128,1024]{1,0:T(8,128)(2,1)S(1)}, u32[]{:S(2)}, u32[]{:S(2)}) collective-permute-start(bf16[128,1024]{1,0:T(8,128)(2,1)S(1)} %collective-permute-done.refs_0_), channel_id=1, source_target_pairs={{0,4},{4,8},{8,12},{12,0},{1,5},{5,9},{9,13},{13,1},{2,6},{6,10},{... | collective-permute-start | bytes 786440 | tf_op jit(solution)/shard_map/ppermute | solution.py:25
  18.0 1.1 %pad_maximum_fusion.1.own_ref = bf16[2,128,1024]{2,1,0:T(8,128)(2,1)S(1)} fusion(bf16[1,128,1024]{2,1,0:T(8,128)(2,1)} %bitcast.3, bf16[1,128,1024]{2,1,0:T(8,128)(2,1)} %bitcast.13), kind=kLoop, calls=%fused_computation.9 | loop fusion | flops 262144 | bytes 1048576 | tf_op jit(solution)/shard_map/stack | solution.py:232
  19.1 0.0 collective-permute-done.4.refs_0_.refs_1_
  19.1 1.6 %collective-permute-start.5 = (bf16[128,1024]{1,0:T(8,128)(2,1)S(1)}, bf16[128,1024]{1,0:T(8,128)(2,1)S(1)}, u32[]{:S(2)}, u32[]{:S(2)}) collective-permute-start(bf16[128,1024]{1,0:T(8,128)(2,1)S(1)} %collective-permute-done.3.refs_3_), channel_id=1, source_target_pairs={{0,4},{4,8},{8,12},{12,0},{1,5},{5,9},{9,13},{13,1},{2,6},{6,10},{... | collective-permute-start | bytes 786440 | tf_op jit(solution)/shard_map/ppermute | solution.py:25
  20.7 0.0 collective-permute-done.6.refs_6_.refs_2_
  20.7 5.1 %collective-permute-done.1.refs_1_ = bf16[128,1024]{1,0:T(8,128)(2,1)S(1)} collective-permute-done((bf16[128,1024]{1,0:T(8,128)(2,1)S(1)}, bf16[128,1024]{1,0:T(8,128)(2,1)S(1)}, u32[]{:S(2)}, u32[]{:S(2)}) %collective-permute-start.1) | collective-permute-done | bytes 262176 | tf_op jit(solution)/shard_map/ppermute | solution.py:25
  25.8 0.0 collective-permute-start.9
  25.8 0.0 collective-permute-done.7.refs_7_.refs_3_
  25.8 0.5 collective-permute-start.10
  26.4 2.7 %collective-permute-done.8.refs_8_.refs_4_ = bf16[10,128,128]{2,1,0:T(8,128)(2,1)S(1)} collective-permute-done((bf16[10,128,128]{2,1,0:T(8,128)(2,1)}, bf16[10,128,128]{2,1,0:T(8,128)(2,1)S(1)}, u32[]{:S(2)}, u32[]{:S(2)}) %collective-permute-start.8) | collective-permute-done | bytes 327712 | tf_op jit(solution)/shard_map/ppermute | solution.py:29
  29.0 0.0 collective-permute-start.11
  29.0 0.3 collective-permute-start.2
  29.4 1.3 %collective-permute-done.5.refs_4_ = bf16[128,1024]{1,0:T(8,128)(2,1)S(1)} collective-permute-done((bf16[128,1024]{1,0:T(8,128)(2,1)S(1)}, bf16[128,1024]{1,0:T(8,128)(2,1)S(1)}, u32[]{:S(2)}, u32[]{:S(2)}) %collective-permute-start.5) | collective-permute-done | bytes 262176 | tf_op jit(solution)/shard_map/ppermute | solution.py:25
  30.7 0.8 collective-permute-start.12
  31.4 6.7 %collective-permute-done.2.refs_2_ = bf16[128,1024]{1,0:T(8,128)(2,1)S(1)} collective-permute-done((bf16[128,1024]{1,0:T(8,128)(2,1)S(1)}, bf16[128,1024]{1,0:T(8,128)(2,1)S(1)}, u32[]{:S(2)}, u32[]{:S(2)}) %collective-permute-start.2) | collective-permute-done | bytes 262176 | tf_op jit(solution)/shard_map/ppermute | solution.py:25
  38.1 2.3 %shard_map.111 = (bf16[32,128,128]{2,1,0:T(8,128)(2,1)S(1)}, bf16[32,128,128]{2,1,0:T(8,128)(2,1)S(1)}, f32[33,128,128]{2,1,0:T(8,128)S(1)}, f32[33,128,128]{2,1,0:T(8,128)S(1)}, f32[33,128,128]{2,1,0:T(8,128)S(1)}) custom-call(s32[122]{0:T(128)S(1)} %concatenate.6.meta, bf16[2,128,1024]{2,1,0:T(8,128)(2,1)S(1)} %pad_maximum_fusion.1.own_ref, ...), custom_call_target="tpu_custom_call" | custom-call | flops 1048576 | bytes 1048576 | tf_op jit(solution)/shard_map/pallas_call | solution.py:214
  40.4 0.0 collective-permute-done.9.refs_1_.refs_5_
  40.4 0.0 collective-permute-done.10.refs_2_.refs_6_
  40.4 0.0 collective-permute-done.11.refs_3_.refs_7_
  40.5 3.4 %shard_map.112 = (f32[32,128,128]{2,1,0:T(8,128)S(1)}, f32[32,128,128]{2,1,0:T(8,128)S(1)}, bf16[32,128,128]{2,1,0:T(8,128)(2,1)S(1)}, f32[33,128,128]{2,1,0:T(8,128)S(1)}) custom-call(s32[122]{0:T(128)S(1)} %concatenate.6.meta, bf16[32,128,128]{2,1,0:T(8,128)(2,1)S(1)} %get-tuple-element.29.xs, bf16[32,128,128]{2,1,0:T(8,128)(2,1)S(1)} %get-tuple-element.30.gs.gs_early, ...), custom_call_target="tpu_custom_call" | custom-call | flops 1048576 | bytes 1048576 | tf_op jit(solution)/shard_map/pallas_call | solution.py:214
  43.9 0.0 collective-permute-done.12.g_ref
  43.9 2.6 %shard_map.113 = (bf16[32,128,128]{2,1,0:T(8,128)(2,1)S(1)}, bf16[32,128,128]{2,1,0:T(8,128)(2,1)S(1)}, bf16[32,128,128]{2,1,0:T(8,128)(2,1)S(1)}, bf16[30,128,128]{2,1,0:T(8,128)(2,1)S(1)}, f32[30,128,128]{2,1,0:T(8,128)S(1)}) custom-call(s32[122]{0:T(128)S(1)} %concatenate.6.meta, bf16[32,128,128]{2,1,0:T(8,128)(2,1)S(1)} %get-tuple-element.29.xs, ...), custom_call_target="tpu_custom_call" | custom-call | flops 1048576 | bytes 12582912 | tf_op jit(solution)/shard_map/pallas_call | solution.py:214
  46.5 0.1 collective-permute-start.17
  46.6 1.3 %shard_map.115 = (bf16[30,128,128]{2,1,0:T(8,128)(2,1)S(1)}, f32[30,128,128]{2,1,0:T(8,128)S(1)}) custom-call(s32[122]{0:T(128)S(1)} %concatenate.6.meta, bf16[32,128,128]{2,1,0:T(8,128)(2,1)S(1)} %get-tuple-element.29.xs, bf16[32,128,128]{2,1,0:T(8,128)(2,1)S(1)} %get-tuple-element.47.gs, bf16[32,128,128]{2,1,0:T(8,128)(2,1)S(1)} %get-tuple-element.36.act, ...), custom_call_target="tpu_custom_call" | custom-call | flops 1048576 | bytes 6291456 | tf_op jit(solution)/shard_map/pallas_call | solution.py:214
  47.9 0.6 collective-permute-start.16
  48.5 0.6 collective-permute-done.17
  49.1 0.3 add_convert_fusion
  49.5 1.6 %collective-permute-start.18 = (bf16[30,128,128]{2,1,0:T(8,128)(2,1)S(1)}, bf16[30,128,128]{2,1,0:T(8,128)(2,1)S(1)}, u32[]{:S(2)}, u32[]{:S(2)}) collective-permute-start(bf16[30,128,128]{2,1,0:T(8,128)(2,1)S(1)} %add_convert_fusion), channel_id=1, source_target_pairs={{0,2},{1,3},{2,0},{3,1},{4,6},{5,7},{6,4},{7,5},{8,10},{9,11},{10,... | collective-permute-start | bytes 2949128 | tf_op jit(solution)/shard_map/ppermute | solution.py:29
  51.0 2.7 %shard_map.114 = (f32[128,1024]{1,0:T(8,128)S(1)}, bf16[128,1024]{1,0:T(8,128)(2,1)S(1)}, bf16[128,1024]{1,0:T(8,128)(2,1)S(1)}, bf16[128,1024]{1,0:T(8,128)(2,1)S(1)}) custom-call(s32[122]{0:T(128)S(1)} %concatenate.6.meta, bf16[32,128,128]{2,1,0:T(8,128)(2,1)S(1)} %get-tuple-element.41.gate_delta, bf16[32,128,128]{2,1,0:T(8,128)(2,1)S(1)} %get-tuple-element.42.up_delta, ...), custom_call_target="tpu_custom_call" | custom-call | flops 1048576 | bytes 12582912 | tf_op jit(solution)/shard_map/pallas_call | solution.py:214
  53.8 0.4 collective-permute-start.13
  54.1 5.1 %collective-permute-start.14 = (bf16[128,1024]{1,0:T(8,128)(2,1)S(1)}, bf16[128,1024]{1,0:T(8,128)(2,1)S(1)}, u32[]{:S(2)}, u32[]{:S(2)}) collective-permute-start(bf16[128,1024]{1,0:T(8,128)(2,1)S(1)} %get-tuple-element.45), channel_id=1, source_target_pairs={{0,8},{4,12},{8,0},{12,4},{1,9},{5,13},{9,1},{13,5},{2,10},{6,14},... | collective-permute-start | bytes 786440 | tf_op jit(solution)/shard_map/ppermute | solution.py:25
  59.2 0.0 collective-permute-start.15
  59.3 4.8 %collective-permute-done.13 = bf16[128,1024]{1,0:T(8,128)(2,1)S(1)} collective-permute-done((bf16[128,1024]{1,0:T(8,128)(2,1)S(1)}, bf16[128,1024]{1,0:T(8,128)(2,1)S(1)}, u32[]{:S(2)}, u32[]{:S(2)}) %collective-permute-start.13) | collective-permute-done | bytes 262176 | tf_op jit(solution)/shard_map/ppermute | solution.py:25
  64.0 12.6 %collective-permute-done.14 = bf16[128,1024]{1,0:T(8,128)(2,1)S(1)} collective-permute-done((bf16[128,1024]{1,0:T(8,128)(2,1)S(1)}, bf16[128,1024]{1,0:T(8,128)(2,1)S(1)}, u32[]{:S(2)}, u32[]{:S(2)}) %collective-permute-start.14) | collective-permute-done | bytes 262176 | tf_op jit(solution)/shard_map/ppermute | solution.py:25
  76.6 4.8 %collective-permute-done.15 = bf16[128,1024]{1,0:T(8,128)(2,1)S(1)} collective-permute-done((bf16[128,1024]{1,0:T(8,128)(2,1)S(1)}, bf16[128,1024]{1,0:T(8,128)(2,1)S(1)}, u32[]{:S(2)}, u32[]{:S(2)}) %collective-permute-start.15) | collective-permute-done | bytes 262176 | tf_op jit(solution)/shard_map/ppermute | solution.py:25
  81.4 0.9 %add_convert_fusion.1 = bf16[128,1024]{1,0:T(8,128)(2,1)} fusion(bf16[128,1024]{1,0:T(8,128)(2,1)S(1)} %collective-permute-done.15, bf16[128,1024]{1,0:T(8,128)(2,1)S(1)} %collective-permute-done.14, f32[128,1024]{1,0:T(8,128)S(1)} %get-tuple-element.43, bf16[128,1024]{1,0:T(8,128)(2,1)S(1)} %collective-permute-done.13), kind=kLoop, calls=%fused_computation.10 | loop fusion | flops 917504 | bytes 1572864 | tf_op jit(solution)/shard_map/convert_element_type | solution.py:303
  82.2 0.0 collective-permute-done.16
  82.2 0.3 convert_add_fusion
  82.5 0.0 collective-permute-done.18
  82.5 1.1 %fusion.5 = (bf16[1,1,10,128,128]{4,3,2,1,0:T(8,128)(2,1)}, bf16[1,1,10,128,128]{4,3,2,1,0:T(8,128)(2,1)}, bf16[1,1,10,128,128]{4,3,2,1,0:T(8,128)(2,1)}) fusion(f32[30,128,128]{2,1,0:T(8,128)S(1)} %convert_add_fusion, bf16[30,128,128]{2,1,0:T(8,128)(2,1)S(1)} %collective-permute-done.18), kind=kLoop, calls=%fused_computation.13 | loop fusion | flops 1474560 | bytes 3932160 | tf_op jit(solution)/shard_map/reshape | solution.py:298
Async XLA Ops:
  0.6 1.4 %copy-start = (bf16[128,1024]{1,0:T(8,128)(2,1)S(1)}, bf16[128,1024]{1,0:T(8,128)(2,1)}, u32[]{:S(2)}) copy-start(bf16[128,1024]{1,0:T(8,128)(2,1)} %param.8) | copy-start | bytes 786436
  0.6 12.1 %copy-start.1 = (s32[1,4,10]{2,1,0:T(4,128)S(1)}, s32[1,4,10]{2,1,0:T(4,128)}, u32[]{:S(2)}) copy-start(s32[1,4,10]{2,1,0:T(4,128)} %param.13) | copy-start | bytes 484
  0.7 12.2 %copy-start.2 = (s32[1,4,10]{2,1,0:T(4,128)S(1)}, s32[1,4,10]{2,1,0:T(4,128)}, u32[]{:S(2)}) copy-start(s32[1,4,10]{2,1,0:T(4,128)} %param.14) | copy-start | bytes 484
  0.7 12.2 %copy-start.3 = (s32[1,4,10]{2,1,0:T(4,128)S(1)}, s32[1,4,10]{2,1,0:T(4,128)}, u32[]{:S(2)}) copy-start(s32[1,4,10]{2,1,0:T(4,128)} %param.15) | copy-start | bytes 484
  2.0 17.1 %collective-permute-start.4 = (bf16[30,128,128]{2,1,0:T(8,128)(2,1)S(1)}, bf16[30,128,128]{2,1,0:T(8,128)(2,1)S(1)}, u32[]{:S(2)}, u32[]{:S(2)}) collective-permute-start(bf16[30,128,128]{2,1,0:T(8,128)(2,1)S(1)} %pad_maximum_fusion.refs_5_.refs_0_), channel_id=1, source_target_pairs={{0,1},{1,0},{2,3},{3,2},{4,5},{5,4},{6,7},{7,6},{8,9},{9,8},{10,11... | collective-permute-start | bytes 2949128 | tf_op jit(solution)/shard_map/ppermute | solution.py:29
  2.1 9.2 %collective-permute-start = (bf16[128,1024]{1,0:T(8,128)(2,1)S(1)}, bf16[128,1024]{1,0:T(8,128)(2,1)S(1)}, u32[]{:S(2)}, u32[]{:S(2)}) collective-permute-start(bf16[128,1024]{1,0:T(8,128)(2,1)S(1)} %copy-done), channel_id=1, source_target_pairs={{0,4},{4,8},{8,12},{12,0},{1,5},{5,9},{9,13},{13,1},{2,6},{6,10},{... | collective-permute-start | bytes 786440 | tf_op jit(solution)/shard_map/ppermute | solution.py:25
  3.7 12.7 %collective-permute-start.3 = (bf16[128,1024]{1,0:T(8,128)(2,1)}, bf16[128,1024]{1,0:T(8,128)(2,1)S(1)}, u32[]{:S(2)}, u32[]{:S(2)}) collective-permute-start(bf16[128,1024]{1,0:T(8,128)(2,1)} %param.9), channel_id=1, source_target_pairs={{0,4},{4,8},{8,12},{12,0},{1,5},{5,9},{9,13},{13,1},{2,6},{6,10},{... | collective-permute-start | bytes 786440 | tf_op jit(solution)/shard_map/ppermute | solution.py:25
  5.3 15.4 %collective-permute-start.6 = (bf16[10,128,128]{2,1,0:T(8,128)(2,1)}, bf16[10,128,128]{2,1,0:T(8,128)(2,1)S(1)}, u32[]{:S(2)}, u32[]{:S(2)}) collective-permute-start(bf16[10,128,128]{2,1,0:T(8,128)(2,1)} %bitcast.4), channel_id=1, source_target_pairs={{0,2},{1,3},{2,0},{3,1},{4,6},{5,7},{6,4},{7,5},{8,10},{9,11},{10,... | collective-permute-start | bytes 983048 | tf_op jit(solution)/shard_map/ppermute | solution.py:29
  6.8 19.1 %collective-permute-start.7 = (bf16[10,128,128]{2,1,0:T(8,128)(2,1)}, bf16[10,128,128]{2,1,0:T(8,128)(2,1)S(1)}, u32[]{:S(2)}, u32[]{:S(2)}) collective-permute-start(bf16[10,128,128]{2,1,0:T(8,128)(2,1)} %bitcast.5), channel_id=1, source_target_pairs={{0,2},{1,3},{2,0},{3,1},{4,6},{5,7},{6,4},{7,5},{8,10},{9,11},{10,... | collective-permute-start | bytes 983048 | tf_op jit(solution)/shard_map/ppermute | solution.py:29
  11.2 17.8 %collective-permute-start.8 = (bf16[10,128,128]{2,1,0:T(8,128)(2,1)}, bf16[10,128,128]{2,1,0:T(8,128)(2,1)S(1)}, u32[]{:S(2)}, u32[]{:S(2)}) collective-permute-start(bf16[10,128,128]{2,1,0:T(8,128)(2,1)} %bitcast.6), channel_id=1, source_target_pairs={{0,2},{1,3},{2,0},{3,1},{4,6},{5,7},{6,4},{7,5},{8,10},{9,11},{10,... | collective-permute-start | bytes 983048 | tf_op jit(solution)/shard_map/ppermute | solution.py:29
  16.4 9.4 %collective-permute-start.1 = (bf16[128,1024]{1,0:T(8,128)(2,1)S(1)}, bf16[128,1024]{1,0:T(8,128)(2,1)S(1)}, u32[]{:S(2)}, u32[]{:S(2)}) collective-permute-start(bf16[128,1024]{1,0:T(8,128)(2,1)S(1)} %collective-permute-done.refs_0_), channel_id=1, source_target_pairs={{0,4},{4,8},{8,12},{12,0},{1,5},{5,9},{9,13},{13,1},{2,6},{6,10},{... | collective-permute-start | bytes 786440 | tf_op jit(solution)/shard_map/ppermute | solution.py:25
  19.1 11.6 %collective-permute-start.5 = (bf16[128,1024]{1,0:T(8,128)(2,1)S(1)}, bf16[128,1024]{1,0:T(8,128)(2,1)S(1)}, u32[]{:S(2)}, u32[]{:S(2)}) collective-permute-start(bf16[128,1024]{1,0:T(8,128)(2,1)S(1)} %collective-permute-done.3.refs_3_), channel_id=1, source_target_pairs={{0,4},{4,8},{8,12},{12,0},{1,5},{5,9},{9,13},{13,1},{2,6},{6,10},{... | collective-permute-start | bytes 786440 | tf_op jit(solution)/shard_map/ppermute | solution.py:25
  25.8 14.6 %collective-permute-start.9 = (bf16[10,128,128]{2,1,0:T(8,128)(2,1)S(1)}, bf16[10,128,128]{2,1,0:T(8,128)(2,1)S(1)}, u32[]{:S(2)}, u32[]{:S(2)}) collective-permute-start(bf16[10,128,128]{2,1,0:T(8,128)(2,1)S(1)} %collective-permute-done.6.refs_6_.refs_2_), channel_id=1, source_target_pairs={{0,1},{1,0},{2,3},{3,2},{4,5},{5,4},{6,7},{7,6},{8,9},{9,8},{10,11... | collective-permute-start | bytes 983048 | tf_op jit(solution)/shard_map/ppermute | solution.py:29
  25.8 14.6 %collective-permute-start.10 = (bf16[10,128,128]{2,1,0:T(8,128)(2,1)S(1)}, bf16[10,128,128]{2,1,0:T(8,128)(2,1)S(1)}, u32[]{:S(2)}, u32[]{:S(2)}) collective-permute-start(bf16[10,128,128]{2,1,0:T(8,128)(2,1)S(1)} %collective-permute-done.7.refs_7_.refs_3_), channel_id=1, source_target_pairs={{0,1},{1,0},{2,3},{3,2},{4,5},{5,4},{6,7},{7,6},{8,9},{9,8},{10,11... | collective-permute-start | bytes 983048 | tf_op jit(solution)/shard_map/ppermute | solution.py:29
  29.0 11.4 %collective-permute-start.11 = (bf16[10,128,128]{2,1,0:T(8,128)(2,1)S(1)}, bf16[10,128,128]{2,1,0:T(8,128)(2,1)S(1)}, u32[]{:S(2)}, u32[]{:S(2)}) collective-permute-start(bf16[10,128,128]{2,1,0:T(8,128)(2,1)S(1)} %collective-permute-done.8.refs_8_.refs_4_), channel_id=1, source_target_pairs={{0,1},{1,0},{2,3},{3,2},{4,5},{5,4},{6,7},{7,6},{8,9},{9,8},{10,11... | collective-permute-start | bytes 983048 | tf_op jit(solution)/shard_map/ppermute | solution.py:29
  29.0 9.1 %collective-permute-start.2 = (bf16[128,1024]{1,0:T(8,128)(2,1)S(1)}, bf16[128,1024]{1,0:T(8,128)(2,1)S(1)}, u32[]{:S(2)}, u32[]{:S(2)}) collective-permute-start(bf16[128,1024]{1,0:T(8,128)(2,1)S(1)} %collective-permute-done.1.refs_1_), channel_id=1, source_target_pairs={{0,4},{4,8},{8,12},{12,0},{1,5},{5,9},{9,13},{13,1},{2,6},{6,10},{... | collective-permute-start | bytes 786440 | tf_op jit(solution)/shard_map/ppermute | solution.py:25
  30.7 13.2 %collective-permute-start.12 = (bf16[128,1024]{1,0:T(8,128)(2,1)S(1)}, bf16[128,1024]{1,0:T(8,128)(2,1)S(1)}, u32[]{:S(2)}, u32[]{:S(2)}) collective-permute-start(bf16[128,1024]{1,0:T(8,128)(2,1)S(1)} %collective-permute-done.5.refs_4_), channel_id=1, source_target_pairs={{0,4},{4,8},{8,12},{12,0},{1,5},{5,9},{9,13},{13,1},{2,6},{6,10},{... | collective-permute-start | bytes 786440 | tf_op jit(solution)/shard_map/ppermute | solution.py:25
  46.5 2.6 %collective-permute-start.17 = (bf16[30,128,128]{2,1,0:T(8,128)(2,1)S(1)}, bf16[30,128,128]{2,1,0:T(8,128)(2,1)S(1)}, u32[]{:S(2)}, u32[]{:S(2)}) collective-permute-start(bf16[30,128,128]{2,1,0:T(8,128)(2,1)S(1)} %get-tuple-element.51), channel_id=1, source_target_pairs={{0,1},{1,0},{2,3},{3,2},{4,5},{5,4},{6,7},{7,6},{8,9},{9,8},{10,11... | collective-permute-start | bytes 2949128 | tf_op jit(solution)/shard_map/ppermute | solution.py:29
  47.9 34.3 %collective-permute-start.16 = (bf16[30,128,128]{2,1,0:T(8,128)(2,1)S(1)}, bf16[30,128,128]{2,1,0:T(8,128)(2,1)S(1)}, u32[]{:S(2)}, u32[]{:S(2)}) collective-permute-start(bf16[30,128,128]{2,1,0:T(8,128)(2,1)S(1)} %get-tuple-element.49), channel_id=1, source_target_pairs={{0,1},{1,0},{2,3},{3,2},{4,5},{5,4},{6,7},{7,6},{8,9},{9,8},{10,11... | collective-permute-start | bytes 2949128 | tf_op jit(solution)/shard_map/ppermute | solution.py:29
  49.5 33.1 %collective-permute-start.18 = (bf16[30,128,128]{2,1,0:T(8,128)(2,1)S(1)}, bf16[30,128,128]{2,1,0:T(8,128)(2,1)S(1)}, u32[]{:S(2)}, u32[]{:S(2)}) collective-permute-start(bf16[30,128,128]{2,1,0:T(8,128)(2,1)S(1)} %add_convert_fusion), channel_id=1, source_target_pairs={{0,2},{1,3},{2,0},{3,1},{4,6},{5,7},{6,4},{7,5},{8,10},{9,11},{10,... | collective-permute-start | bytes 2949128 | tf_op jit(solution)/shard_map/ppermute | solution.py:29
  53.8 10.3 %collective-permute-start.13 = (bf16[128,1024]{1,0:T(8,128)(2,1)S(1)}, bf16[128,1024]{1,0:T(8,128)(2,1)S(1)}, u32[]{:S(2)}, u32[]{:S(2)}) collective-permute-start(bf16[128,1024]{1,0:T(8,128)(2,1)S(1)} %get-tuple-element.44), channel_id=1, source_target_pairs={{0,4},{4,8},{8,12},{12,0},{1,5},{5,9},{9,13},{13,1},{2,6},{6,10},{... | collective-permute-start | bytes 786440 | tf_op jit(solution)/shard_map/ppermute | solution.py:25
  54.1 22.4 %collective-permute-start.14 = (bf16[128,1024]{1,0:T(8,128)(2,1)S(1)}, bf16[128,1024]{1,0:T(8,128)(2,1)S(1)}, u32[]{:S(2)}, u32[]{:S(2)}) collective-permute-start(bf16[128,1024]{1,0:T(8,128)(2,1)S(1)} %get-tuple-element.45), channel_id=1, source_target_pairs={{0,8},{4,12},{8,0},{12,4},{1,9},{5,13},{9,1},{13,5},{2,10},{6,14},... | collective-permute-start | bytes 786440 | tf_op jit(solution)/shard_map/ppermute | solution.py:25
  59.2 22.1 %collective-permute-start.15 = (bf16[128,1024]{1,0:T(8,128)(2,1)S(1)}, bf16[128,1024]{1,0:T(8,128)(2,1)S(1)}, u32[]{:S(2)}, u32[]{:S(2)}) collective-permute-start(bf16[128,1024]{1,0:T(8,128)(2,1)S(1)} %get-tuple-element.46), channel_id=1, source_target_pairs={{0,12},{4,0},{8,4},{12,8},{1,13},{5,1},{9,5},{13,9},{2,14},{6,2},{... | collective-permute-start | bytes 786440 | tf_op jit(solution)/shard_map/ppermute | solution.py:25

commit v3 on v2

--- a/solution.py
+++ b/solution.py
@@ -16,8 +16,9 @@
 TN = (((0,), (0,)), ((), ()))
 MIB = 1024 * 1024
 LONGEST_RING = 8
-EVEN_MIB, ODD_MIB, DELTA_MIB, INPUT_MIB, NEAR_MIB = 20, 24, 28, 16, 14
-EVEN_COST, ODD_COST, DELTA_COST, INPUT_COST, NEAR_COST = 1, 1, 12, 12, 6
+PIECES = 2
+EARLY_MIB, LATE_MIB, DELTA_MIB, INPUT_MIB, NEAR_MIB = 18, 22, 28, 16, 14
+EARLY_COST, LATE_COST, DELTA_COST, INPUT_COST, NEAR_COST = 8, 8, 8, 8, 8
 
 
 def rotate(x, axis, shift):
@@ -29,20 +30,18 @@
     return lax.ppermute(x, axis, [(i, i ^ bit) for i in range(lax.axis_size(axis))])
 
 
-def ring_gather(x, g, axis, ready):
+def ring_gather(x, g, axis, hold):
     n = lax.axis_size(axis)
     if n > LONGEST_RING:
         me = lax.axis_index(axis)
         return [
-            [piece] + [
-                lax.dynamic_index_in_dim(whole, (me - i + n) % n, 0, keepdims=False) for i in range(1, n)
-            ]
-            for piece, whole in ((x, lax.all_gather(x, axis)), (g, lax.all_gather(g, axis)))
+            [own] + [lax.dynamic_index_in_dim(whole, (me - i + n) % n, 0, keepdims=False) for i in range(1, n)]
+            for own, whole in ((x, lax.all_gather(x, axis)), (g, lax.all_gather(g, axis)))
         ]
     xs, gs = [x], [g]
-    for step in range(1, n):
+    for hop in range(1, n):
         xs.append(rotate(xs[-1], axis, 1))
-        gs.append(rotate(after(gs[-1], *ready) if step == 2 else gs[-1], axis, 1))
+        gs.append(rotate(after(gs[-1], *hold) if hop == 2 else gs[-1], axis, 1))
     return xs, gs
 
 
@@ -85,20 +84,10 @@
         )
 
 
-def forward_products(d, meta, group, j, xs, gs, gate_acc, up_acc, hidden):
-    me_blk, me_dp = d.here(meta)
-    owner = me_dp ^ j
-    add_products(d, meta, 0, owner, group, xs, NN, gate_acc)
-    add_products(d, meta, 1, owner, group, xs, NN, up_acc)
-    if d.paired:
-        there = owner != shard_at(d, me_blk, d.n_blk - 1)
-        pl.when(there)(functools.partial(add_products, d, meta, 2, owner, group, gs, NT, hidden))
-
-
 def take_groups(refs, places):
     groups, at = {}, 0
     for j in places:
-        size = 1 if j < 2 else 3
+        size = 3 if j else 1
         groups[j] = refs[at : at + size]
         at += size
     return groups, refs[at:]
@@ -108,32 +97,58 @@
     return lax.rem(me - i + d.n_blk, d.n_blk)
 
 
-def even_kernel(d, meta, own_ref, *refs):
-    x_refs, g_refs = refs[: d.n_blk - 1], refs[d.n_blk - 1 : 2 * d.n_blk - 3]
-    groups, outs = take_groups(refs[2 * d.n_blk - 3 :], range(0, d.n_dp, 2))
-    xs, gs, gate_acc, up_acc, hidden = outs
-    me_blk, _ = d.here(meta)
-    own_x, own_g = own_ref.at[0], own_ref.at[1]
-    for i, x_ref in enumerate((own_x, *x_refs)):
-        d.spread(x_ref, shard_at(d, me_blk, i), xs)
-    for i, g_ref in enumerate((own_g, *g_refs)):
-        d.spread(g_ref, shard_at(d, me_blk, i), gs)
+def spread_all(d, me, refs, target):
+    for i, ref in enumerate(refs):
+        d.spread(ref, shard_at(d, me, i), target)
+
+
+def early_kernel(d, meta, own_ref, *refs):
+    x_refs, g_refs = refs[: d.n_blk - 2], refs[d.n_blk - 2 : 2 * d.n_blk - 4]
+    groups, outs = take_groups(refs[2 * d.n_blk - 4 :], range(d.n_dp))
+    gate_acc, up_acc, hidden, xs, gs = outs
+    me_blk, me_dp = d.here(meta)
     for acc in (gate_acc, up_acc, hidden):
         acc[...] = jnp.zeros_like(acc)
+    if not d.paired:
+        return
+    spread_all(d, me_blk, (own_ref.at[0], *x_refs), xs)
+    spread_all(d, me_blk, (own_ref.at[1], *g_refs), gs)
     for j, group in groups.items():
-        forward_products(d, meta, group, j, xs, gs, gate_acc, up_acc, hidden)
-
-
-def odd_kernel(d, meta, xs, gs, gate_even, up_even, *refs):
-    groups, outs = take_groups(refs, range(1, d.n_dp, 2))
-    gate_slope, up_slope, act, hidden, gate_acc, up_acc = outs
-    for acc in (gate_acc, up_acc, hidden):
+        owner = me_dp ^ j
+
+        @pl.when(owner != shard_at(d, me_blk, d.n_blk - 1))
+        def _():
+            add_products(d, meta, 0, owner, group, xs, NN, gate_acc)
+            add_products(d, meta, 1, owner, group, xs, NN, up_acc)
+            add_products(d, meta, 2, owner, group, gs, NT, hidden)
+
+
+def when_late(d, meta, owner, work):
+    if d.paired:
+        pl.when(owner == shard_at(d, meta[0], d.n_blk - 1))(work)
+    else:
+        work()
+
+
+def late_kernel(d, meta, own_ref, *refs):
+    x_refs, (gate_early, up_early) = refs[: d.n_blk - 1], refs[d.n_blk - 1 : d.n_blk + 1]
+    groups, outs = take_groups(refs[d.n_blk + 1 :], range(d.n_dp))
+    gate_slope, up_slope, act, xs, gate_acc, up_acc = outs
+    me_blk, me_dp = d.here(meta)
+    for acc in (gate_acc, up_acc):
         acc[...] = jnp.zeros_like(acc)
+    spread_all(d, me_blk, (own_ref.at[0], *x_refs), xs)
     for j, group in groups.items():
-        forward_products(d, meta, group, j, xs, gs, gate_acc, up_acc, hidden)
+        owner = me_dp ^ j
+
+        def work():
+            add_products(d, meta, 0, owner, group, xs, NN, gate_acc)
+            add_products(d, meta, 1, owner, group, xs, NN, up_acc)
+
+        when_late(d, meta, owner, work)
 
     def activation(c, _):
-        gate, up = gate_even[c] + gate_acc[c], up_even[c] + up_acc[c]
+        gate, up = gate_early[c] + gate_acc[c], up_early[c] + up_acc[c]
         sig = jax.nn.sigmoid(gate)
         activated = gate * sig
         act[c] = (activated * up).astype(BF16)
@@ -141,7 +156,7 @@
         up_slope[c] = activated
         return 0
 
-    lax.fori_loop(0, d.cols, activation, 0)
+    lax.fori_loop(0, d.cols, activation, 0, unroll=4)
 
 
 def partial_grads(d, j, meta, xs, gs, act, gate_delta, up_delta, out_ref):
@@ -157,30 +172,25 @@
             out_ref[matrix * d.cap + s] = jnp.where(used, product, 0.0).astype(out_ref.dtype)
 
 
-def delta_kernel(d, places, meta, xs, gs_early, act, gate_slope, up_slope, hidden_even, hidden_odd, g_ref, *refs):
-    groups, outs = take_groups(refs, range(d.n_dp))
+def delta_kernel(d, places, meta, own_ref, xs, act, gate_slope, up_slope, hidden, *refs):
+    g_refs = refs[: d.n_blk - 1]
+    groups, outs = take_groups(refs[d.n_blk - 1 :], range(d.n_dp))
     gate_delta, up_delta, gs = outs[:3]
     part_refs, more = outs[3:-1], outs[-1]
     me_blk, me_dp = d.here(meta)
-    last = shard_at(d, me_blk, d.n_blk - 1)
-    gs[...] = gs_early[...]
-    d.spread(g_ref, last, gs)
     more[...] = jnp.zeros_like(more)
-    for j in range(d.n_dp):
+    spread_all(d, me_blk, (own_ref.at[1], *g_refs), gs)
+    for j, group in groups.items():
         owner = me_dp ^ j
-        late = functools.partial(add_products, d, meta, 2, owner, groups[j], gs, NT, more)
-        if d.paired:
-            pl.when(owner == last)(late)
-        else:
-            late()
+        when_late(d, meta, owner, functools.partial(add_products, d, meta, 2, owner, group, gs, NT, more))
 
     def deltas(c, _):
-        total = (hidden_even[c] + hidden_odd[c]) + more[c]
+        total = hidden[c] + more[c]
         gate_delta[c] = (total * gate_slope[c]).astype(BF16)
         up_delta[c] = (total * up_slope[c]).astype(BF16)
         return 0
 
-    lax.fori_loop(0, d.cols, deltas, 0)
+    lax.fori_loop(0, d.cols, deltas, 0, unroll=4)
     for j, part_ref in zip(places, part_refs):
         partial_grads(d, j, meta, xs, gs, act, gate_delta, up_delta, part_ref)
 
@@ -204,8 +214,16 @@
             out_ref[:, b * BLOCK : (b + 1) * BLOCK] = acc[shard * d.shard_blocks + b].astype(out_ref.dtype)
 
 
-def near_kernel(d, places, meta, xs, gs, act, gate_delta, up_delta, *part_refs):
-    for j, part_ref in zip(places, part_refs):
+class Pieces:
+    def __init__(self, refs):
+        self.refs, self.size, self.dtype = refs, refs[0].shape[0], refs[0].dtype
+
+    def __setitem__(self, at, value):
+        self.refs[at // self.size][at % self.size] = value
+
+
+def near_kernel(d, meta, xs, gs, act, gate_delta, up_delta, own_ref, *next_refs):
+    for j, part_ref in ((1, Pieces(next_refs)), (0, own_ref)):
         partial_grads(d, j, meta, xs, gs, act, gate_delta, up_delta, part_ref)
 
 
@@ -232,16 +250,20 @@
     own_pair = jnp.stack([inputs, out_grad])
 
     matrices = [blocks[0, 0] for blocks in (gate_blocks, up_blocks, down_blocks)]
-    groups = {0: [jnp.concatenate(matrices)]}
-    groups[1] = [xor_swap(groups[0][0], "dp", 1)]
-    x_pieces, g_pieces = ring_gather(inputs, out_grad, "blk", (own_pair, groups[0][0], groups[1][0], meta))
+    groups = {0: [jnp.concatenate(matrices)], 1: [xor_swap(x, "dp", 1) for x in matrices]}
+    own = (own_pair, groups[0][0], meta)
     bit = 2
     while bit < n_dp:
         for j in range(0, bit, 2):
-            groups[j ^ bit] = [xor_swap(x, "dp", bit) for x in (groups[j] if j else matrices)]
+            gate, up, down = groups[j] if j else matrices
+            gate = xor_swap(after(gate, *groups[1]), "dp", bit)
+            up = xor_swap(after(up, *own), "dp", bit)
+            down = xor_swap(after(down, gate), "dp", bit)
+            groups[j ^ bit] = [gate, up, down]
         bit *= 2
+    x_pieces, g_pieces = ring_gather(inputs, out_grad, "blk", (*own, *groups[1]))
     for j in range(2, n_dp, 2):
-        groups[j + 1] = [xor_swap(after(x, *x_pieces[-2:-1]), "dp", 1) for x in groups[j]]
+        groups[j + 1] = [xor_swap(after(x, x_pieces[-2]), "dp", 1) for x in groups[j]]
 
     def grid(count, kind):
         return jax.ShapeDtypeStruct((count, tokens, BLOCK), kind)
@@ -252,40 +274,46 @@
     def blocks_at(places):
         return [x for j in places for x in groups[j]]
 
+    everyone = blocks_at(range(n_dp))
     sums = [grid(d.cols + 1, F32)] * 3
-    xs, gs, gate_even, up_even, hidden_even = call(
-        functools.partial(even_kernel, d), [grid(d.rows, BF16)] * 2 + sums, [], EVEN_MIB, EVEN_COST,
-        meta, own_pair, *x_pieces[1:], *g_pieces[1:-1], *blocks_at(range(0, n_dp, 2)),
-    )
-    gate_slope, up_slope, act, hidden_odd = call(
-        functools.partial(odd_kernel, d),
-        [grid(d.cols, F32), grid(d.cols, F32), grid(d.cols, BF16), grid(d.cols + 1, F32)],
-        [pltpu.VMEM((d.cols + 1, tokens, BLOCK), F32)] * 2, ODD_MIB, ODD_COST,
-        meta, xs, gs, gate_even, up_even, *blocks_at(range(1, n_dp, 2)),
+    gate_early, up_early, hidden = call(
+        functools.partial(early_kernel, d), sums, [pltpu.VMEM((d.rows, tokens, BLOCK), BF16)] * 2, EARLY_MIB, EARLY_COST,
+        meta, own_pair, *x_pieces[1:-1], *g_pieces[1:-1], *everyone,
+    )
+    gate_slope, up_slope, act, xs = call(
+        functools.partial(late_kernel, d),
+        [grid(d.cols, F32), grid(d.cols, F32), grid(d.cols, BF16), grid(d.rows, BF16)],
+        [pltpu.VMEM((d.cols + 1, tokens, BLOCK), F32)] * 2, LATE_MIB, LATE_COST,
+        meta, own_pair, *x_pieces[1:], gate_early, up_early, *everyone,
     )
     later = list(range(n_dp - 1, 1, -1))
     gate_delta, up_delta, gs, *parts_later = call(
         functools.partial(delta_kernel, d, later),
         [grid(d.cols, BF16), grid(d.cols, BF16), grid(d.rows, BF16)] + [part(j) for j in later],
         [pltpu.VMEM((d.cols + 1, tokens, BLOCK), F32)],
-        DELTA_MIB, DELTA_COST, meta, xs, gs, act, gate_slope, up_slope, hidden_even, hidden_odd,
-        g_pieces[-1], *blocks_at(range(n_dp)),
+        DELTA_MIB, DELTA_COST, meta, own_pair, xs, act, gate_slope, up_slope, hidden, *g_pieces[1:], *everyone,
     )
     own, *far = call(
         functools.partial(input_kernel, d),
         [jax.ShapeDtypeStruct((tokens, width), F32)] + [jax.ShapeDtypeStruct((tokens, width), BF16)] * (n_blk - 1),
         [pltpu.VMEM((d.rows + 1, tokens, BLOCK), F32)],
-        INPUT_MIB, INPUT_COST, meta, gate_delta, up_delta, *blocks_at(range(n_dp)),
-    )
-    near = [1, 0]
-    parts_near = call(
-        functools.partial(near_kernel, d, near),
-        [part(j) for j in near], [], NEAR_MIB, NEAR_COST, meta, xs, gs, act, gate_delta, up_delta,
-    )
-    by_place = dict(zip(later + near, [*parts_later, *parts_near]))
-    parts = [by_place[j] for j in range(n_dp)]
-
-    bit = 1
+        INPUT_MIB, INPUT_COST, meta, gate_delta, up_delta, *everyone,
+    )
+    far_parts = dict(zip(later, parts_later))
+
+    relayed = []
+    for j in range(2, n_dp, 2):
+        other = xor_swap(far_parts[j + 1], "dp", 1)
+        relayed.append(far_parts[j] + after(other, *far).astype(F32))
+    moved = [rotate(far[shift - 1], "blk", shift) for shift in range(1, n_blk)]
+    part_own, *parts_next = call(
+        functools.partial(near_kernel, d),
+        [part(0)] + [jax.ShapeDtypeStruct((3 * cap // PIECES, BLOCK, BLOCK), BF16)] * PIECES,
+        [], NEAR_MIB, NEAR_COST, meta, xs, gs, act, after(gate_delta, *relayed), up_delta,
+    )
+    part_own = part_own + jnp.concatenate([xor_swap(piece, "dp", 1) for piece in parts_next]).astype(F32)
+    parts = [part_own, *relayed]
+    bit = 2
     while bit < n_dp:
         arrived = [xor_swap(parts[j + 1].astype(BF16), "dp", bit) for j in range(0, len(parts), 2)]
         kept = parts[::2]
@@ -298,8 +326,8 @@
         .reshape(1, 1, cap, BLOCK, BLOCK)
         for m in range(3)
     ]
-    for shift in range(1, n_blk):
-        own = own + rotate(far[shift - 1], "blk", shift).astype(F32)
+    for piece in moved:
+        own = own + piece.astype(F32)
     return own.astype(BF16), *grads
 
 

time: 83.8 us -> 78.5 us (0.937)
  waiting for transfers between devices: 45.9 us -> 39.4 us
  starting transfers between devices: 19.3 us -> 20.9 us
    ppermute x9, waiting for transfers between devices: 42.5 us -> 33.2 us  [rotate(): return lax.ppermute(x, axis, [(i, (i + shift) % n) for i in range(n)])]
    ppermute x10 -> x13, waiting for transfers between devices: 3.35 us -> 6.13 us  [xor_swap(): lax.ppermute(x, axis, [(i, i ^ bit) for i in range(lax.axis_size(axis))])]
    ppermute x9, starting transfers between devices: 13 us -> 14.2 us  [rotate(): return lax.ppermute(x, axis, [(i, (i + shift) % n) for i in range(n)])]
    ppermute x10 -> x13, starting transfers between devices: 6.3 us -> 6.67 us  [xor_swap(): lax.ppermute(x, axis, [(i, i ^ bit) for i in range(lax.axis_size(axis))])]
  transfers between devices with their start and end apart: 19 -> 22, of which waited for: 10 -> 13; matrix products, arithmetic and copies ran while one was open for 3% -> 5% of each run, Pallas kernels for 12% -> 12%
where the time goes in v3:
time: 78.5 us; the launch traced here: 78.1 us
  waiting for transfers between devices  39.4 us (50%)
  starting transfers between devices  20.9 us (27%)
  Pallas kernels  11.7 us (15%)
  other arithmetic  5.01 us (6%)
  between operations  0.81 us (1%)
    ppermute x9, waiting for transfers between devices, rotate(): return lax.ppermute(x, axis, [(i, (i + shift) % n) for i in range(n)])  33.2 us
    ppermute x9, starting transfers between devices, rotate(): return lax.ppermute(x, axis, [(i, (i + shift) % n) for i in range(n)])  14.2 us
    pallas_call x5, Pallas kernels, call(): pl.pallas_call(kernel, out_shape=outs, in_specs=[pl.BlockSpec(memory_spac...  11.7 us
    ppermute x13, starting transfers between devices, xor_swap(): lax.ppermute(x, axis, [(i, i ^ bit) for i in range(lax.axis_size(axis))])  6.67 us
    ppermute x13, waiting for transfers between devices, xor_swap(): lax.ppermute(x, axis, [(i, i ^ bit) for i in range(lax.axis_size(axis))])  6.13 us
  transfers between devices with their start and end apart: 22, of which 13 were waited for; matrix products, arithmetic and copies ran while one was open for 5% of the time, Pallas kernels for 12%

profile of v3, /device:TPU:8, one launch (start us, length us, event | category | flops | bytes accessed | tf_op | source)
XLA Modules:
  0.0 78.1 jit_solution(9639474021905917285)
XLA Ops:
  0.6 0.0 copy-start
  0.6 0.0 copy-start.1
  0.7 0.0 copy-start.2
  0.7 0.0 copy-start.3
  0.7 0.0 copy-start.4
  0.7 0.1 collective-permute-start.4
  0.8 0.5 collective-permute-start.5
  1.3 0.1 collective-permute-start.6
  1.3 1.3 %collective-permute-done.4.refs_5_.refs_6_.refs_4_.refs_1_ = bf16[10,128,128]{2,1,0:T(8,128)(2,1)S(1)} collective-permute-done((bf16[10,128,128]{2,1,0:T(8,128)(2,1)}, bf16[10,128,128]{2,1,0:T(8,128)(2,1)S(1)}, u32[]{:S(2)}, u32[]{:S(2)}) %collective-permute-start.4) | collective-permute-done | bytes 327712 | tf_op jit(solution)/shard_map/ppermute | solution.py:30
  2.6 0.5 collective-permute-done.5.refs_6_.refs_7_.refs_5_.refs_2_
  3.1 0.5 collective-permute-done.6.refs_7_.refs_8_.refs_6_.refs_3_
  3.5 1.5 %collective-permute-start.8 = (bf16[10,128,128]{2,1,0:T(8,128)(2,1)}, bf16[10,128,128]{2,1,0:T(8,128)(2,1)S(1)}, u32[]{:S(2)}, u32[]{:S(2)}) collective-permute-start(bf16[10,128,128]{2,1,0:T(8,128)(2,1)} %bitcast.14), channel_id=1, source_target_pairs={{0,2},{1,3},{2,0},{3,1},{4,6},{5,7},{6,4},{7,5},{8,10},{9,11},{10,... | collective-permute-start | bytes 983048 | tf_op jit(solution)/shard_map/ppermute | solution.py:30
  5.0 1.6 %collective-permute-start = (bf16[128,1024]{1,0:T(8,128)(2,1)}, bf16[128,1024]{1,0:T(8,128)(2,1)S(1)}, u32[]{:S(2)}, u32[]{:S(2)}) collective-permute-start(bf16[128,1024]{1,0:T(8,128)(2,1)} %param.8), channel_id=1, source_target_pairs={{0,4},{4,8},{8,12},{12,0},{1,5},{5,9},{9,13},{13,1},{2,6},{6,10},{... | collective-permute-start | bytes 786440 | tf_op jit(solution)/shard_map/ppermute | solution.py:26
  6.6 1.6 %collective-permute-start.3 = (bf16[128,1024]{1,0:T(8,128)(2,1)}, bf16[128,1024]{1,0:T(8,128)(2,1)S(1)}, u32[]{:S(2)}, u32[]{:S(2)}) collective-permute-start(bf16[128,1024]{1,0:T(8,128)(2,1)} %param.9), channel_id=1, source_target_pairs={{0,4},{4,8},{8,12},{12,0},{1,5},{5,9},{9,13},{13,1},{2,6},{6,10},{... | collective-permute-start | bytes 786440 | tf_op jit(solution)/shard_map/ppermute | solution.py:26
  8.2 1.3 %pad_maximum_fusion.refs_4_.refs_5_.refs_3_.refs_0_ = bf16[30,128,128]{2,1,0:T(8,128)(2,1)S(1)} fusion(bf16[10,128,128]{2,1,0:T(8,128)(2,1)} %bitcast.20, bf16[10,128,128]{2,1,0:T(8,128)(2,1)} %bitcast.17, bf16[10,128,128]{2,1,0:T(8,128)(2,1)} %bitcast.15), kind=kLoop, calls=%fused_computation.2 | loop fusion | flops 983040 | bytes 1966080 | tf_op jit(solution)/shard_map/concatenate | solution.py:253
  9.5 0.1 reshape.26
  9.6 0.1 reshape.27
  9.6 0.1 reshape.28
  9.7 0.1 concatenate.9.meta
  9.8 1.1 %pad_maximum_fusion.1.own_ref = bf16[2,128,1024]{2,1,0:T(8,128)(2,1)S(1)} fusion(bf16[1,128,1024]{2,1,0:T(8,128)(2,1)} %bitcast.23, bf16[1,128,1024]{2,1,0:T(8,128)(2,1)} %bitcast.22), kind=kLoop, calls=%fused_computation.9 | loop fusion | flops 262144 | bytes 1048576 | tf_op jit(solution)/shard_map/stack | solution.py:250
  10.9 0.6 collective-permute-start.9
  11.5 2.5 %collective-permute-done.8.refs_8_.refs_9_.refs_7_.refs_4_ = bf16[10,128,128]{2,1,0:T(8,128)(2,1)S(1)} collective-permute-done((bf16[10,128,128]{2,1,0:T(8,128)(2,1)}, bf16[10,128,128]{2,1,0:T(8,128)(2,1)S(1)}, u32[]{:S(2)}, u32[]{:S(2)}) %collective-permute-start.8) | collective-permute-done | bytes 327712 | tf_op jit(solution)/shard_map/ppermute | solution.py:30
  14.1 1.7 %collective-permute-start.10 = (bf16[10,128,128]{2,1,0:T(8,128)(2,1)S(1)}, bf16[10,128,128]{2,1,0:T(8,128)(2,1)S(1)}, u32[]{:S(2)}, u32[]{:S(2)}) collective-permute-start(bf16[10,128,128]{2,1,0:T(8,128)(2,1)S(1)} %bitcast.21), channel_id=1, source_target_pairs={{0,2},{1,3},{2,0},{3,1},{4,6},{5,7},{6,4},{7,5},{8,10},{9,11},{10,... | collective-permute-start | bytes 983048 | tf_op jit(solution)/shard_map/ppermute | solution.py:30
  15.8 0.0 collective-permute-done.refs_0_
  15.8 1.6 %collective-permute-start.1 = (bf16[128,1024]{1,0:T(8,128)(2,1)S(1)}, bf16[128,1024]{1,0:T(8,128)(2,1)S(1)}, u32[]{:S(2)}, u32[]{:S(2)}) collective-permute-start(bf16[128,1024]{1,0:T(8,128)(2,1)S(1)} %collective-permute-done.refs_0_), channel_id=1, source_target_pairs={{0,4},{4,8},{8,12},{12,0},{1,5},{5,9},{9,13},{13,1},{2,6},{6,10},{... | collective-permute-start | bytes 786440 | tf_op jit(solution)/shard_map/ppermute | solution.py:26
  17.4 2.7 %collective-permute-done.3.refs_2_.refs_0_ = bf16[128,1024]{1,0:T(8,128)(2,1)S(1)} collective-permute-done((bf16[128,1024]{1,0:T(8,128)(2,1)}, bf16[128,1024]{1,0:T(8,128)(2,1)S(1)}, u32[]{:S(2)}, u32[]{:S(2)}) %collective-permute-start.3) | collective-permute-done | bytes 262176 | tf_op jit(solution)/shard_map/ppermute | solution.py:26
  20.0 1.6 %collective-permute-start.7 = (bf16[128,1024]{1,0:T(8,128)(2,1)S(1)}, bf16[128,1024]{1,0:T(8,128)(2,1)S(1)}, u32[]{:S(2)}, u32[]{:S(2)}) collective-permute-start(bf16[128,1024]{1,0:T(8,128)(2,1)S(1)} %collective-permute-done.3.refs_2_.refs_0_), channel_id=1, source_target_pairs={{0,4},{4,8},{8,12},{12,0},{1,5},{5,9},{9,13},{13,1},{2,6},{6,10},{... | collective-permute-start | bytes 786440 | tf_op jit(solution)/shard_map/ppermute | solution.py:26
  21.6 0.0 collective-permute-done.9.refs_9_.refs_10_.refs_8_.refs_5_
  21.6 4.0 %collective-permute-done.1.refs_1_ = bf16[128,1024]{1,0:T(8,128)(2,1)S(1)} collective-permute-done((bf16[128,1024]{1,0:T(8,128)(2,1)S(1)}, bf16[128,1024]{1,0:T(8,128)(2,1)S(1)}, u32[]{:S(2)}, u32[]{:S(2)}) %collective-permute-start.1) | collective-permute-done | bytes 262176 | tf_op jit(solution)/shard_map/ppermute | solution.py:26
  25.7 0.0 collective-permute-start.12
  25.7 0.5 collective-permute-start.11
  26.2 1.4 %collective-permute-done.10.refs_10_.refs_11_.refs_9_.refs_6_ = bf16[10,128,128]{2,1,0:T(8,128)(2,1)S(1)} collective-permute-done((bf16[10,128,128]{2,1,0:T(8,128)(2,1)S(1)}, bf16[10,128,128]{2,1,0:T(8,128)(2,1)S(1)}, u32[]{:S(2)}, u32[]{:S(2)}) %collective-permute-start.10) | collective-permute-done | bytes 327712 | tf_op jit(solution)/shard_map/ppermute | solution.py:30
  27.5 0.0 collective-permute-start.13
  27.5 1.6 %collective-permute-start.2 = (bf16[128,1024]{1,0:T(8,128)(2,1)S(1)}, bf16[128,1024]{1,0:T(8,128)(2,1)S(1)}, u32[]{:S(2)}, u32[]{:S(2)}) collective-permute-start(bf16[128,1024]{1,0:T(8,128)(2,1)S(1)} %collective-permute-done.1.refs_1_), channel_id=1, source_target_pairs={{0,4},{4,8},{8,12},{12,0},{1,5},{5,9},{9,13},{13,1},{2,6},{6,10},{... | collective-permute-start | bytes 786440 | tf_op jit(solution)/shard_map/ppermute | solution.py:26
  29.1 1.0 %collective-permute-done.7.refs_3_.refs_1_ = bf16[128,1024]{1,0:T(8,128)(2,1)S(1)} collective-permute-done((bf16[128,1024]{1,0:T(8,128)(2,1)S(1)}, bf16[128,1024]{1,0:T(8,128)(2,1)S(1)}, u32[]{:S(2)}, u32[]{:S(2)}) %collective-permute-start.7) | collective-permute-done | bytes 262176 | tf_op jit(solution)/shard_map/ppermute | solution.py:26
  30.1 1.6 %collective-permute-start.14 = (bf16[128,1024]{1,0:T(8,128)(2,1)S(1)}, bf16[128,1024]{1,0:T(8,128)(2,1)S(1)}, u32[]{:S(2)}, u32[]{:S(2)}) collective-permute-start(bf16[128,1024]{1,0:T(8,128)(2,1)S(1)} %collective-permute-done.7.refs_3_.refs_1_), channel_id=1, source_target_pairs={{0,4},{4,8},{8,12},{12,0},{1,5},{5,9},{9,13},{13,1},{2,6},{6,10},{... | collective-permute-start | bytes 786440 | tf_op jit(solution)/shard_map/ppermute | solution.py:26
  31.7 0.0 collective-permute-done.12.refs_12_.refs_13_.refs_11_.refs_8_
  31.7 0.0 collective-permute-done.11.refs_11_.refs_12_.refs_10_.refs_7_
  31.7 0.0 collective-permute-done.13.refs_13_.refs_14_.refs_12_.refs_9_
  31.7 2.9 %shard_map.111 = (f32[33,128,128]{2,1,0:T(8,128)S(1)}, f32[33,128,128]{2,1,0:T(8,128)S(1)}, f32[33,128,128]{2,1,0:T(8,128)S(1)}) custom-call(s32[122]{0:T(128)S(1)} %concatenate.9.meta, bf16[2,128,1024]{2,1,0:T(8,128)(2,1)S(1)} %pad_maximum_fusion.1.own_ref, bf16[128,1024]{1,0:T(8,128)(2,1)S(1)} %collective-permute-done.refs_0_, ...), custom_call_target="tpu_custom_call" | custom-call | flops 1048576 | bytes 8388608 | tf_op jit(solution)/shard_map/pallas_call | solution.py:232
  34.7 2.0 %collective-permute-done.2.refs_2_ = bf16[128,1024]{1,0:T(8,128)(2,1)S(1)} collective-permute-done((bf16[128,1024]{1,0:T(8,128)(2,1)S(1)}, bf16[128,1024]{1,0:T(8,128)(2,1)S(1)}, u32[]{:S(2)}, u32[]{:S(2)}) %collective-permute-start.2) | collective-permute-done | bytes 262176 | tf_op jit(solution)/shard_map/ppermute | solution.py:26
  36.6 2.3 %shard_map.112 = (f32[32,128,128]{2,1,0:T(8,128)S(1)}, f32[32,128,128]{2,1,0:T(8,128)S(1)}, bf16[32,128,128]{2,1,0:T(8,128)(2,1)S(1)}, bf16[32,128,128]{2,1,0:T(8,128)(2,1)S(1)}) custom-call(s32[122]{0:T(128)S(1)} %concatenate.9.meta, bf16[2,128,1024]{2,1,0:T(8,128)(2,1)S(1)} %pad_maximum_fusion.1.own_ref, ...), custom_call_target="tpu_custom_call" | custom-call | flops 1048576 | bytes 8388608 | tf_op jit(solution)/shard_map/pallas_call | solution.py:232
  38.9 2.9 %collective-permute-done.14.refs_2_ = bf16[128,1024]{1,0:T(8,128)(2,1)S(1)} collective-permute-done((bf16[128,1024]{1,0:T(8,128)(2,1)S(1)}, bf16[128,1024]{1,0:T(8,128)(2,1)S(1)}, u32[]{:S(2)}, u32[]{:S(2)}) %collective-permute-start.14) | collective-permute-done | bytes 262176 | tf_op jit(solution)/shard_map/ppermute | solution.py:26
  41.9 2.4 %shard_map.113 = (bf16[32,128,128]{2,1,0:T(8,128)(2,1)S(1)}, bf16[32,128,128]{2,1,0:T(8,128)(2,1)S(1)}, bf16[32,128,128]{2,1,0:T(8,128)(2,1)S(1)}, bf16[30,128,128]{2,1,0:T(8,128)(2,1)S(1)}, f32[30,128,128]{2,1,0:T(8,128)S(1)}) custom-call(s32[122]{0:T(128)S(1)} %concatenate.9.meta, bf16[2,128,1024]{2,1,0:T(8,128)(2,1)S(1)} %pad_maximum_fusion.1.own_ref, ...), custom_call_target="tpu_custom_call" | custom-call | flops 1048576 | bytes 8388608 | tf_op jit(solution)/shard_map/pallas_call | solution.py:232
  44.3 0.1 collective-permute-start.18
  44.4 2.7 %shard_map.114 = (f32[128,1024]{1,0:T(8,128)S(1)}, bf16[128,1024]{1,0:T(8,128)(2,1)S(1)}, bf16[128,1024]{1,0:T(8,128)(2,1)S(1)}, bf16[128,1024]{1,0:T(8,128)(2,1)S(1)}) custom-call(s32[122]{0:T(128)S(1)} %concatenate.9.meta, bf16[32,128,128]{2,1,0:T(8,128)(2,1)S(1)} %get-tuple-element.56.gate_delta, bf16[32,128,128]{2,1,0:T(8,128)(2,1)S(1)} %get-tuple-element.47.up_delta, ...), custom_call_target="tpu_custom_call" | custom-call | flops 1048576 | bytes 8388608 | tf_op jit(solution)/shard_map/pallas_call | solution.py:232
  47.1 1.6 %collective-permute-start.15 = (bf16[128,1024]{1,0:T(8,128)(2,1)S(1)}, bf16[128,1024]{1,0:T(8,128)(2,1)S(1)}, u32[]{:S(2)}, u32[]{:S(2)}) collective-permute-start(bf16[128,1024]{1,0:T(8,128)(2,1)S(1)} %get-tuple-element.49), channel_id=1, source_target_pairs={{0,4},{4,8},{8,12},{12,0},{1,5},{5,9},{9,13},{13,1},{2,6},{6,10},{... | collective-permute-start | bytes 786440 | tf_op jit(solution)/shard_map/ppermute | solution.py:26
  48.8 0.0 collective-permute-done.18
  48.8 0.3 convert_add_fusion.1
  49.1 1.5 %collective-permute-start.21 = (bf16[30,128,128]{2,1,0:T(8,128)(2,1)S(1)}, bf16[30,128,128]{2,1,0:T(8,128)(2,1)S(1)}, u32[]{:S(2)}, u32[]{:S(2)}) collective-permute-start(bf16[30,128,128]{2,1,0:T(8,128)(2,1)S(1)} %convert_add_fusion.1), channel_id=1, source_target_pairs={{0,2},{1,3},{2,0},{3,1},{4,6},{5,7},{6,4},{7,5},{8,10},{9,11},{10,... | collective-permute-start | bytes 2949128 | tf_op jit(solution)/shard_map/ppermute | solution.py:30
  50.6 3.1 %collective-permute-start.16 = (bf16[128,1024]{1,0:T(8,128)(2,1)S(1)}, bf16[128,1024]{1,0:T(8,128)(2,1)S(1)}, u32[]{:S(2)}, u32[]{:S(2)}) collective-permute-start(bf16[128,1024]{1,0:T(8,128)(2,1)S(1)} %get-tuple-element.50), channel_id=1, source_target_pairs={{0,8},{4,12},{8,0},{12,4},{1,9},{5,13},{9,1},{13,5},{2,10},{6,14},... | collective-permute-start | bytes 786440 | tf_op jit(solution)/shard_map/ppermute | solution.py:26
  53.7 0.0 collective-permute-start.17
  53.7 1.3 %shard_map.115 = (f32[30,128,128]{2,1,0:T(8,128)S(1)}, bf16[15,128,128]{2,1,0:T(8,128)(2,1)S(1)}, bf16[15,128,128]{2,1,0:T(8,128)(2,1)S(1)}) custom-call(s32[122]{0:T(128)S(1)} %concatenate.9.meta, bf16[32,128,128]{2,1,0:T(8,128)(2,1)S(1)} %get-tuple-element.41.xs, bf16[32,128,128]{2,1,0:T(8,128)(2,1)S(1)} %get-tuple-element.52.gs, ...), custom_call_target="tpu_custom_call" | custom-call | flops 1048576 | bytes 8388608 | tf_op jit(solution)/shard_map/pallas_call | solution.py:232
  55.1 0.1 collective-permute-start.19
  55.2 1.8 %collective-permute-done.15 = bf16[128,1024]{1,0:T(8,128)(2,1)S(1)} collective-permute-done((bf16[128,1024]{1,0:T(8,128)(2,1)S(1)}, bf16[128,1024]{1,0:T(8,128)(2,1)S(1)}, u32[]{:S(2)}, u32[]{:S(2)}) %collective-permute-start.15) | collective-permute-done | bytes 262176 | tf_op jit(solution)/shard_map/ppermute | solution.py:26
  57.0 0.0 collective-permute-start.20
  57.0 14.8 %collective-permute-done.16 = bf16[128,1024]{1,0:T(8,128)(2,1)S(1)} collective-permute-done((bf16[128,1024]{1,0:T(8,128)(2,1)S(1)}, bf16[128,1024]{1,0:T(8,128)(2,1)S(1)}, u32[]{:S(2)}, u32[]{:S(2)}) %collective-permute-start.16) | collective-permute-done | bytes 262176 | tf_op jit(solution)/shard_map/ppermute | solution.py:26
  71.8 3.9 %collective-permute-done.17 = bf16[128,1024]{1,0:T(8,128)(2,1)S(1)} collective-permute-done((bf16[128,1024]{1,0:T(8,128)(2,1)S(1)}, bf16[128,1024]{1,0:T(8,128)(2,1)S(1)}, u32[]{:S(2)}, u32[]{:S(2)}) %collective-permute-start.17) | collective-permute-done | bytes 262176 | tf_op jit(solution)/shard_map/ppermute | solution.py:26
  75.8 0.9 %add_convert_fusion = bf16[128,1024]{1,0:T(8,128)(2,1)} fusion(bf16[128,1024]{1,0:T(8,128)(2,1)S(1)} %collective-permute-done.17, bf16[128,1024]{1,0:T(8,128)(2,1)S(1)} %collective-permute-done.16, f32[128,1024]{1,0:T(8,128)S(1)} %get-tuple-element.48, bf16[128,1024]{1,0:T(8,128)(2,1)S(1)} %collective-permute-done.15), kind=kLoop, calls=%fused_computation.10 | loop fusion | flops 917504 | bytes 1572864 | tf_op jit(solution)/shard_map/convert_element_type | solution.py:331
  76.6 0.0 collective-permute-done.19
  76.6 0.0 collective-permute-done.20
  76.6 0.3 convert_add_fusion
  77.0 0.0 collective-permute-done.21
  77.0 1.1 %fusion.5 = (bf16[1,1,10,128,128]{4,3,2,1,0:T(8,128)(2,1)}, bf16[1,1,10,128,128]{4,3,2,1,0:T(8,128)(2,1)}, bf16[1,1,10,128,128]{4,3,2,1,0:T(8,128)(2,1)}) fusion(f32[30,128,128]{2,1,0:T(8,128)S(1)} %convert_add_fusion, bf16[30,128,128]{2,1,0:T(8,128)(2,1)S(1)} %collective-permute-done.21), kind=kLoop, calls=%fused_computation.13 | loop fusion | flops 1474560 | bytes 3932160 | tf_op jit(solution)/shard_map/reshape | solution.py:326
  (5 shorter events, 0.0 us)
Async XLA Ops:
  0.6 10.3 %copy-start = (bf16[1,1,10,128,128]{4,3,2,1,0:T(8,128)(2,1)S(1)}, bf16[1,1,10,128,128]{4,3,2,1,0:T(8,128)(2,1)}, u32[]{:S(2)}) copy-start(bf16[1,1,10,128,128]{4,3,2,1,0:T(8,128)(2,1)} %param.11) | copy-start | bytes 983044
  0.6 13.4 %copy-start.1 = (bf16[1,1,10,128,128]{4,3,2,1,0:T(8,128)(2,1)S(1)}, bf16[1,1,10,128,128]{4,3,2,1,0:T(8,128)(2,1)}, u32[]{:S(2)}) copy-start(bf16[1,1,10,128,128]{4,3,2,1,0:T(8,128)(2,1)} %param.12) | copy-start | bytes 983044
  0.7 8.8 %copy-start.2 = (s32[1,4,10]{2,1,0:T(4,128)S(1)}, s32[1,4,10]{2,1,0:T(4,128)}, u32[]{:S(2)}) copy-start(s32[1,4,10]{2,1,0:T(4,128)} %param.13) | copy-start | bytes 484
  0.7 8.9 %copy-start.3 = (s32[1,4,10]{2,1,0:T(4,128)S(1)}, s32[1,4,10]{2,1,0:T(4,128)}, u32[]{:S(2)}) copy-start(s32[1,4,10]{2,1,0:T(4,128)} %param.14) | copy-start | bytes 484
  0.7 9.0 %copy-start.4 = (s32[1,4,10]{2,1,0:T(4,128)S(1)}, s32[1,4,10]{2,1,0:T(4,128)}, u32[]{:S(2)}) copy-start(s32[1,4,10]{2,1,0:T(4,128)} %param.15) | copy-start | bytes 484
  0.7 1.9 %collective-permute-start.4 = (bf16[10,128,128]{2,1,0:T(8,128)(2,1)}, bf16[10,128,128]{2,1,0:T(8,128)(2,1)S(1)}, u32[]{:S(2)}, u32[]{:S(2)}) collective-permute-start(bf16[10,128,128]{2,1,0:T(8,128)(2,1)} %bitcast.13), channel_id=1, source_target_pairs={{0,1},{1,0},{2,3},{3,2},{4,5},{5,4},{6,7},{7,6},{8,9},{9,8},{10,11... | collective-permute-start | bytes 983048 | tf_op jit(solution)/shard_map/ppermute | solution.py:30
  0.8 2.3 %collective-permute-start.5 = (bf16[10,128,128]{2,1,0:T(8,128)(2,1)}, bf16[10,128,128]{2,1,0:T(8,128)(2,1)S(1)}, u32[]{:S(2)}, u32[]{:S(2)}) collective-permute-start(bf16[10,128,128]{2,1,0:T(8,128)(2,1)} %bitcast.16), channel_id=1, source_target_pairs={{0,1},{1,0},{2,3},{3,2},{4,5},{5,4},{6,7},{7,6},{8,9},{9,8},{10,11... | collective-permute-start | bytes 983048 | tf_op jit(solution)/shard_map/ppermute | solution.py:30
  1.3 2.3 %collective-permute-start.6 = (bf16[10,128,128]{2,1,0:T(8,128)(2,1)}, bf16[10,128,128]{2,1,0:T(8,128)(2,1)S(1)}, u32[]{:S(2)}, u32[]{:S(2)}) collective-permute-start(bf16[10,128,128]{2,1,0:T(8,128)(2,1)} %bitcast.19), channel_id=1, source_target_pairs={{0,1},{1,0},{2,3},{3,2},{4,5},{5,4},{6,7},{7,6},{8,9},{9,8},{10,11... | collective-permute-start | bytes 983048 | tf_op jit(solution)/shard_map/ppermute | solution.py:30
  3.5 10.5 %collective-permute-start.8 = (bf16[10,128,128]{2,1,0:T(8,128)(2,1)}, bf16[10,128,128]{2,1,0:T(8,128)(2,1)S(1)}, u32[]{:S(2)}, u32[]{:S(2)}) collective-permute-start(bf16[10,128,128]{2,1,0:T(8,128)(2,1)} %bitcast.14), channel_id=1, source_target_pairs={{0,2},{1,3},{2,0},{3,1},{4,6},{5,7},{6,4},{7,5},{8,10},{9,11},{10,... | collective-permute-start | bytes 983048 | tf_op jit(solution)/shard_map/ppermute | solution.py:30
  5.0 10.8 %collective-permute-start = (bf16[128,1024]{1,0:T(8,128)(2,1)}, bf16[128,1024]{1,0:T(8,128)(2,1)S(1)}, u32[]{:S(2)}, u32[]{:S(2)}) collective-permute-start(bf16[128,1024]{1,0:T(8,128)(2,1)} %param.8), channel_id=1, source_target_pairs={{0,4},{4,8},{8,12},{12,0},{1,5},{5,9},{9,13},{13,1},{2,6},{6,10},{... | collective-permute-start | bytes 786440 | tf_op jit(solution)/shard_map/ppermute | solution.py:26
  6.6 13.4 %collective-permute-start.3 = (bf16[128,1024]{1,0:T(8,128)(2,1)}, bf16[128,1024]{1,0:T(8,128)(2,1)S(1)}, u32[]{:S(2)}, u32[]{:S(2)}) collective-permute-start(bf16[128,1024]{1,0:T(8,128)(2,1)} %param.9), channel_id=1, source_target_pairs={{0,4},{4,8},{8,12},{12,0},{1,5},{5,9},{9,13},{13,1},{2,6},{6,10},{... | collective-permute-start | bytes 786440 | tf_op jit(solution)/shard_map/ppermute | solution.py:26
  10.9 10.7 %collective-permute-start.9 = (bf16[10,128,128]{2,1,0:T(8,128)(2,1)S(1)}, bf16[10,128,128]{2,1,0:T(8,128)(2,1)S(1)}, u32[]{:S(2)}, u32[]{:S(2)}) collective-permute-start(bf16[10,128,128]{2,1,0:T(8,128)(2,1)S(1)} %bitcast.18), channel_id=1, source_target_pairs={{0,2},{1,3},{2,0},{3,1},{4,6},{5,7},{6,4},{7,5},{8,10},{9,11},{10,... | collective-permute-start | bytes 983048 | tf_op jit(solution)/shard_map/ppermute | solution.py:30
  14.1 13.5 %collective-permute-start.10 = (bf16[10,128,128]{2,1,0:T(8,128)(2,1)S(1)}, bf16[10,128,128]{2,1,0:T(8,128)(2,1)S(1)}, u32[]{:S(2)}, u32[]{:S(2)}) collective-permute-start(bf16[10,128,128]{2,1,0:T(8,128)(2,1)S(1)} %bitcast.21), channel_id=1, source_target_pairs={{0,2},{1,3},{2,0},{3,1},{4,6},{5,7},{6,4},{7,5},{8,10},{9,11},{10,... | collective-permute-start | bytes 983048 | tf_op jit(solution)/shard_map/ppermute | solution.py:30
  15.8 9.9 %collective-permute-start.1 = (bf16[128,1024]{1,0:T(8,128)(2,1)S(1)}, bf16[128,1024]{1,0:T(8,128)(2,1)S(1)}, u32[]{:S(2)}, u32[]{:S(2)}) collective-permute-start(bf16[128,1024]{1,0:T(8,128)(2,1)S(1)} %collective-permute-done.refs_0_), channel_id=1, source_target_pairs={{0,4},{4,8},{8,12},{12,0},{1,5},{5,9},{9,13},{13,1},{2,6},{6,10},{... | collective-permute-start | bytes 786440 | tf_op jit(solution)/shard_map/ppermute | solution.py:26
  20.0 10.1 %collective-permute-start.7 = (bf16[128,1024]{1,0:T(8,128)(2,1)S(1)}, bf16[128,1024]{1,0:T(8,128)(2,1)S(1)}, u32[]{:S(2)}, u32[]{:S(2)}) collective-permute-start(bf16[128,1024]{1,0:T(8,128)(2,1)S(1)} %collective-permute-done.3.refs_2_.refs_0_), channel_id=1, source_target_pairs={{0,4},{4,8},{8,12},{12,0},{1,5},{5,9},{9,13},{13,1},{2,6},{6,10},{... | collective-permute-start | bytes 786440 | tf_op jit(solution)/shard_map/ppermute | solution.py:26
  25.7 6.1 %collective-permute-start.12 = (bf16[10,128,128]{2,1,0:T(8,128)(2,1)S(1)}, bf16[10,128,128]{2,1,0:T(8,128)(2,1)S(1)}, u32[]{:S(2)}, u32[]{:S(2)}) collective-permute-start(bf16[10,128,128]{2,1,0:T(8,128)(2,1)S(1)} %collective-permute-done.9.refs_9_.refs_10_.refs_8_.refs_5_), channel_id=1, source_target_pairs={{0,1},{1,0},{2,3},{3,2},{4,5},{5,4},{6,7},{7,6},{8,9},{9,8},{10,11... | collective-permute-start | bytes 983048 | tf_op jit(solution)/shard_map/ppermute | solution.py:30
  25.7 6.1 %collective-permute-start.11 = (bf16[10,128,128]{2,1,0:T(8,128)(2,1)S(1)}, bf16[10,128,128]{2,1,0:T(8,128)(2,1)S(1)}, u32[]{:S(2)}, u32[]{:S(2)}) collective-permute-start(bf16[10,128,128]{2,1,0:T(8,128)(2,1)S(1)} %collective-permute-done.8.refs_8_.refs_9_.refs_7_.refs_4_), channel_id=1, source_target_pairs={{0,1},{1,0},{2,3},{3,2},{4,5},{5,4},{6,7},{7,6},{8,9},{9,8},{10,11... | collective-permute-start | bytes 983048 | tf_op jit(solution)/shard_map/ppermute | solution.py:30
  27.5 4.2 %collective-permute-start.13 = (bf16[10,128,128]{2,1,0:T(8,128)(2,1)S(1)}, bf16[10,128,128]{2,1,0:T(8,128)(2,1)S(1)}, u32[]{:S(2)}, u32[]{:S(2)}) collective-permute-start(bf16[10,128,128]{2,1,0:T(8,128)(2,1)S(1)} %collective-permute-done.10.refs_10_.refs_11_.refs_9_.refs_6_), channel_id=1, source_target_pairs={{0,1},{1,0},{2,3},{3,2},{4,5},{5,4},{6,7},{7,6},{8,9},{9,8},{10,11... | collective-permute-start | bytes 983048 | tf_op jit(solution)/shard_map/ppermute | solution.py:30
  27.5 9.1 %collective-permute-start.2 = (bf16[128,1024]{1,0:T(8,128)(2,1)S(1)}, bf16[128,1024]{1,0:T(8,128)(2,1)S(1)}, u32[]{:S(2)}, u32[]{:S(2)}) collective-permute-start(bf16[128,1024]{1,0:T(8,128)(2,1)S(1)} %collective-permute-done.1.refs_1_), channel_id=1, source_target_pairs={{0,4},{4,8},{8,12},{12,0},{1,5},{5,9},{9,13},{13,1},{2,6},{6,10},{... | collective-permute-start | bytes 786440 | tf_op jit(solution)/shard_map/ppermute | solution.py:26
  30.1 11.7 %collective-permute-start.14 = (bf16[128,1024]{1,0:T(8,128)(2,1)S(1)}, bf16[128,1024]{1,0:T(8,128)(2,1)S(1)}, u32[]{:S(2)}, u32[]{:S(2)}) collective-permute-start(bf16[128,1024]{1,0:T(8,128)(2,1)S(1)} %collective-permute-done.7.refs_3_.refs_1_), channel_id=1, source_target_pairs={{0,4},{4,8},{8,12},{12,0},{1,5},{5,9},{9,13},{13,1},{2,6},{6,10},{... | collective-permute-start | bytes 786440 | tf_op jit(solution)/shard_map/ppermute | solution.py:26
  44.3 4.4 %collective-permute-start.18 = (bf16[30,128,128]{2,1,0:T(8,128)(2,1)S(1)}, bf16[30,128,128]{2,1,0:T(8,128)(2,1)S(1)}, u32[]{:S(2)}, u32[]{:S(2)}) collective-permute-start(bf16[30,128,128]{2,1,0:T(8,128)(2,1)S(1)} %get-tuple-element.54), channel_id=1, source_target_pairs={{0,1},{1,0},{2,3},{3,2},{4,5},{5,4},{6,7},{7,6},{8,9},{9,8},{10,11... | collective-permute-start | bytes 2949128 | tf_op jit(solution)/shard_map/ppermute | solution.py:30
  47.1 9.9 %collective-permute-start.15 = (bf16[128,1024]{1,0:T(8,128)(2,1)S(1)}, bf16[128,1024]{1,0:T(8,128)(2,1)S(1)}, u32[]{:S(2)}, u32[]{:S(2)}) collective-permute-start(bf16[128,1024]{1,0:T(8,128)(2,1)S(1)} %get-tuple-element.49), channel_id=1, source_target_pairs={{0,4},{4,8},{8,12},{12,0},{1,5},{5,9},{9,13},{13,1},{2,6},{6,10},{... | collective-permute-start | bytes 786440 | tf_op jit(solution)/shard_map/ppermute | solution.py:26
  49.1 27.9 %collective-permute-start.21 = (bf16[30,128,128]{2,1,0:T(8,128)(2,1)S(1)}, bf16[30,128,128]{2,1,0:T(8,128)(2,1)S(1)}, u32[]{:S(2)}, u32[]{:S(2)}) collective-permute-start(bf16[30,128,128]{2,1,0:T(8,128)(2,1)S(1)} %convert_add_fusion.1), channel_id=1, source_target_pairs={{0,2},{1,3},{2,0},{3,1},{4,6},{5,7},{6,4},{7,5},{8,10},{9,11},{10,... | collective-permute-start | bytes 2949128 | tf_op jit(solution)/shard_map/ppermute | solution.py:30
  50.6 21.2 %collective-permute-start.16 = (bf16[128,1024]{1,0:T(8,128)(2,1)S(1)}, bf16[128,1024]{1,0:T(8,128)(2,1)S(1)}, u32[]{:S(2)}, u32[]{:S(2)}) collective-permute-start(bf16[128,1024]{1,0:T(8,128)(2,1)S(1)} %get-tuple-element.50), channel_id=1, source_target_pairs={{0,8},{4,12},{8,0},{12,4},{1,9},{5,13},{9,1},{13,5},{2,10},{6,14},... | collective-permute-start | bytes 786440 | tf_op jit(solution)/shard_map/ppermute | solution.py:26
  53.7 22.0 %collective-permute-start.17 = (bf16[128,1024]{1,0:T(8,128)(2,1)S(1)}, bf16[128,1024]{1,0:T(8,128)(2,1)S(1)}, u32[]{:S(2)}, u32[]{:S(2)}) collective-permute-start(bf16[128,1024]{1,0:T(8,128)(2,1)S(1)} %get-tuple-element.51), channel_id=1, source_target_pairs={{0,12},{4,0},{8,4},{12,8},{1,13},{5,1},{9,5},{13,9},{2,14},{6,2},{... | collective-permute-start | bytes 786440 | tf_op jit(solution)/shard_map/ppermute | solution.py:26
  55.1 21.5 %collective-permute-start.19 = (bf16[15,128,128]{2,1,0:T(8,128)(2,1)S(1)}, bf16[15,128,128]{2,1,0:T(8,128)(2,1)S(1)}, u32[]{:S(2)}, u32[]{:S(2)}) collective-permute-start(bf16[15,128,128]{2,1,0:T(8,128)(2,1)S(1)} %get-tuple-element.58), channel_id=1, source_target_pairs={{0,1},{1,0},{2,3},{3,2},{4,5},{5,4},{6,7},{7,6},{8,9},{9,8},{10,11... | collective-permute-start | bytes 1474568 | tf_op jit(solution)/shard_map/ppermute | solution.py:30
  57.0 19.6 %collective-permute-start.20 = (bf16[15,128,128]{2,1,0:T(8,128)(2,1)S(1)}, bf16[15,128,128]{2,1,0:T(8,128)(2,1)S(1)}, u32[]{:S(2)}, u32[]{:S(2)}) collective-permute-start(bf16[15,128,128]{2,1,0:T(8,128)(2,1)S(1)} %get-tuple-element.59), channel_id=1, source_target_pairs={{0,1},{1,0},{2,3},{3,2},{4,5},{5,4},{6,7},{7,6},{8,9},{9,8},{10,11... | collective-permute-start | bytes 1474568 | tf_op jit(solution)/shard_map/ppermute | solution.py:30

commit v4 on v3

--- a/solution.py
+++ b/solution.py
@@ -87,7 +87,7 @@
 def take_groups(refs, places):
     groups, at = {}, 0
     for j in places:
-        size = 3 if j else 1
+        size = 3 if j > 1 else 1
         groups[j] = refs[at : at + size]
         at += size
     return groups, refs[at:]
@@ -195,23 +195,38 @@
         partial_grads(d, j, meta, xs, gs, act, gate_delta, up_delta, part_ref)
 
 
-def input_kernel(d, meta, gate_delta, up_delta, *refs):
+def input_kernel(d, shifts, meta, gate_delta, up_delta, *refs):
     groups, outs = take_groups(refs, range(d.n_dp))
     out_refs, acc = outs[:-1], outs[-1]
     me_blk, me_dp = d.here(meta)
-    acc[...] = jnp.zeros_like(acc)
-    for j in range(d.n_dp):
-        owner = me_dp ^ j
+
+    def add_owner(owner, group, first_row):
         for matrix, delta in ((0, gate_delta), (1, up_delta)):
             for s in range(d.cap):
                 used, row, col = d.place(meta, matrix, owner, s)
-                acc[jnp.where(used, row, d.rows)] += lax.dot_general(
-                    delta[col], block(d, groups[j], matrix, s), NT, preferred_element_type=F32
+                acc[jnp.where(used, row - first_row, acc.shape[0] - 1)] += lax.dot_general(
+                    delta[col], block(d, group, matrix, s), NT, preferred_element_type=F32
                 )
-    for shift, out_ref in enumerate(out_refs):
+
+    if not d.paired:
+        acc[...] = jnp.zeros_like(acc)
+        for j, group in groups.items():
+            add_owner(me_dp ^ j, group, 0)
+    for shift, out_ref in zip(shifts, out_refs):
         shard = lax.rem(me_blk + shift, d.n_blk)
+        first_row = shard * d.shard_blocks
+        if d.paired:
+            acc[...] = jnp.zeros_like(acc)
+            for j, group in groups.items():
+                pl.when(me_dp ^ j == shard)(functools.partial(add_owner, shard, group, first_row))
         for b in range(d.shard_blocks):
-            out_ref[:, b * BLOCK : (b + 1) * BLOCK] = acc[shard * d.shard_blocks + b].astype(out_ref.dtype)
+            row = b if d.paired else first_row + b
+            out_ref[:, b * BLOCK : (b + 1) * BLOCK] = acc[row].astype(out_ref.dtype)
+
+
+def partial_kernel(d, places, meta, xs, gs, act, gate_delta, up_delta, *part_refs):
+    for j, part_ref in zip(places, part_refs):
+        partial_grads(d, j, meta, xs, gs, act, gate_delta, up_delta, part_ref)
 
 
 class Pieces:
@@ -250,18 +265,19 @@
     own_pair = jnp.stack([inputs, out_grad])
 
     matrices = [blocks[0, 0] for blocks in (gate_blocks, up_blocks, down_blocks)]
-    groups = {0: [jnp.concatenate(matrices)], 1: [xor_swap(x, "dp", 1) for x in matrices]}
+    groups = {0: [jnp.concatenate(matrices)]}
+    groups[1] = [xor_swap(groups[0][0], "dp", 1)]
     own = (own_pair, groups[0][0], meta)
+    x_pieces, g_pieces = ring_gather(inputs, out_grad, "blk", (*own, *groups[1]))
     bit = 2
     while bit < n_dp:
         for j in range(0, bit, 2):
             gate, up, down = groups[j] if j else matrices
-            gate = xor_swap(after(gate, *groups[1]), "dp", bit)
-            up = xor_swap(after(up, *own), "dp", bit)
-            down = xor_swap(after(down, gate), "dp", bit)
+            gate = xor_swap(after(gate, *()), "dp", bit)
+            up = xor_swap(after(up, *(own_pair, meta)), "dp", bit)
+            down = xor_swap(after(down, *(gate,)), "dp", bit)
             groups[j ^ bit] = [gate, up, down]
         bit *= 2
-    x_pieces, g_pieces = ring_gather(inputs, out_grad, "blk", (*own, *groups[1]))
     for j in range(2, n_dp, 2):
         groups[j + 1] = [xor_swap(after(x, x_pieces[-2]), "dp", 1) for x in groups[j]]
 
@@ -286,30 +302,38 @@
         [pltpu.VMEM((d.cols + 1, tokens, BLOCK), F32)] * 2, LATE_MIB, LATE_COST,
         meta, own_pair, *x_pieces[1:], gate_early, up_early, *everyone,
     )
-    later = list(range(n_dp - 1, 1, -1))
-    gate_delta, up_delta, gs, *parts_later = call(
-        functools.partial(delta_kernel, d, later),
-        [grid(d.cols, BF16), grid(d.cols, BF16), grid(d.rows, BF16)] + [part(j) for j in later],
+    sent, kept_back = list(range(3, n_dp, 2)), list(range(2, n_dp, 2))
+    gate_delta, up_delta, gs, *parts_sent = call(
+        functools.partial(delta_kernel, d, sent),
+        [grid(d.cols, BF16), grid(d.cols, BF16), grid(d.rows, BF16)] + [part(j) for j in sent],
         [pltpu.VMEM((d.cols + 1, tokens, BLOCK), F32)],
         DELTA_MIB, DELTA_COST, meta, own_pair, xs, act, gate_slope, up_slope, hidden, *g_pieces[1:], *everyone,
     )
-    own, *far = call(
-        functools.partial(input_kernel, d),
-        [jax.ShapeDtypeStruct((tokens, width), F32)] + [jax.ShapeDtypeStruct((tokens, width), BF16)] * (n_blk - 1),
-        [pltpu.VMEM((d.rows + 1, tokens, BLOCK), F32)],
-        INPUT_MIB, INPUT_COST, meta, gate_delta, up_delta, *everyone,
-    )
-    far_parts = dict(zip(later, parts_later))
-
-    relayed = []
-    for j in range(2, n_dp, 2):
-        other = xor_swap(far_parts[j + 1], "dp", 1)
-        relayed.append(far_parts[j] + after(other, *far).astype(F32))
-    moved = [rotate(far[shift - 1], "blk", shift) for shift in range(1, n_blk)]
+
+    def input_share(shifts, gate_delta):
+        return call(
+            functools.partial(input_kernel, d, shifts),
+            [jax.ShapeDtypeStruct((tokens, width), BF16 if shift else F32) for shift in shifts],
+            [pltpu.VMEM(((d.shard_blocks if d.paired else d.rows) + 1, tokens, BLOCK), F32)],
+            INPUT_MIB, INPUT_COST, meta, gate_delta, up_delta, *everyone,
+        )
+
+    others = [xor_swap(x, "dp", 1) for x in parts_sent]
+    middle = n_blk // 2
+    far = dict(zip([middle], input_share([middle], gate_delta)))
+    parts_kept = call(
+        functools.partial(partial_kernel, d, kept_back), [part(j) for j in kept_back], [], NEAR_MIB, NEAR_COST,
+        meta, xs, gs, act, after(gate_delta, far[middle]), up_delta,
+    )
+    relayed = [kept + after(other, *parts_kept).astype(F32) for kept, other in zip(parts_kept, others)]
+    rest = [shift for shift in range(1, n_blk) if shift != middle] + [0]
+    far.update(zip(rest, input_share(rest, after(gate_delta, *relayed))))
+    own = far.pop(0)
+    moved = [rotate(piece, "blk", shift) for shift, piece in far.items()]
     part_own, *parts_next = call(
         functools.partial(near_kernel, d),
         [part(0)] + [jax.ShapeDtypeStruct((3 * cap // PIECES, BLOCK, BLOCK), BF16)] * PIECES,
-        [], NEAR_MIB, NEAR_COST, meta, xs, gs, act, after(gate_delta, *relayed), up_delta,
+        [], NEAR_MIB, NEAR_COST, meta, xs, gs, act, after(gate_delta, own), up_delta,
     )
     part_own = part_own + jnp.concatenate([xor_swap(piece, "dp", 1) for piece in parts_next]).astype(F32)
     parts = [part_own, *relayed]

time: 78.5 us -> 75.4 us (0.961)
  the two profiles are of different devices: /device:TPU:8 before, /device:TPU:0 now
where the time goes in v4:
time: 75.4 us; the launch traced here: 75.3 us
  waiting for transfers between devices  37.7 us (50%)
  starting transfers between devices  17.7 us (23%)
  Pallas kernels  13.7 us (18%)
  other arithmetic  4.95 us (7%)
  between operations  0.82 us (1%)
    ppermute x9, waiting for transfers between devices, rotate(): return lax.ppermute(x, axis, [(i, (i + shift) % n) for i in range(n)])  34.4 us
    pallas_call x7, Pallas kernels, call(): pl.pallas_call(kernel, out_shape=outs, in_specs=[pl.BlockSpec(memory_spac...  13.7 us
    ppermute x9, starting transfers between devices, rotate(): return lax.ppermute(x, axis, [(i, (i + shift) % n) for i in range(n)])  9.81 us
    ppermute x11, starting transfers between devices, xor_swap(): lax.ppermute(x, axis, [(i, i ^ bit) for i in range(lax.axis_size(axis))])  7.91 us
    ppermute x11, waiting for transfers between devices, xor_swap(): lax.ppermute(x, axis, [(i, i ^ bit) for i in range(lax.axis_size(axis))])  3.39 us
  transfers between devices with their start and end apart: 20, of which 9 were waited for; matrix products, arithmetic and copies ran while one was open for 4% of the time, Pallas kernels for 15%

profile of v4, /device:TPU:0, one launch (start us, length us, event | category | flops | bytes accessed | tf_op | source)
XLA Modules:
  0.0 75.3 jit_solution(2816449428319037481)
XLA Ops:
  0.6 0.0 copy-start
  0.6 0.0 copy-start.1
  0.7 0.0 copy-start.2
  0.7 0.0 copy-start.3
  0.7 0.0 copy-start.4
  0.7 1.3 %pad_maximum_fusion.refs_4_.refs_5_.refs_3_.refs_0_ = bf16[30,128,128]{2,1,0:T(8,128)(2,1)S(1)} fusion(bf16[10,128,128]{2,1,0:T(8,128)(2,1)} %bitcast.17, bf16[10,128,128]{2,1,0:T(8,128)(2,1)} %bitcast.15, bf16[10,128,128]{2,1,0:T(8,128)(2,1)} %bitcast.13), kind=kLoop, calls=%fused_computation.2 | loop fusion | flops 983040 | bytes 1966080 | tf_op jit(solution)/shard_map/concatenate | solution.py:268
  2.0 0.5 collective-permute-start.4
  2.5 2.6 %collective-permute-start.6 = (bf16[10,128,128]{2,1,0:T(8,128)(2,1)S(1)}, bf16[10,128,128]{2,1,0:T(8,128)(2,1)S(1)}, u32[]{:S(2)}, u32[]{:S(2)}) collective-permute-start(bf16[10,128,128]{2,1,0:T(8,128)(2,1)S(1)} %bitcast.14), channel_id=1, source_target_pairs={{0,2},{1,3},{2,0},{3,1},{4,6},{5,7},{6,4},{7,5},{8,10},{9,11},{10,... | collective-permute-start | bytes 983048 | tf_op jit(solution)/shard_map/ppermute | solution.py:30
  5.1 1.6 %collective-permute-start = (bf16[128,1024]{1,0:T(8,128)(2,1)}, bf16[128,1024]{1,0:T(8,128)(2,1)S(1)}, u32[]{:S(2)}, u32[]{:S(2)}) collective-permute-start(bf16[128,1024]{1,0:T(8,128)(2,1)} %param.8), channel_id=1, source_target_pairs={{0,4},{4,8},{8,12},{12,0},{1,5},{5,9},{9,13},{13,1},{2,6},{6,10},{... | collective-permute-start | bytes 786440 | tf_op jit(solution)/shard_map/ppermute | solution.py:26
  6.7 1.6 %collective-permute-start.3 = (bf16[128,1024]{1,0:T(8,128)(2,1)}, bf16[128,1024]{1,0:T(8,128)(2,1)S(1)}, u32[]{:S(2)}, u32[]{:S(2)}) collective-permute-start(bf16[128,1024]{1,0:T(8,128)(2,1)} %param.9), channel_id=1, source_target_pairs={{0,4},{4,8},{8,12},{12,0},{1,5},{5,9},{9,13},{13,1},{2,6},{6,10},{... | collective-permute-start | bytes 786440 | tf_op jit(solution)/shard_map/ppermute | solution.py:26
  8.3 0.1 reshape.26
  8.4 0.1 reshape.27
  8.4 0.0 copy-done.4
  8.4 0.1 reshape.28
  8.5 0.1 concatenate.9.meta
  8.6 1.1 %pad_maximum_fusion.1.own_ref = bf16[2,128,1024]{2,1,0:T(8,128)(2,1)S(1)} fusion(bf16[1,128,1024]{2,1,0:T(8,128)(2,1)} %bitcast.3, bf16[1,128,1024]{2,1,0:T(8,128)(2,1)} %bitcast.2), kind=kLoop, calls=%fused_computation.9 | loop fusion | flops 262144 | bytes 1048576 | tf_op jit(solution)/shard_map/stack | solution.py:265
  9.7 0.0 copy-done.1
  9.7 0.6 collective-permute-start.7
  10.3 3.4 %collective-permute-done.6.refs_6_.refs_7_.refs_5_.refs_2_ = bf16[10,128,128]{2,1,0:T(8,128)(2,1)S(1)} collective-permute-done((bf16[10,128,128]{2,1,0:T(8,128)(2,1)S(1)}, bf16[10,128,128]{2,1,0:T(8,128)(2,1)S(1)}, u32[]{:S(2)}, u32[]{:S(2)}) %collective-permute-start.6) | collective-permute-done | bytes 327712 | tf_op jit(solution)/shard_map/ppermute | solution.py:30
  13.7 2.0 %collective-permute-start.8 = (bf16[10,128,128]{2,1,0:T(8,128)(2,1)}, bf16[10,128,128]{2,1,0:T(8,128)(2,1)S(1)}, u32[]{:S(2)}, u32[]{:S(2)}) collective-permute-start(bf16[10,128,128]{2,1,0:T(8,128)(2,1)} %bitcast.18), channel_id=1, source_target_pairs={{0,2},{1,3},{2,0},{3,1},{4,6},{5,7},{6,4},{7,5},{8,10},{9,11},{10,... | collective-permute-start | bytes 983048 | tf_op jit(solution)/shard_map/ppermute | solution.py:30
  15.6 0.6 collective-permute-done.refs_0_
  16.3 0.9 %collective-permute-start.1 = (bf16[128,1024]{1,0:T(8,128)(2,1)S(1)}, bf16[128,1024]{1,0:T(8,128)(2,1)S(1)}, u32[]{:S(2)}, u32[]{:S(2)}) collective-permute-start(bf16[128,1024]{1,0:T(8,128)(2,1)S(1)} %collective-permute-done.refs_0_), channel_id=1, source_target_pairs={{0,4},{4,8},{8,12},{12,0},{1,5},{5,9},{9,13},{13,1},{2,6},{6,10},{... | collective-permute-start | bytes 786440 | tf_op jit(solution)/shard_map/ppermute | solution.py:26
  17.2 4.7 %collective-permute-done.3.refs_2_.refs_0_ = bf16[128,1024]{1,0:T(8,128)(2,1)S(1)} collective-permute-done((bf16[128,1024]{1,0:T(8,128)(2,1)}, bf16[128,1024]{1,0:T(8,128)(2,1)S(1)}, u32[]{:S(2)}, u32[]{:S(2)}) %collective-permute-start.3) | collective-permute-done | bytes 262176 | tf_op jit(solution)/shard_map/ppermute | solution.py:26
  21.9 0.0 collective-permute-done.4.refs_5_.refs_6_.refs_4_.refs_1_
  21.9 0.0 collective-permute-start.5
  21.9 0.0 collective-permute-done.7.refs_7_.refs_8_.refs_6_.refs_3_
  21.9 5.6 %collective-permute-done.1.refs_1_ = bf16[128,1024]{1,0:T(8,128)(2,1)S(1)} collective-permute-done((bf16[128,1024]{1,0:T(8,128)(2,1)S(1)}, bf16[128,1024]{1,0:T(8,128)(2,1)S(1)}, u32[]{:S(2)}, u32[]{:S(2)}) %collective-permute-start.1) | collective-permute-done | bytes 262176 | tf_op jit(solution)/shard_map/ppermute | solution.py:26
  27.5 0.0 collective-permute-start.10
  27.5 0.5 collective-permute-start.9
  28.0 0.0 collective-permute-done.8.refs_8_.refs_9_.refs_7_.refs_4_
  28.0 0.0 collective-permute-start.11
  28.0 1.3 %collective-permute-start.2 = (bf16[128,1024]{1,0:T(8,128)(2,1)S(1)}, bf16[128,1024]{1,0:T(8,128)(2,1)S(1)}, u32[]{:S(2)}, u32[]{:S(2)}) collective-permute-start(bf16[128,1024]{1,0:T(8,128)(2,1)S(1)} %collective-permute-done.1.refs_1_), channel_id=1, source_target_pairs={{0,4},{4,8},{8,12},{12,0},{1,5},{5,9},{9,13},{13,1},{2,6},{6,10},{... | collective-permute-start | bytes 786440 | tf_op jit(solution)/shard_map/ppermute | solution.py:26
  29.3 3.1 %collective-permute-done.5.refs_3_.refs_1_ = bf16[128,1024]{1,0:T(8,128)(2,1)S(1)} collective-permute-done((bf16[128,1024]{1,0:T(8,128)(2,1)S(1)}, bf16[128,1024]{1,0:T(8,128)(2,1)S(1)}, u32[]{:S(2)}, u32[]{:S(2)}) %collective-permute-start.5) | collective-permute-done | bytes 262176 | tf_op jit(solution)/shard_map/ppermute | solution.py:26
  32.4 0.0 collective-permute-start.12
  32.4 0.0 collective-permute-done.10.refs_10_.refs_11_.refs_9_.refs_6_
  32.4 0.0 collective-permute-done.9.refs_9_.refs_10_.refs_8_.refs_5_
  32.4 0.0 collective-permute-done.11.refs_11_.refs_12_.refs_10_.refs_7_
  32.4 2.9 %shard_map.111 = (f32[33,128,128]{2,1,0:T(8,128)S(1)}, f32[33,128,128]{2,1,0:T(8,128)S(1)}, f32[33,128,128]{2,1,0:T(8,128)S(1)}) custom-call(s32[122]{0:T(128)S(1)} %concatenate.9.meta, bf16[2,128,1024]{2,1,0:T(8,128)(2,1)S(1)} %pad_maximum_fusion.1.own_ref, bf16[128,1024]{1,0:T(8,128)(2,1)S(1)} %collective-permute-done.refs_0_, ...), custom_call_target="tpu_custom_call" | custom-call | flops 1048576 | bytes 8388608 | tf_op jit(solution)/shard_map/pallas_call | solution.py:247
  35.3 3.6 %collective-permute-done.2.refs_2_ = bf16[128,1024]{1,0:T(8,128)(2,1)S(1)} collective-permute-done((bf16[128,1024]{1,0:T(8,128)(2,1)S(1)}, bf16[128,1024]{1,0:T(8,128)(2,1)S(1)}, u32[]{:S(2)}, u32[]{:S(2)}) %collective-permute-start.2) | collective-permute-done | bytes 262176 | tf_op jit(solution)/shard_map/ppermute | solution.py:26
  38.9 2.3 %shard_map.112 = (f32[32,128,128]{2,1,0:T(8,128)S(1)}, f32[32,128,128]{2,1,0:T(8,128)S(1)}, bf16[32,128,128]{2,1,0:T(8,128)(2,1)S(1)}, bf16[32,128,128]{2,1,0:T(8,128)(2,1)S(1)}) custom-call(s32[122]{0:T(128)S(1)} %concatenate.9.meta, bf16[2,128,1024]{2,1,0:T(8,128)(2,1)S(1)} %pad_maximum_fusion.1.own_ref, ...), custom_call_target="tpu_custom_call" | custom-call | flops 1048576 | bytes 8388608 | tf_op jit(solution)/shard_map/pallas_call | solution.py:247
  41.2 2.9 %collective-permute-done.12.refs_2_ = bf16[128,1024]{1,0:T(8,128)(2,1)S(1)} collective-permute-done((bf16[128,1024]{1,0:T(8,128)(2,1)S(1)}, bf16[128,1024]{1,0:T(8,128)(2,1)S(1)}, u32[]{:S(2)}, u32[]{:S(2)}) %collective-permute-start.12) | collective-permute-done | bytes 262176 | tf_op jit(solution)/shard_map/ppermute | solution.py:26
  44.1 2.1 %shard_map.113 = (bf16[32,128,128]{2,1,0:T(8,128)(2,1)S(1)}, bf16[32,128,128]{2,1,0:T(8,128)(2,1)S(1)}, bf16[32,128,128]{2,1,0:T(8,128)(2,1)S(1)}, bf16[30,128,128]{2,1,0:T(8,128)(2,1)S(1)}) custom-call(s32[122]{0:T(128)S(1)} %concatenate.9.meta, bf16[2,128,1024]{2,1,0:T(8,128)(2,1)S(1)} %pad_maximum_fusion.1.own_ref, ...), custom_call_target="tpu_custom_call" | custom-call | flops 1048576 | bytes 8388608 | tf_op jit(solution)/shard_map/pallas_call | solution.py:247
  46.3 0.1 collective-permute-start.13
  46.4 1.2 %shard_map.114 = bf16[128,1024]{1,0:T(8,128)(2,1)S(1)} custom-call(s32[122]{0:T(128)S(1)} %concatenate.9.meta, bf16[32,128,128]{2,1,0:T(8,128)(2,1)S(1)} %get-tuple-element.54.gate_delta, bf16[32,128,128]{2,1,0:T(8,128)(2,1)S(1)} %get-tuple-element.46.up_delta, bf16[30,128,128]{2,1,0:T(8,128)(2,1)S(1)} %pad_maximum_fusion.refs_4_.refs_5_.refs_3_.refs_0_, ...), custom_call_target="tpu_custom_call" | custom-call | flops 1048576 | bytes 8388608 | tf_op jit(solution)/shard_map/pallas_call | solution.py:247
  47.6 0.5 collective-permute-start.14
  48.1 1.0 %shard_map.115 = f32[30,128,128]{2,1,0:T(8,128)S(1)} custom-call(s32[122]{0:T(128)S(1)} %concatenate.9.meta, bf16[32,128,128]{2,1,0:T(8,128)(2,1)S(1)} %get-tuple-element.39.xs, bf16[32,128,128]{2,1,0:T(8,128)(2,1)S(1)} %get-tuple-element.45.gs, bf16[32,128,128]{2,1,0:T(8,128)(2,1)S(1)} %get-tuple-element.40.act, ...), custom_call_target="tpu_custom_call" | custom-call | flops 1048576 | bytes 8388608 | tf_op jit(solution)/shard_map/pallas_call | solution.py:247
  49.2 0.0 collective-permute-done.13
  49.2 0.3 convert_add_fusion.1
  49.5 1.6 %collective-permute-start.19 = (bf16[30,128,128]{2,1,0:T(8,128)(2,1)S(1)}, bf16[30,128,128]{2,1,0:T(8,128)(2,1)S(1)}, u32[]{:S(2)}, u32[]{:S(2)}) collective-permute-start(bf16[30,128,128]{2,1,0:T(8,128)(2,1)S(1)} %convert_add_fusion.1), channel_id=1, source_target_pairs={{0,2},{1,3},{2,0},{3,1},{4,6},{5,7},{6,4},{7,5},{8,10},{9,11},{10,... | collective-permute-start | bytes 2949128 | tf_op jit(solution)/shard_map/ppermute | solution.py:30
  51.1 2.8 %shard_map.116 = (bf16[128,1024]{1,0:T(8,128)(2,1)S(1)}, bf16[128,1024]{1,0:T(8,128)(2,1)S(1)}, f32[128,1024]{1,0:T(8,128)S(1)}) custom-call(s32[122]{0:T(128)S(1)} %concatenate.9.meta, bf16[32,128,128]{2,1,0:T(8,128)(2,1)S(1)} %get-tuple-element.54.gate_delta, bf16[32,128,128]{2,1,0:T(8,128)(2,1)S(1)} %get-tuple-element.46.up_delta, ...), custom_call_target="tpu_custom_call" | custom-call | flops 1048576 | bytes 8388608 | tf_op jit(solution)/shard_map/pallas_call | solution.py:247
  53.9 1.6 %collective-permute-start.15 = (bf16[128,1024]{1,0:T(8,128)(2,1)S(1)}, bf16[128,1024]{1,0:T(8,128)(2,1)S(1)}, u32[]{:S(2)}, u32[]{:S(2)}) collective-permute-start(bf16[128,1024]{1,0:T(8,128)(2,1)S(1)} %get-tuple-element.52), channel_id=1, source_target_pairs={{0,4},{4,8},{8,12},{12,0},{1,5},{5,9},{9,13},{13,1},{2,6},{6,10},{... | collective-permute-start | bytes 786440 | tf_op jit(solution)/shard_map/ppermute | solution.py:26
  55.5 2.3 %collective-permute-start.16 = (bf16[128,1024]{1,0:T(8,128)(2,1)S(1)}, bf16[128,1024]{1,0:T(8,128)(2,1)S(1)}, u32[]{:S(2)}, u32[]{:S(2)}) collective-permute-start(bf16[128,1024]{1,0:T(8,128)(2,1)S(1)} %get-tuple-element.53), channel_id=1, source_target_pairs={{0,12},{4,0},{8,4},{12,8},{1,13},{5,1},{9,5},{13,9},{2,14},{6,2},{... | collective-permute-start | bytes 786440 | tf_op jit(solution)/shard_map/ppermute | solution.py:26
  57.8 1.3 %shard_map.117 = (f32[30,128,128]{2,1,0:T(8,128)S(1)}, bf16[15,128,128]{2,1,0:T(8,128)(2,1)S(1)}, bf16[15,128,128]{2,1,0:T(8,128)(2,1)S(1)}) custom-call(s32[122]{0:T(128)S(1)} %concatenate.9.meta, bf16[32,128,128]{2,1,0:T(8,128)(2,1)S(1)} %get-tuple-element.39.xs, bf16[32,128,128]{2,1,0:T(8,128)(2,1)S(1)} %get-tuple-element.45.gs, ...), custom_call_target="tpu_custom_call" | custom-call | flops 1048576 | bytes 8388608 | tf_op jit(solution)/shard_map/pallas_call | solution.py:247
  59.1 0.1 collective-permute-start.17
  59.2 8.3 %collective-permute-done.14 = bf16[128,1024]{1,0:T(8,128)(2,1)S(1)} collective-permute-done((bf16[128,1024]{1,0:T(8,128)(2,1)S(1)}, bf16[128,1024]{1,0:T(8,128)(2,1)S(1)}, u32[]{:S(2)}, u32[]{:S(2)}) %collective-permute-start.14) | collective-permute-done | bytes 262176 | tf_op jit(solution)/shard_map/ppermute | solution.py:26
  67.5 0.0 collective-permute-start.18
  67.5 0.0 collective-permute-done.15
  67.5 5.5 %collective-permute-done.16 = bf16[128,1024]{1,0:T(8,128)(2,1)S(1)} collective-permute-done((bf16[128,1024]{1,0:T(8,128)(2,1)S(1)}, bf16[128,1024]{1,0:T(8,128)(2,1)S(1)}, u32[]{:S(2)}, u32[]{:S(2)}) %collective-permute-start.16) | collective-permute-done | bytes 262176 | tf_op jit(solution)/shard_map/ppermute | solution.py:26
  73.0 0.9 %add_convert_fusion = bf16[128,1024]{1,0:T(8,128)(2,1)} fusion(bf16[128,1024]{1,0:T(8,128)(2,1)S(1)} %collective-permute-done.16, bf16[128,1024]{1,0:T(8,128)(2,1)S(1)} %collective-permute-done.15, f32[128,1024]{1,0:T(8,128)S(1)} %get-tuple-element.51, bf16[128,1024]{1,0:T(8,128)(2,1)S(1)} %collective-permute-done.14), kind=kLoop, calls=%fused_computation.10 | loop fusion | flops 917504 | bytes 1572864 | tf_op jit(solution)/shard_map/convert_element_type | solution.py:355
  73.9 0.0 collective-permute-done.17
  73.9 0.0 collective-permute-done.18
  73.9 0.3 convert_add_fusion
  74.2 0.0 collective-permute-done.19
  74.2 1.1 %fusion.5 = (bf16[1,1,10,128,128]{4,3,2,1,0:T(8,128)(2,1)}, bf16[1,1,10,128,128]{4,3,2,1,0:T(8,128)(2,1)}, bf16[1,1,10,128,128]{4,3,2,1,0:T(8,128)(2,1)}) fusion(f32[30,128,128]{2,1,0:T(8,128)S(1)} %convert_add_fusion, bf16[30,128,128]{2,1,0:T(8,128)(2,1)S(1)} %collective-permute-done.19), kind=kLoop, calls=%fused_computation.13 | loop fusion | flops 1474560 | bytes 3932160 | tf_op jit(solution)/shard_map/reshape | solution.py:350
  (3 shorter events, 0.0 us)
Async XLA Ops:
  0.6 1.9 %copy-start = (bf16[1,1,10,128,128]{4,3,2,1,0:T(8,128)(2,1)S(1)}, bf16[1,1,10,128,128]{4,3,2,1,0:T(8,128)(2,1)}, u32[]{:S(2)}) copy-start(bf16[1,1,10,128,128]{4,3,2,1,0:T(8,128)(2,1)} %param.10) | copy-start | bytes 983044
  0.6 9.1 %copy-start.1 = (bf16[1,1,10,128,128]{4,3,2,1,0:T(8,128)(2,1)S(1)}, bf16[1,1,10,128,128]{4,3,2,1,0:T(8,128)(2,1)}, u32[]{:S(2)}) copy-start(bf16[1,1,10,128,128]{4,3,2,1,0:T(8,128)(2,1)} %param.11) | copy-start | bytes 983044
  0.7 7.6 %copy-start.2 = (s32[1,4,10]{2,1,0:T(4,128)S(1)}, s32[1,4,10]{2,1,0:T(4,128)}, u32[]{:S(2)}) copy-start(s32[1,4,10]{2,1,0:T(4,128)} %param.13) | copy-start | bytes 484
  0.7 7.7 %copy-start.3 = (s32[1,4,10]{2,1,0:T(4,128)S(1)}, s32[1,4,10]{2,1,0:T(4,128)}, u32[]{:S(2)}) copy-start(s32[1,4,10]{2,1,0:T(4,128)} %param.14) | copy-start | bytes 484
  0.7 7.8 %copy-start.4 = (s32[1,4,10]{2,1,0:T(4,128)S(1)}, s32[1,4,10]{2,1,0:T(4,128)}, u32[]{:S(2)}) copy-start(s32[1,4,10]{2,1,0:T(4,128)} %param.15) | copy-start | bytes 484
  2.0 19.9 %collective-permute-start.4 = (bf16[30,128,128]{2,1,0:T(8,128)(2,1)S(1)}, bf16[30,128,128]{2,1,0:T(8,128)(2,1)S(1)}, u32[]{:S(2)}, u32[]{:S(2)}) collective-permute-start(bf16[30,128,128]{2,1,0:T(8,128)(2,1)S(1)} %pad_maximum_fusion.refs_4_.refs_5_.refs_3_.refs_0_), channel_id=1, source_target_pairs={{0,1},{1,0},{2,3},{3,2},{4,5},{5,4},{6,7},{7,6},{8,9},{9,8},{10,11... | collective-permute-start | bytes 2949128 | tf_op jit(solution)/shard_map/ppermute | solution.py:30
  2.5 11.1 %collective-permute-start.6 = (bf16[10,128,128]{2,1,0:T(8,128)(2,1)S(1)}, bf16[10,128,128]{2,1,0:T(8,128)(2,1)S(1)}, u32[]{:S(2)}, u32[]{:S(2)}) collective-permute-start(bf16[10,128,128]{2,1,0:T(8,128)(2,1)S(1)} %bitcast.14), channel_id=1, source_target_pairs={{0,2},{1,3},{2,0},{3,1},{4,6},{5,7},{6,4},{7,5},{8,10},{9,11},{10,... | collective-permute-start | bytes 983048 | tf_op jit(solution)/shard_map/ppermute | solution.py:30
  5.1 11.1 %collective-permute-start = (bf16[128,1024]{1,0:T(8,128)(2,1)}, bf16[128,1024]{1,0:T(8,128)(2,1)S(1)}, u32[]{:S(2)}, u32[]{:S(2)}) collective-permute-start(bf16[128,1024]{1,0:T(8,128)(2,1)} %param.8), channel_id=1, source_target_pairs={{0,4},{4,8},{8,12},{12,0},{1,5},{5,9},{9,13},{13,1},{2,6},{6,10},{... | collective-permute-start | bytes 786440 | tf_op jit(solution)/shard_map/ppermute | solution.py:26
  6.7 15.2 %collective-permute-start.3 = (bf16[128,1024]{1,0:T(8,128)(2,1)}, bf16[128,1024]{1,0:T(8,128)(2,1)S(1)}, u32[]{:S(2)}, u32[]{:S(2)}) collective-permute-start(bf16[128,1024]{1,0:T(8,128)(2,1)} %param.9), channel_id=1, source_target_pairs={{0,4},{4,8},{8,12},{12,0},{1,5},{5,9},{9,13},{13,1},{2,6},{6,10},{... | collective-permute-start | bytes 786440 | tf_op jit(solution)/shard_map/ppermute | solution.py:26
  9.7 12.2 %collective-permute-start.7 = (bf16[10,128,128]{2,1,0:T(8,128)(2,1)S(1)}, bf16[10,128,128]{2,1,0:T(8,128)(2,1)S(1)}, u32[]{:S(2)}, u32[]{:S(2)}) collective-permute-start(bf16[10,128,128]{2,1,0:T(8,128)(2,1)S(1)} %bitcast.16), channel_id=1, source_target_pairs={{0,2},{1,3},{2,0},{3,1},{4,6},{5,7},{6,4},{7,5},{8,10},{9,11},{10,... | collective-permute-start | bytes 983048 | tf_op jit(solution)/shard_map/ppermute | solution.py:30
  13.7 14.3 %collective-permute-start.8 = (bf16[10,128,128]{2,1,0:T(8,128)(2,1)}, bf16[10,128,128]{2,1,0:T(8,128)(2,1)S(1)}, u32[]{:S(2)}, u32[]{:S(2)}) collective-permute-start(bf16[10,128,128]{2,1,0:T(8,128)(2,1)} %bitcast.18), channel_id=1, source_target_pairs={{0,2},{1,3},{2,0},{3,1},{4,6},{5,7},{6,4},{7,5},{8,10},{9,11},{10,... | collective-permute-start | bytes 983048 | tf_op jit(solution)/shard_map/ppermute | solution.py:30
  16.3 11.2 %collective-permute-start.1 = (bf16[128,1024]{1,0:T(8,128)(2,1)S(1)}, bf16[128,1024]{1,0:T(8,128)(2,1)S(1)}, u32[]{:S(2)}, u32[]{:S(2)}) collective-permute-start(bf16[128,1024]{1,0:T(8,128)(2,1)S(1)} %collective-permute-done.refs_0_), channel_id=1, source_target_pairs={{0,4},{4,8},{8,12},{12,0},{1,5},{5,9},{9,13},{13,1},{2,6},{6,10},{... | collective-permute-start | bytes 786440 | tf_op jit(solution)/shard_map/ppermute | solution.py:26
  21.9 10.5 %collective-permute-start.5 = (bf16[128,1024]{1,0:T(8,128)(2,1)S(1)}, bf16[128,1024]{1,0:T(8,128)(2,1)S(1)}, u32[]{:S(2)}, u32[]{:S(2)}) collective-permute-start(bf16[128,1024]{1,0:T(8,128)(2,1)S(1)} %collective-permute-done.3.refs_2_.refs_0_), channel_id=1, source_target_pairs={{0,4},{4,8},{8,12},{12,0},{1,5},{5,9},{9,13},{13,1},{2,6},{6,10},{... | collective-permute-start | bytes 786440 | tf_op jit(solution)/shard_map/ppermute | solution.py:26
  27.5 4.9 %collective-permute-start.10 = (bf16[10,128,128]{2,1,0:T(8,128)(2,1)S(1)}, bf16[10,128,128]{2,1,0:T(8,128)(2,1)S(1)}, u32[]{:S(2)}, u32[]{:S(2)}) collective-permute-start(bf16[10,128,128]{2,1,0:T(8,128)(2,1)S(1)} %collective-permute-done.7.refs_7_.refs_8_.refs_6_.refs_3_), channel_id=1, source_target_pairs={{0,1},{1,0},{2,3},{3,2},{4,5},{5,4},{6,7},{7,6},{8,9},{9,8},{10,11... | collective-permute-start | bytes 983048 | tf_op jit(solution)/shard_map/ppermute | solution.py:30
  27.5 4.9 %collective-permute-start.9 = (bf16[10,128,128]{2,1,0:T(8,128)(2,1)S(1)}, bf16[10,128,128]{2,1,0:T(8,128)(2,1)S(1)}, u32[]{:S(2)}, u32[]{:S(2)}) collective-permute-start(bf16[10,128,128]{2,1,0:T(8,128)(2,1)S(1)} %collective-permute-done.6.refs_6_.refs_7_.refs_5_.refs_2_), channel_id=1, source_target_pairs={{0,1},{1,0},{2,3},{3,2},{4,5},{5,4},{6,7},{7,6},{8,9},{9,8},{10,11... | collective-permute-start | bytes 983048 | tf_op jit(solution)/shard_map/ppermute | solution.py:30
  28.0 4.4 %collective-permute-start.11 = (bf16[10,128,128]{2,1,0:T(8,128)(2,1)S(1)}, bf16[10,128,128]{2,1,0:T(8,128)(2,1)S(1)}, u32[]{:S(2)}, u32[]{:S(2)}) collective-permute-start(bf16[10,128,128]{2,1,0:T(8,128)(2,1)S(1)} %collective-permute-done.8.refs_8_.refs_9_.refs_7_.refs_4_), channel_id=1, source_target_pairs={{0,1},{1,0},{2,3},{3,2},{4,5},{5,4},{6,7},{7,6},{8,9},{9,8},{10,11... | collective-permute-start | bytes 983048 | tf_op jit(solution)/shard_map/ppermute | solution.py:30
  28.0 10.9 %collective-permute-start.2 = (bf16[128,1024]{1,0:T(8,128)(2,1)S(1)}, bf16[128,1024]{1,0:T(8,128)(2,1)S(1)}, u32[]{:S(2)}, u32[]{:S(2)}) collective-permute-start(bf16[128,1024]{1,0:T(8,128)(2,1)S(1)} %collective-permute-done.1.refs_1_), channel_id=1, source_target_pairs={{0,4},{4,8},{8,12},{12,0},{1,5},{5,9},{9,13},{13,1},{2,6},{6,10},{... | collective-permute-start | bytes 786440 | tf_op jit(solution)/shard_map/ppermute | solution.py:26
  32.4 11.7 %collective-permute-start.12 = (bf16[128,1024]{1,0:T(8,128)(2,1)S(1)}, bf16[128,1024]{1,0:T(8,128)(2,1)S(1)}, u32[]{:S(2)}, u32[]{:S(2)}) collective-permute-start(bf16[128,1024]{1,0:T(8,128)(2,1)S(1)} %collective-permute-done.5.refs_3_.refs_1_), channel_id=1, source_target_pairs={{0,4},{4,8},{8,12},{12,0},{1,5},{5,9},{9,13},{13,1},{2,6},{6,10},{... | collective-permute-start | bytes 786440 | tf_op jit(solution)/shard_map/ppermute | solution.py:26
  46.3 2.9 %collective-permute-start.13 = (bf16[30,128,128]{2,1,0:T(8,128)(2,1)S(1)}, bf16[30,128,128]{2,1,0:T(8,128)(2,1)S(1)}, u32[]{:S(2)}, u32[]{:S(2)}) collective-permute-start(bf16[30,128,128]{2,1,0:T(8,128)(2,1)S(1)} %get-tuple-element.48), channel_id=1, source_target_pairs={{0,1},{1,0},{2,3},{3,2},{4,5},{5,4},{6,7},{7,6},{8,9},{9,8},{10,11... | collective-permute-start | bytes 2949128 | tf_op jit(solution)/shard_map/ppermute | solution.py:30
  47.6 19.9 %collective-permute-start.14 = (bf16[128,1024]{1,0:T(8,128)(2,1)S(1)}, bf16[128,1024]{1,0:T(8,128)(2,1)S(1)}, u32[]{:S(2)}, u32[]{:S(2)}) collective-permute-start(bf16[128,1024]{1,0:T(8,128)(2,1)S(1)} %shard_map.114), channel_id=1, source_target_pairs={{0,8},{4,12},{8,0},{12,4},{1,9},{5,13},{9,1},{13,5},{2,10},{6,14},... | collective-permute-start | bytes 786440 | tf_op jit(solution)/shard_map/ppermute | solution.py:26
  49.5 24.6 %collective-permute-start.19 = (bf16[30,128,128]{2,1,0:T(8,128)(2,1)S(1)}, bf16[30,128,128]{2,1,0:T(8,128)(2,1)S(1)}, u32[]{:S(2)}, u32[]{:S(2)}) collective-permute-start(bf16[30,128,128]{2,1,0:T(8,128)(2,1)S(1)} %convert_add_fusion.1), channel_id=1, source_target_pairs={{0,2},{1,3},{2,0},{3,1},{4,6},{5,7},{6,4},{7,5},{8,10},{9,11},{10,... | collective-permute-start | bytes 2949128 | tf_op jit(solution)/shard_map/ppermute | solution.py:30
  53.9 13.6 %collective-permute-start.15 = (bf16[128,1024]{1,0:T(8,128)(2,1)S(1)}, bf16[128,1024]{1,0:T(8,128)(2,1)S(1)}, u32[]{:S(2)}, u32[]{:S(2)}) collective-permute-start(bf16[128,1024]{1,0:T(8,128)(2,1)S(1)} %get-tuple-element.52), channel_id=1, source_target_pairs={{0,4},{4,8},{8,12},{12,0},{1,5},{5,9},{9,13},{13,1},{2,6},{6,10},{... | collective-permute-start | bytes 786440 | tf_op jit(solution)/shard_map/ppermute | solution.py:26
  55.5 17.5 %collective-permute-start.16 = (bf16[128,1024]{1,0:T(8,128)(2,1)S(1)}, bf16[128,1024]{1,0:T(8,128)(2,1)S(1)}, u32[]{:S(2)}, u32[]{:S(2)}) collective-permute-start(bf16[128,1024]{1,0:T(8,128)(2,1)S(1)} %get-tuple-element.53), channel_id=1, source_target_pairs={{0,12},{4,0},{8,4},{12,8},{1,13},{5,1},{9,5},{13,9},{2,14},{6,2},{... | collective-permute-start | bytes 786440 | tf_op jit(solution)/shard_map/ppermute | solution.py:26
  59.1 14.8 %collective-permute-start.17 = (bf16[15,128,128]{2,1,0:T(8,128)(2,1)S(1)}, bf16[15,128,128]{2,1,0:T(8,128)(2,1)S(1)}, u32[]{:S(2)}, u32[]{:S(2)}) collective-permute-start(bf16[15,128,128]{2,1,0:T(8,128)(2,1)S(1)} %get-tuple-element.56), channel_id=1, source_target_pairs={{0,1},{1,0},{2,3},{3,2},{4,5},{5,4},{6,7},{7,6},{8,9},{9,8},{10,11... | collective-permute-start | bytes 1474568 | tf_op jit(solution)/shard_map/ppermute | solution.py:30
  67.5 6.4 %collective-permute-start.18 = (bf16[15,128,128]{2,1,0:T(8,128)(2,1)S(1)}, bf16[15,128,128]{2,1,0:T(8,128)(2,1)S(1)}, u32[]{:S(2)}, u32[]{:S(2)}) collective-permute-start(bf16[15,128,128]{2,1,0:T(8,128)(2,1)S(1)} %get-tuple-element.57), channel_id=1, source_target_pairs={{0,1},{1,0},{2,3},{3,2},{4,5},{5,4},{6,7},{7,6},{8,9},{9,8},{10,11... | collective-permute-start | bytes 1474568 | tf_op jit(solution)/shard_map/ppermute | solution.py:30

commit v5 on v4

--- a/solution.py
+++ b/solution.py
@@ -190,7 +190,7 @@
         up_delta[c] = (total * up_slope[c]).astype(BF16)
         return 0
 
-    lax.fori_loop(0, d.cols, deltas, 0, unroll=4)
+    lax.fori_loop(0, d.cols, deltas, 0, unroll=16)
     for j, part_ref in zip(places, part_refs):
         partial_grads(d, j, meta, xs, gs, act, gate_delta, up_delta, part_ref)
 

time: 75.4 us -> 75.4 us (level)
  no operation moved by 1% of the time
where the time goes in v5:
time: 75.4 us; the launch traced here: 75.2 us
  waiting for transfers between devices  37.8 us (50%)
  starting transfers between devices  17.7 us (23%)
  Pallas kernels  13.6 us (18%)
  other arithmetic  4.95 us (7%)
  between operations  0.82 us (1%)
    ppermute x9, waiting for transfers between devices, rotate(): return lax.ppermute(x, axis, [(i, (i + shift) % n) for i in range(n)])  34.4 us
    pallas_call x7, Pallas kernels, call(): pl.pallas_call(kernel, out_shape=outs, in_specs=[pl.BlockSpec(memory_spac...  13.6 us
    ppermute x9, starting transfers between devices, rotate(): return lax.ppermute(x, axis, [(i, (i + shift) % n) for i in range(n)])  9.8 us
    ppermute x11, starting transfers between devices, xor_swap(): lax.ppermute(x, axis, [(i, i ^ bit) for i in range(lax.axis_size(axis))])  7.92 us
    ppermute x11, waiting for transfers between devices, xor_swap(): lax.ppermute(x, axis, [(i, i ^ bit) for i in range(lax.axis_size(axis))])  3.39 us
  transfers between devices with their start and end apart: 20, of which 9 were waited for; matrix products, arithmetic and copies ran while one was open for 4% of the time, Pallas kernels for 15%

profile of v5, /device:TPU:0, one launch (start us, length us, event | category | flops | bytes accessed | tf_op | source)
XLA Modules:
  0.0 75.2 jit_solution(9964841213156349203)
XLA Ops:
  0.6 0.0 copy-start
  0.6 0.0 copy-start.1
  0.7 0.0 copy-start.2
  0.7 0.0 copy-start.3
  0.7 1.3 %pad_maximum_fusion.refs_4_.refs_5_.refs_3_.refs_0_ = bf16[30,128,128]{2,1,0:T(8,128)(2,1)S(1)} fusion(bf16[10,128,128]{2,1,0:T(8,128)(2,1)} %bitcast.17, bf16[10,128,128]{2,1,0:T(8,128)(2,1)} %bitcast.15, bf16[10,128,128]{2,1,0:T(8,128)(2,1)} %bitcast.13), kind=kLoop, calls=%fused_computation.2 | loop fusion | flops 983040 | bytes 1966080 | tf_op jit(solution)/shard_map/concatenate | solution.py:268
  2.0 0.5 collective-permute-start.4
  2.5 0.0 copy-done
  2.5 2.6 %collective-permute-start.6 = (bf16[10,128,128]{2,1,0:T(8,128)(2,1)S(1)}, bf16[10,128,128]{2,1,0:T(8,128)(2,1)S(1)}, u32[]{:S(2)}, u32[]{:S(2)}) collective-permute-start(bf16[10,128,128]{2,1,0:T(8,128)(2,1)S(1)} %bitcast.14), channel_id=1, source_target_pairs={{0,2},{1,3},{2,0},{3,1},{4,6},{5,7},{6,4},{7,5},{8,10},{9,11},{10,... | collective-permute-start | bytes 983048 | tf_op jit(solution)/shard_map/ppermute | solution.py:30
  5.1 1.6 %collective-permute-start = (bf16[128,1024]{1,0:T(8,128)(2,1)}, bf16[128,1024]{1,0:T(8,128)(2,1)S(1)}, u32[]{:S(2)}, u32[]{:S(2)}) collective-permute-start(bf16[128,1024]{1,0:T(8,128)(2,1)} %param.8), channel_id=1, source_target_pairs={{0,4},{4,8},{8,12},{12,0},{1,5},{5,9},{9,13},{13,1},{2,6},{6,10},{... | collective-permute-start | bytes 786440 | tf_op jit(solution)/shard_map/ppermute | solution.py:26
  6.7 1.6 %collective-permute-start.3 = (bf16[128,1024]{1,0:T(8,128)(2,1)}, bf16[128,1024]{1,0:T(8,128)(2,1)S(1)}, u32[]{:S(2)}, u32[]{:S(2)}) collective-permute-start(bf16[128,1024]{1,0:T(8,128)(2,1)} %param.9), channel_id=1, source_target_pairs={{0,4},{4,8},{8,12},{12,0},{1,5},{5,9},{9,13},{13,1},{2,6},{6,10},{... | collective-permute-start | bytes 786440 | tf_op jit(solution)/shard_map/ppermute | solution.py:26
  8.3 0.0 copy-done.2
  8.3 0.1 reshape.26
  8.4 0.0 copy-done.3
  8.4 0.1 reshape.27
  8.4 0.1 reshape.28
  8.5 0.1 concatenate.9.meta
  8.6 1.1 %pad_maximum_fusion.1.own_ref = bf16[2,128,1024]{2,1,0:T(8,128)(2,1)S(1)} fusion(bf16[1,128,1024]{2,1,0:T(8,128)(2,1)} %bitcast.3, bf16[1,128,1024]{2,1,0:T(8,128)(2,1)} %bitcast.2), kind=kLoop, calls=%fused_computation.9 | loop fusion | flops 262144 | bytes 1048576 | tf_op jit(solution)/shard_map/stack | solution.py:265
  9.7 0.6 collective-permute-start.7
  10.3 3.4 %collective-permute-done.6.refs_6_.refs_7_.refs_5_.refs_2_ = bf16[10,128,128]{2,1,0:T(8,128)(2,1)S(1)} collective-permute-done((bf16[10,128,128]{2,1,0:T(8,128)(2,1)S(1)}, bf16[10,128,128]{2,1,0:T(8,128)(2,1)S(1)}, u32[]{:S(2)}, u32[]{:S(2)}) %collective-permute-start.6) | collective-permute-done | bytes 327712 | tf_op jit(solution)/shard_map/ppermute | solution.py:30
  13.7 2.0 %collective-permute-start.8 = (bf16[10,128,128]{2,1,0:T(8,128)(2,1)}, bf16[10,128,128]{2,1,0:T(8,128)(2,1)S(1)}, u32[]{:S(2)}, u32[]{:S(2)}) collective-permute-start(bf16[10,128,128]{2,1,0:T(8,128)(2,1)} %bitcast.18), channel_id=1, source_target_pairs={{0,2},{1,3},{2,0},{3,1},{4,6},{5,7},{6,4},{7,5},{8,10},{9,11},{10,... | collective-permute-start | bytes 983048 | tf_op jit(solution)/shard_map/ppermute | solution.py:30
  15.6 0.6 collective-permute-done.refs_0_
  16.3 0.9 %collective-permute-start.1 = (bf16[128,1024]{1,0:T(8,128)(2,1)S(1)}, bf16[128,1024]{1,0:T(8,128)(2,1)S(1)}, u32[]{:S(2)}, u32[]{:S(2)}) collective-permute-start(bf16[128,1024]{1,0:T(8,128)(2,1)S(1)} %collective-permute-done.refs_0_), channel_id=1, source_target_pairs={{0,4},{4,8},{8,12},{12,0},{1,5},{5,9},{9,13},{13,1},{2,6},{6,10},{... | collective-permute-start | bytes 786440 | tf_op jit(solution)/shard_map/ppermute | solution.py:26
  17.2 4.7 %collective-permute-done.3.refs_2_.refs_0_ = bf16[128,1024]{1,0:T(8,128)(2,1)S(1)} collective-permute-done((bf16[128,1024]{1,0:T(8,128)(2,1)}, bf16[128,1024]{1,0:T(8,128)(2,1)S(1)}, u32[]{:S(2)}, u32[]{:S(2)}) %collective-permute-start.3) | collective-permute-done | bytes 262176 | tf_op jit(solution)/shard_map/ppermute | solution.py:26
  21.9 0.0 collective-permute-done.4.refs_5_.refs_6_.refs_4_.refs_1_
  21.9 0.0 collective-permute-start.5
  21.9 0.0 collective-permute-done.7.refs_7_.refs_8_.refs_6_.refs_3_
  21.9 5.6 %collective-permute-done.1.refs_1_ = bf16[128,1024]{1,0:T(8,128)(2,1)S(1)} collective-permute-done((bf16[128,1024]{1,0:T(8,128)(2,1)S(1)}, bf16[128,1024]{1,0:T(8,128)(2,1)S(1)}, u32[]{:S(2)}, u32[]{:S(2)}) %collective-permute-start.1) | collective-permute-done | bytes 262176 | tf_op jit(solution)/shard_map/ppermute | solution.py:26
  27.5 0.0 collective-permute-start.10
  27.5 0.5 collective-permute-start.9
  28.0 0.0 collective-permute-done.8.refs_8_.refs_9_.refs_7_.refs_4_
  28.0 0.0 collective-permute-start.11
  28.0 1.3 %collective-permute-start.2 = (bf16[128,1024]{1,0:T(8,128)(2,1)S(1)}, bf16[128,1024]{1,0:T(8,128)(2,1)S(1)}, u32[]{:S(2)}, u32[]{:S(2)}) collective-permute-start(bf16[128,1024]{1,0:T(8,128)(2,1)S(1)} %collective-permute-done.1.refs_1_), channel_id=1, source_target_pairs={{0,4},{4,8},{8,12},{12,0},{1,5},{5,9},{9,13},{13,1},{2,6},{6,10},{... | collective-permute-start | bytes 786440 | tf_op jit(solution)/shard_map/ppermute | solution.py:26
  29.3 3.1 %collective-permute-done.5.refs_3_.refs_1_ = bf16[128,1024]{1,0:T(8,128)(2,1)S(1)} collective-permute-done((bf16[128,1024]{1,0:T(8,128)(2,1)S(1)}, bf16[128,1024]{1,0:T(8,128)(2,1)S(1)}, u32[]{:S(2)}, u32[]{:S(2)}) %collective-permute-start.5) | collective-permute-done | bytes 262176 | tf_op jit(solution)/shard_map/ppermute | solution.py:26
  32.4 0.0 collective-permute-start.12
  32.4 0.0 collective-permute-done.10.refs_10_.refs_11_.refs_9_.refs_6_
  32.4 0.0 collective-permute-done.9.refs_9_.refs_10_.refs_8_.refs_5_
  32.4 0.0 collective-permute-done.11.refs_11_.refs_12_.refs_10_.refs_7_
  32.4 2.9 %shard_map.111 = (f32[33,128,128]{2,1,0:T(8,128)S(1)}, f32[33,128,128]{2,1,0:T(8,128)S(1)}, f32[33,128,128]{2,1,0:T(8,128)S(1)}) custom-call(s32[122]{0:T(128)S(1)} %concatenate.9.meta, bf16[2,128,1024]{2,1,0:T(8,128)(2,1)S(1)} %pad_maximum_fusion.1.own_ref, bf16[128,1024]{1,0:T(8,128)(2,1)S(1)} %collective-permute-done.refs_0_, ...), custom_call_target="tpu_custom_call" | custom-call | flops 1048576 | bytes 8388608 | tf_op jit(solution)/shard_map/pallas_call | solution.py:247
  35.3 3.6 %collective-permute-done.2.refs_2_ = bf16[128,1024]{1,0:T(8,128)(2,1)S(1)} collective-permute-done((bf16[128,1024]{1,0:T(8,128)(2,1)S(1)}, bf16[128,1024]{1,0:T(8,128)(2,1)S(1)}, u32[]{:S(2)}, u32[]{:S(2)}) %collective-permute-start.2) | collective-permute-done | bytes 262176 | tf_op jit(solution)/shard_map/ppermute | solution.py:26
  38.9 2.3 %shard_map.112 = (f32[32,128,128]{2,1,0:T(8,128)S(1)}, f32[32,128,128]{2,1,0:T(8,128)S(1)}, bf16[32,128,128]{2,1,0:T(8,128)(2,1)S(1)}, bf16[32,128,128]{2,1,0:T(8,128)(2,1)S(1)}) custom-call(s32[122]{0:T(128)S(1)} %concatenate.9.meta, bf16[2,128,1024]{2,1,0:T(8,128)(2,1)S(1)} %pad_maximum_fusion.1.own_ref, ...), custom_call_target="tpu_custom_call" | custom-call | flops 1048576 | bytes 8388608 | tf_op jit(solution)/shard_map/pallas_call | solution.py:247
  41.2 2.9 %collective-permute-done.12.refs_2_ = bf16[128,1024]{1,0:T(8,128)(2,1)S(1)} collective-permute-done((bf16[128,1024]{1,0:T(8,128)(2,1)S(1)}, bf16[128,1024]{1,0:T(8,128)(2,1)S(1)}, u32[]{:S(2)}, u32[]{:S(2)}) %collective-permute-start.12) | collective-permute-done | bytes 262176 | tf_op jit(solution)/shard_map/ppermute | solution.py:26
  44.1 2.1 %shard_map.113 = (bf16[32,128,128]{2,1,0:T(8,128)(2,1)S(1)}, bf16[32,128,128]{2,1,0:T(8,128)(2,1)S(1)}, bf16[32,128,128]{2,1,0:T(8,128)(2,1)S(1)}, bf16[30,128,128]{2,1,0:T(8,128)(2,1)S(1)}) custom-call(s32[122]{0:T(128)S(1)} %concatenate.9.meta, bf16[2,128,1024]{2,1,0:T(8,128)(2,1)S(1)} %pad_maximum_fusion.1.own_ref, ...), custom_call_target="tpu_custom_call" | custom-call | flops 1048576 | bytes 8388608 | tf_op jit(solution)/shard_map/pallas_call | solution.py:247
  46.3 0.1 collective-permute-start.13
  46.3 1.2 %shard_map.114 = bf16[128,1024]{1,0:T(8,128)(2,1)S(1)} custom-call(s32[122]{0:T(128)S(1)} %concatenate.9.meta, bf16[32,128,128]{2,1,0:T(8,128)(2,1)S(1)} %get-tuple-element.54.gate_delta, bf16[32,128,128]{2,1,0:T(8,128)(2,1)S(1)} %get-tuple-element.46.up_delta, bf16[30,128,128]{2,1,0:T(8,128)(2,1)S(1)} %pad_maximum_fusion.refs_4_.refs_5_.refs_3_.refs_0_, ...), custom_call_target="tpu_custom_call" | custom-call | flops 1048576 | bytes 8388608 | tf_op jit(solution)/shard_map/pallas_call | solution.py:247
  47.6 0.5 collective-permute-start.14
  48.1 1.0 %shard_map.115 = f32[30,128,128]{2,1,0:T(8,128)S(1)} custom-call(s32[122]{0:T(128)S(1)} %concatenate.9.meta, bf16[32,128,128]{2,1,0:T(8,128)(2,1)S(1)} %get-tuple-element.39.xs, bf16[32,128,128]{2,1,0:T(8,128)(2,1)S(1)} %get-tuple-element.45.gs, bf16[32,128,128]{2,1,0:T(8,128)(2,1)S(1)} %get-tuple-element.40.act, ...), custom_call_target="tpu_custom_call" | custom-call | flops 1048576 | bytes 8388608 | tf_op jit(solution)/shard_map/pallas_call | solution.py:247
  49.1 0.0 collective-permute-done.13
  49.1 0.3 convert_add_fusion.1
  49.5 1.6 %collective-permute-start.19 = (bf16[30,128,128]{2,1,0:T(8,128)(2,1)S(1)}, bf16[30,128,128]{2,1,0:T(8,128)(2,1)S(1)}, u32[]{:S(2)}, u32[]{:S(2)}) collective-permute-start(bf16[30,128,128]{2,1,0:T(8,128)(2,1)S(1)} %convert_add_fusion.1), channel_id=1, source_target_pairs={{0,2},{1,3},{2,0},{3,1},{4,6},{5,7},{6,4},{7,5},{8,10},{9,11},{10,... | collective-permute-start | bytes 2949128 | tf_op jit(solution)/shard_map/ppermute | solution.py:30
  51.1 2.8 %shard_map.116 = (bf16[128,1024]{1,0:T(8,128)(2,1)S(1)}, bf16[128,1024]{1,0:T(8,128)(2,1)S(1)}, f32[128,1024]{1,0:T(8,128)S(1)}) custom-call(s32[122]{0:T(128)S(1)} %concatenate.9.meta, bf16[32,128,128]{2,1,0:T(8,128)(2,1)S(1)} %get-tuple-element.54.gate_delta, bf16[32,128,128]{2,1,0:T(8,128)(2,1)S(1)} %get-tuple-element.46.up_delta, ...), custom_call_target="tpu_custom_call" | custom-call | flops 1048576 | bytes 8388608 | tf_op jit(solution)/shard_map/pallas_call | solution.py:247
  53.9 1.6 %collective-permute-start.15 = (bf16[128,1024]{1,0:T(8,128)(2,1)S(1)}, bf16[128,1024]{1,0:T(8,128)(2,1)S(1)}, u32[]{:S(2)}, u32[]{:S(2)}) collective-permute-start(bf16[128,1024]{1,0:T(8,128)(2,1)S(1)} %get-tuple-element.52), channel_id=1, source_target_pairs={{0,4},{4,8},{8,12},{12,0},{1,5},{5,9},{9,13},{13,1},{2,6},{6,10},{... | collective-permute-start | bytes 786440 | tf_op jit(solution)/shard_map/ppermute | solution.py:26
  55.5 2.3 %collective-permute-start.16 = (bf16[128,1024]{1,0:T(8,128)(2,1)S(1)}, bf16[128,1024]{1,0:T(8,128)(2,1)S(1)}, u32[]{:S(2)}, u32[]{:S(2)}) collective-permute-start(bf16[128,1024]{1,0:T(8,128)(2,1)S(1)} %get-tuple-element.53), channel_id=1, source_target_pairs={{0,12},{4,0},{8,4},{12,8},{1,13},{5,1},{9,5},{13,9},{2,14},{6,2},{... | collective-permute-start | bytes 786440 | tf_op jit(solution)/shard_map/ppermute | solution.py:26
  57.7 1.3 %shard_map.117 = (f32[30,128,128]{2,1,0:T(8,128)S(1)}, bf16[15,128,128]{2,1,0:T(8,128)(2,1)S(1)}, bf16[15,128,128]{2,1,0:T(8,128)(2,1)S(1)}) custom-call(s32[122]{0:T(128)S(1)} %concatenate.9.meta, bf16[32,128,128]{2,1,0:T(8,128)(2,1)S(1)} %get-tuple-element.39.xs, bf16[32,128,128]{2,1,0:T(8,128)(2,1)S(1)} %get-tuple-element.45.gs, ...), custom_call_target="tpu_custom_call" | custom-call | flops 1048576 | bytes 8388608 | tf_op jit(solution)/shard_map/pallas_call | solution.py:247
  59.1 0.1 collective-permute-start.17
  59.2 8.3 %collective-permute-done.14 = bf16[128,1024]{1,0:T(8,128)(2,1)S(1)} collective-permute-done((bf16[128,1024]{1,0:T(8,128)(2,1)S(1)}, bf16[128,1024]{1,0:T(8,128)(2,1)S(1)}, u32[]{:S(2)}, u32[]{:S(2)}) %collective-permute-start.14) | collective-permute-done | bytes 262176 | tf_op jit(solution)/shard_map/ppermute | solution.py:26
  67.5 0.0 collective-permute-start.18
  67.5 0.0 collective-permute-done.15
  67.5 5.5 %collective-permute-done.16 = bf16[128,1024]{1,0:T(8,128)(2,1)S(1)} collective-permute-done((bf16[128,1024]{1,0:T(8,128)(2,1)S(1)}, bf16[128,1024]{1,0:T(8,128)(2,1)S(1)}, u32[]{:S(2)}, u32[]{:S(2)}) %collective-permute-start.16) | collective-permute-done | bytes 262176 | tf_op jit(solution)/shard_map/ppermute | solution.py:26
  73.0 0.9 %add_convert_fusion = bf16[128,1024]{1,0:T(8,128)(2,1)} fusion(bf16[128,1024]{1,0:T(8,128)(2,1)S(1)} %collective-permute-done.16, bf16[128,1024]{1,0:T(8,128)(2,1)S(1)} %collective-permute-done.15, f32[128,1024]{1,0:T(8,128)S(1)} %get-tuple-element.51, bf16[128,1024]{1,0:T(8,128)(2,1)S(1)} %collective-permute-done.14), kind=kLoop, calls=%fused_computation.10 | loop fusion | flops 917504 | bytes 1572864 | tf_op jit(solution)/shard_map/convert_element_type | solution.py:355
  73.9 0.0 collective-permute-done.17
  73.9 0.0 collective-permute-done.18
  73.9 0.3 convert_add_fusion
  74.1 0.0 collective-permute-done.19
  74.1 1.1 %fusion.5 = (bf16[1,1,10,128,128]{4,3,2,1,0:T(8,128)(2,1)}, bf16[1,1,10,128,128]{4,3,2,1,0:T(8,128)(2,1)}, bf16[1,1,10,128,128]{4,3,2,1,0:T(8,128)(2,1)}) fusion(f32[30,128,128]{2,1,0:T(8,128)S(1)} %convert_add_fusion, bf16[30,128,128]{2,1,0:T(8,128)(2,1)S(1)} %collective-permute-done.19), kind=kLoop, calls=%fused_computation.13 | loop fusion | flops 1474560 | bytes 3932160 | tf_op jit(solution)/shard_map/reshape | solution.py:350
  (3 shorter events, 0.0 us)
Async XLA Ops:
  0.6 1.9 %copy-start = (bf16[1,1,10,128,128]{4,3,2,1,0:T(8,128)(2,1)S(1)}, bf16[1,1,10,128,128]{4,3,2,1,0:T(8,128)(2,1)}, u32[]{:S(2)}) copy-start(bf16[1,1,10,128,128]{4,3,2,1,0:T(8,128)(2,1)} %param.10) | copy-start | bytes 983044
  0.6 9.1 %copy-start.1 = (bf16[1,1,10,128,128]{4,3,2,1,0:T(8,128)(2,1)S(1)}, bf16[1,1,10,128,128]{4,3,2,1,0:T(8,128)(2,1)}, u32[]{:S(2)}) copy-start(bf16[1,1,10,128,128]{4,3,2,1,0:T(8,128)(2,1)} %param.11) | copy-start | bytes 983044
  0.7 7.6 %copy-start.2 = (s32[1,4,10]{2,1,0:T(4,128)S(1)}, s32[1,4,10]{2,1,0:T(4,128)}, u32[]{:S(2)}) copy-start(s32[1,4,10]{2,1,0:T(4,128)} %param.13) | copy-start | bytes 484
  0.7 7.7 %copy-start.3 = (s32[1,4,10]{2,1,0:T(4,128)S(1)}, s32[1,4,10]{2,1,0:T(4,128)}, u32[]{:S(2)}) copy-start(s32[1,4,10]{2,1,0:T(4,128)} %param.14) | copy-start | bytes 484
  0.7 7.8 %copy-start.4 = (s32[1,4,10]{2,1,0:T(4,128)S(1)}, s32[1,4,10]{2,1,0:T(4,128)}, u32[]{:S(2)}) copy-start(s32[1,4,10]{2,1,0:T(4,128)} %param.15) | copy-start | bytes 484
  2.0 19.9 %collective-permute-start.4 = (bf16[30,128,128]{2,1,0:T(8,128)(2,1)S(1)}, bf16[30,128,128]{2,1,0:T(8,128)(2,1)S(1)}, u32[]{:S(2)}, u32[]{:S(2)}) collective-permute-start(bf16[30,128,128]{2,1,0:T(8,128)(2,1)S(1)} %pad_maximum_fusion.refs_4_.refs_5_.refs_3_.refs_0_), channel_id=1, source_target_pairs={{0,1},{1,0},{2,3},{3,2},{4,5},{5,4},{6,7},{7,6},{8,9},{9,8},{10,11... | collective-permute-start | bytes 2949128 | tf_op jit(solution)/shard_map/ppermute | solution.py:30
  2.5 11.1 %collective-permute-start.6 = (bf16[10,128,128]{2,1,0:T(8,128)(2,1)S(1)}, bf16[10,128,128]{2,1,0:T(8,128)(2,1)S(1)}, u32[]{:S(2)}, u32[]{:S(2)}) collective-permute-start(bf16[10,128,128]{2,1,0:T(8,128)(2,1)S(1)} %bitcast.14), channel_id=1, source_target_pairs={{0,2},{1,3},{2,0},{3,1},{4,6},{5,7},{6,4},{7,5},{8,10},{9,11},{10,... | collective-permute-start | bytes 983048 | tf_op jit(solution)/shard_map/ppermute | solution.py:30
  5.1 11.1 %collective-permute-start = (bf16[128,1024]{1,0:T(8,128)(2,1)}, bf16[128,1024]{1,0:T(8,128)(2,1)S(1)}, u32[]{:S(2)}, u32[]{:S(2)}) collective-permute-start(bf16[128,1024]{1,0:T(8,128)(2,1)} %param.8), channel_id=1, source_target_pairs={{0,4},{4,8},{8,12},{12,0},{1,5},{5,9},{9,13},{13,1},{2,6},{6,10},{... | collective-permute-start | bytes 786440 | tf_op jit(solution)/shard_map/ppermute | solution.py:26
  6.7 15.2 %collective-permute-start.3 = (bf16[128,1024]{1,0:T(8,128)(2,1)}, bf16[128,1024]{1,0:T(8,128)(2,1)S(1)}, u32[]{:S(2)}, u32[]{:S(2)}) collective-permute-start(bf16[128,1024]{1,0:T(8,128)(2,1)} %param.9), channel_id=1, source_target_pairs={{0,4},{4,8},{8,12},{12,0},{1,5},{5,9},{9,13},{13,1},{2,6},{6,10},{... | collective-permute-start | bytes 786440 | tf_op jit(solution)/shard_map/ppermute | solution.py:26
  9.7 12.2 %collective-permute-start.7 = (bf16[10,128,128]{2,1,0:T(8,128)(2,1)S(1)}, bf16[10,128,128]{2,1,0:T(8,128)(2,1)S(1)}, u32[]{:S(2)}, u32[]{:S(2)}) collective-permute-start(bf16[10,128,128]{2,1,0:T(8,128)(2,1)S(1)} %bitcast.16), channel_id=1, source_target_pairs={{0,2},{1,3},{2,0},{3,1},{4,6},{5,7},{6,4},{7,5},{8,10},{9,11},{10,... | collective-permute-start | bytes 983048 | tf_op jit(solution)/shard_map/ppermute | solution.py:30
  13.7 14.3 %collective-permute-start.8 = (bf16[10,128,128]{2,1,0:T(8,128)(2,1)}, bf16[10,128,128]{2,1,0:T(8,128)(2,1)S(1)}, u32[]{:S(2)}, u32[]{:S(2)}) collective-permute-start(bf16[10,128,128]{2,1,0:T(8,128)(2,1)} %bitcast.18), channel_id=1, source_target_pairs={{0,2},{1,3},{2,0},{3,1},{4,6},{5,7},{6,4},{7,5},{8,10},{9,11},{10,... | collective-permute-start | bytes 983048 | tf_op jit(solution)/shard_map/ppermute | solution.py:30
  16.3 11.2 %collective-permute-start.1 = (bf16[128,1024]{1,0:T(8,128)(2,1)S(1)}, bf16[128,1024]{1,0:T(8,128)(2,1)S(1)}, u32[]{:S(2)}, u32[]{:S(2)}) collective-permute-start(bf16[128,1024]{1,0:T(8,128)(2,1)S(1)} %collective-permute-done.refs_0_), channel_id=1, source_target_pairs={{0,4},{4,8},{8,12},{12,0},{1,5},{5,9},{9,13},{13,1},{2,6},{6,10},{... | collective-permute-start | bytes 786440 | tf_op jit(solution)/shard_map/ppermute | solution.py:26
  21.9 10.5 %collective-permute-start.5 = (bf16[128,1024]{1,0:T(8,128)(2,1)S(1)}, bf16[128,1024]{1,0:T(8,128)(2,1)S(1)}, u32[]{:S(2)}, u32[]{:S(2)}) collective-permute-start(bf16[128,1024]{1,0:T(8,128)(2,1)S(1)} %collective-permute-done.3.refs_2_.refs_0_), channel_id=1, source_target_pairs={{0,4},{4,8},{8,12},{12,0},{1,5},{5,9},{9,13},{13,1},{2,6},{6,10},{... | collective-permute-start | bytes 786440 | tf_op jit(solution)/shard_map/ppermute | solution.py:26
  27.5 4.9 %collective-permute-start.10 = (bf16[10,128,128]{2,1,0:T(8,128)(2,1)S(1)}, bf16[10,128,128]{2,1,0:T(8,128)(2,1)S(1)}, u32[]{:S(2)}, u32[]{:S(2)}) collective-permute-start(bf16[10,128,128]{2,1,0:T(8,128)(2,1)S(1)} %collective-permute-done.7.refs_7_.refs_8_.refs_6_.refs_3_), channel_id=1, source_target_pairs={{0,1},{1,0},{2,3},{3,2},{4,5},{5,4},{6,7},{7,6},{8,9},{9,8},{10,11... | collective-permute-start | bytes 983048 | tf_op jit(solution)/shard_map/ppermute | solution.py:30
  27.5 4.9 %collective-permute-start.9 = (bf16[10,128,128]{2,1,0:T(8,128)(2,1)S(1)}, bf16[10,128,128]{2,1,0:T(8,128)(2,1)S(1)}, u32[]{:S(2)}, u32[]{:S(2)}) collective-permute-start(bf16[10,128,128]{2,1,0:T(8,128)(2,1)S(1)} %collective-permute-done.6.refs_6_.refs_7_.refs_5_.refs_2_), channel_id=1, source_target_pairs={{0,1},{1,0},{2,3},{3,2},{4,5},{5,4},{6,7},{7,6},{8,9},{9,8},{10,11... | collective-permute-start | bytes 983048 | tf_op jit(solution)/shard_map/ppermute | solution.py:30
  28.0 4.4 %collective-permute-start.11 = (bf16[10,128,128]{2,1,0:T(8,128)(2,1)S(1)}, bf16[10,128,128]{2,1,0:T(8,128)(2,1)S(1)}, u32[]{:S(2)}, u32[]{:S(2)}) collective-permute-start(bf16[10,128,128]{2,1,0:T(8,128)(2,1)S(1)} %collective-permute-done.8.refs_8_.refs_9_.refs_7_.refs_4_), channel_id=1, source_target_pairs={{0,1},{1,0},{2,3},{3,2},{4,5},{5,4},{6,7},{7,6},{8,9},{9,8},{10,11... | collective-permute-start | bytes 983048 | tf_op jit(solution)/shard_map/ppermute | solution.py:30
  28.0 10.9 %collective-permute-start.2 = (bf16[128,1024]{1,0:T(8,128)(2,1)S(1)}, bf16[128,1024]{1,0:T(8,128)(2,1)S(1)}, u32[]{:S(2)}, u32[]{:S(2)}) collective-permute-start(bf16[128,1024]{1,0:T(8,128)(2,1)S(1)} %collective-permute-done.1.refs_1_), channel_id=1, source_target_pairs={{0,4},{4,8},{8,12},{12,0},{1,5},{5,9},{9,13},{13,1},{2,6},{6,10},{... | collective-permute-start | bytes 786440 | tf_op jit(solution)/shard_map/ppermute | solution.py:26
  32.4 11.7 %collective-permute-start.12 = (bf16[128,1024]{1,0:T(8,128)(2,1)S(1)}, bf16[128,1024]{1,0:T(8,128)(2,1)S(1)}, u32[]{:S(2)}, u32[]{:S(2)}) collective-permute-start(bf16[128,1024]{1,0:T(8,128)(2,1)S(1)} %collective-permute-done.5.refs_3_.refs_1_), channel_id=1, source_target_pairs={{0,4},{4,8},{8,12},{12,0},{1,5},{5,9},{9,13},{13,1},{2,6},{6,10},{... | collective-permute-start | bytes 786440 | tf_op jit(solution)/shard_map/ppermute | solution.py:26
  46.3 2.9 %collective-permute-start.13 = (bf16[30,128,128]{2,1,0:T(8,128)(2,1)S(1)}, bf16[30,128,128]{2,1,0:T(8,128)(2,1)S(1)}, u32[]{:S(2)}, u32[]{:S(2)}) collective-permute-start(bf16[30,128,128]{2,1,0:T(8,128)(2,1)S(1)} %get-tuple-element.48), channel_id=1, source_target_pairs={{0,1},{1,0},{2,3},{3,2},{4,5},{5,4},{6,7},{7,6},{8,9},{9,8},{10,11... | collective-permute-start | bytes 2949128 | tf_op jit(solution)/shard_map/ppermute | solution.py:30
  47.6 19.9 %collective-permute-start.14 = (bf16[128,1024]{1,0:T(8,128)(2,1)S(1)}, bf16[128,1024]{1,0:T(8,128)(2,1)S(1)}, u32[]{:S(2)}, u32[]{:S(2)}) collective-permute-start(bf16[128,1024]{1,0:T(8,128)(2,1)S(1)} %shard_map.114), channel_id=1, source_target_pairs={{0,8},{4,12},{8,0},{12,4},{1,9},{5,13},{9,1},{13,5},{2,10},{6,14},... | collective-permute-start | bytes 786440 | tf_op jit(solution)/shard_map/ppermute | solution.py:26
  49.5 24.7 %collective-permute-start.19 = (bf16[30,128,128]{2,1,0:T(8,128)(2,1)S(1)}, bf16[30,128,128]{2,1,0:T(8,128)(2,1)S(1)}, u32[]{:S(2)}, u32[]{:S(2)}) collective-permute-start(bf16[30,128,128]{2,1,0:T(8,128)(2,1)S(1)} %convert_add_fusion.1), channel_id=1, source_target_pairs={{0,2},{1,3},{2,0},{3,1},{4,6},{5,7},{6,4},{7,5},{8,10},{9,11},{10,... | collective-permute-start | bytes 2949128 | tf_op jit(solution)/shard_map/ppermute | solution.py:30
  53.9 13.7 %collective-permute-start.15 = (bf16[128,1024]{1,0:T(8,128)(2,1)S(1)}, bf16[128,1024]{1,0:T(8,128)(2,1)S(1)}, u32[]{:S(2)}, u32[]{:S(2)}) collective-permute-start(bf16[128,1024]{1,0:T(8,128)(2,1)S(1)} %get-tuple-element.52), channel_id=1, source_target_pairs={{0,4},{4,8},{8,12},{12,0},{1,5},{5,9},{9,13},{13,1},{2,6},{6,10},{... | collective-permute-start | bytes 786440 | tf_op jit(solution)/shard_map/ppermute | solution.py:26
  55.5 17.6 %collective-permute-start.16 = (bf16[128,1024]{1,0:T(8,128)(2,1)S(1)}, bf16[128,1024]{1,0:T(8,128)(2,1)S(1)}, u32[]{:S(2)}, u32[]{:S(2)}) collective-permute-start(bf16[128,1024]{1,0:T(8,128)(2,1)S(1)} %get-tuple-element.53), channel_id=1, source_target_pairs={{0,12},{4,0},{8,4},{12,8},{1,13},{5,1},{9,5},{13,9},{2,14},{6,2},{... | collective-permute-start | bytes 786440 | tf_op jit(solution)/shard_map/ppermute | solution.py:26
  59.1 14.8 %collective-permute-start.17 = (bf16[15,128,128]{2,1,0:T(8,128)(2,1)S(1)}, bf16[15,128,128]{2,1,0:T(8,128)(2,1)S(1)}, u32[]{:S(2)}, u32[]{:S(2)}) collective-permute-start(bf16[15,128,128]{2,1,0:T(8,128)(2,1)S(1)} %get-tuple-element.56), channel_id=1, source_target_pairs={{0,1},{1,0},{2,3},{3,2},{4,5},{5,4},{6,7},{7,6},{8,9},{9,8},{10,11... | collective-permute-start | bytes 1474568 | tf_op jit(solution)/shard_map/ppermute | solution.py:30
  67.5 6.4 %collective-permute-start.18 = (bf16[15,128,128]{2,1,0:T(8,128)(2,1)S(1)}, bf16[15,128,128]{2,1,0:T(8,128)(2,1)S(1)}, u32[]{:S(2)}, u32[]{:S(2)}) collective-permute-start(bf16[15,128,128]{2,1,0:T(8,128)(2,1)S(1)} %get-tuple-element.57), channel_id=1, source_target_pairs={{0,1},{1,0},{2,3},{3,2},{4,5},{5,4},{6,7},{7,6},{8,9},{9,8},{10,11... | collective-permute-start | bytes 1474568 | tf_op jit(solution)/shard_map/ppermute | solution.py:30
